TPU v7x, 32 devices: a whole 2x2x4 slice. The times are simulated.
32 devices in a mesh: seq: 8 (over z, y), rep: 4 (over x, core).
Axes of the slice: x: 2, y: 2, z: 4, core: 2. Of those that a mesh axis runs over, the one named last changes fastest.
Arguments:
- hidden_in: bfloat16 [4, 2048, 2048], P('rep', 'seq'), may hold values from -6 to 6
- out_grad: bfloat16 [4, 2048, 2048], P('rep', 'seq'), may hold values from -6 to 6
- segment_ids: int32 [4, 2048], P('rep'), may hold values from 0 to 7, never falling along the last dimension, each value on 1 to 512 neighbouring positions
- row_position: int32 [4, 2048], P('rep'), may hold values from 0 to 2047, as said below
- gain_first: bfloat16 [2048], P('seq'), may hold values from 0.5 to 1.5
- shift_first: bfloat16 [2048], P('seq'), may hold values from -1.5 to 1.5
- qkv_weight: bfloat16 [2048, 2304], P('seq'), may hold values from -0.1875 to 0.1875
- qv_bias: bfloat16 [2176], P('seq'), may hold values from -2.5 to 2.5
- out_weight: bfloat16 [2048, 2048], P('seq'), may hold values from -0.375 to 0.375
- out_bias: bfloat16 [2048], P('seq'), may hold values from -2.5 to 2.5
- gain_second: bfloat16 [2048], P('seq'), may hold values from 0.5 to 1.5
- shift_second: bfloat16 [2048], P('seq'), may hold values from -1.5 to 1.5
- fc_weight: bfloat16 [2048, 8192], P('seq'), may hold values from -0.125 to 0.125
- fc_bias: bfloat16 [8192], P('seq'), may hold values from -2.5 to 2.5
- proj_weight: bfloat16 [8192, 2048], P('seq'), may hold values from -0.0625 to 0.0625
- proj_bias: bfloat16 [2048], P('seq'), may hold values from -2.5 to 2.5
Outputs:
- hidden_out: bfloat16 [4, 2048, 2048], P('rep', 'seq')
- input_grad: float32 [4, 2048, 2048], P('rep', 'seq')
- dgain_first: float32 [2048], P('seq')
- dshift_first: float32 [2048], P('seq')
- dqkv_weight: float32 [2048, 2304], P('seq')
- dqv_bias: float32 [2176], P('seq')
- dout_weight: float32 [2048, 2048], P('seq')
- dout_bias: float32 [2048], P('seq')
- dgain_second: float32 [2048], P('seq')
- dshift_second: float32 [2048], P('seq')
- dfc_weight: float32 [2048, 8192], P('seq')
- dfc_bias: float32 [8192], P('seq')
- dproj_weight: float32 [8192, 2048], P('seq')
- dproj_bias: float32 [2048], P('seq')
Inputs may be any that keep to these rules, and one draw needn't show every extreme that they name: `row_position`: in each window the values form a permutation of 0 to 2047. Of the 256 stored rows with indices in [j * 256, (j + 1) * 256), at most 64 have places in [k * 256, (k + 1) * 256) for any k, and for every j exactly 64 do for one k. `segment_ids`: segment numbers never fall along a window's sequence order; each segment has at most 512 places.
All inputs are finite; a program needn't handle non-finite values.
Results may differ from a plain program's by a relative error of at most 0.02.
Values may be sent and summed in bfloat16 or wider, within the bound.
No kernel may reach another device: no remote copies, remote signals or barrier semaphores. Data moves between devices by JAX's collectives and lax.ppermute only.
A program may use at most 384 MiB of HBM per device.

v0:
```python
import math

import jax
import jax.numpy as jnp
from jax import lax
from jax.sharding import PartitionSpec as P

HD = 128
KBLK = 512


EPSILON = 1e-05
NEGATIVE = -1e30


def layer_norm(values, gain_vec, shift_vec):
    center = values - jnp.mean(values, axis=-1, keepdims=True)
    spread = jnp.mean(center * center, axis=-1, keepdims=True)
    return center * lax.rsqrt(spread + EPSILON) * gain_vec + shift_vec


def gelu_tanh(values):
    tanh_arg = math.sqrt(2.0 / math.pi) * (values + 0.044715 * values * values * values)
    return 0.5 * values * (1.0 + jnp.tanh(tanh_arg))


def shards(
    hidden_in,
    out_grad,
    segment_ids,
    row_position,
    gain_first,
    shift_first,
    qkv_weight,
    qv_bias,
    out_weight,
    out_bias,
    gain_second,
    shift_second,
    fc_weight,
    fc_bias,
    proj_weight,
    proj_bias,
):
    seq_count = lax.axis_size("seq")
    seq_index = lax.axis_index("seq")
    row_count = hidden_in.shape[1]
    model_width = hidden_in.shape[2]
    window = row_count * seq_count
    capacity = 2 * row_count // seq_count
    heads = model_width // HD
    scale = 1.0 / math.sqrt(HD)
    padding_id = max(8, window // 256) - 1
    places = row_position[0]
    segments = segment_ids[0]
    lane_ids = jnp.arange(seq_count, dtype=jnp.int32)
    targets = (places // row_count).reshape(seq_count, row_count)
    onehot = (targets[:, :, None] == lane_ids[None, None, :]).astype(jnp.int32)
    rank_ids = jnp.sum((jnp.cumsum(onehot, axis=1) - onehot) * onehot, axis=2).reshape(window)
    send_table = places // row_count * capacity + rank_ids
    first_row = seq_index * row_count
    send_slots = lax.dynamic_slice_in_dim(send_table, first_row, row_count)
    stored_at = jnp.zeros((window,), jnp.int32).at[places].set(jnp.arange(window, dtype=jnp.int32))
    own_stored = lax.dynamic_slice_in_dim(stored_at, first_row, row_count)
    recv_slots = own_stored // row_count * capacity + rank_ids[own_stored]
    slot_total = seq_count * capacity

    def packed(values, slot_ids):
        blank_rows = jnp.zeros((slot_total, values.shape[1]), values.dtype)
        return blank_rows.at[slot_ids].set(values).reshape(seq_count, capacity, values.shape[1])

    def unpacked(received, slot_ids):
        return received.reshape(slot_total, received.shape[2])[slot_ids]

    own_places = first_row + jnp.arange(row_count, dtype=jnp.int32)
    own_segments = lax.dynamic_slice_in_dim(segments, first_row, row_count)
    own_live = own_segments != padding_id
    live_float = own_live.astype(jnp.float32)
    doc_start = jnp.sum((segments < own_segments[0]).astype(jnp.int32))
    block_low = doc_start // KBLK
    block_high = (first_row + row_count - 1) // KBLK + 1

    def block_mask(block_id):
        key_places = block_id * KBLK + jnp.arange(KBLK, dtype=jnp.int32)
        key_segments = lax.dynamic_slice_in_dim(segments, block_id * KBLK, KBLK)
        allowed = (
            (own_segments[:, None] == key_segments[None, :])
            & (key_places[None, :] <= own_places[:, None])
            & own_live[:, None]
        )
        return allowed[:, None, :]

    def block_scores(queries_flat, keys_block):
        raw_scores = jnp.einsum(
            "rd,kd->rk", queries_flat, keys_block, preferred_element_type=jnp.float32
        )
        return raw_scores.reshape(row_count, heads, KBLK) * scale

    first_gain, first_shift, full_qkv, full_qvbias, full_out, full_outbias = (
        lax.all_gather(gain_first, "seq", axis=0, tiled=True),
        lax.all_gather(shift_first, "seq", axis=0, tiled=True),
        lax.all_gather(qkv_weight, "seq", axis=0, tiled=True),
        lax.all_gather(qv_bias, "seq", axis=0, tiled=True),
        lax.all_gather(out_weight, "seq", axis=0, tiled=True),
        lax.all_gather(out_bias, "seq", axis=0, tiled=True),
    )
    inputs_f32 = hidden_in[0].astype(jnp.float32)
    normed1, norm1_pull = jax.vjp(
        layer_norm, inputs_f32, first_gain.astype(jnp.float32), first_shift.astype(jnp.float32)
    )
    normed1_low = normed1.astype(jnp.bfloat16)
    projected = jnp.dot(normed1_low, full_qkv, preferred_element_type=jnp.float32)
    qv_float = full_qvbias.astype(jnp.float32)
    queries = (projected[:, :model_width] + qv_float[:model_width]).astype(jnp.bfloat16)
    kv_shift = jnp.concatenate([jnp.zeros((HD,), jnp.float32), qv_float[model_width:]])
    key_value = (projected[:, model_width:] + kv_shift).astype(jnp.bfloat16)
    arrived = lax.all_to_all(
        packed(queries, send_slots), "seq", split_axis=0, concat_axis=0, tiled=True
    )
    query_places = unpacked(arrived, recv_slots)
    window_kv = lax.all_gather(key_value, "seq", axis=0, tiled=True)
    kv_places = window_kv[stored_at]
    queries_flat = query_places.reshape(row_count * heads, HD)

    def forward_block(block_id, carry):
        running_max, row_sums, weighted = carry
        kv_block = lax.dynamic_slice_in_dim(kv_places, block_id * KBLK, KBLK)
        keys_block = kv_block[:, :HD]
        values_block = kv_block[:, HD:]
        scores = block_scores(queries_flat, keys_block)
        allowed = block_mask(block_id)
        masked = jnp.where(allowed, scores, NEGATIVE)
        new_max = jnp.maximum(running_max, jnp.max(masked, axis=2))
        exp_weights = jnp.exp(masked - new_max[:, :, None]) * allowed.astype(jnp.float32)
        shrink = jnp.exp(running_max - new_max)
        row_sums = row_sums * shrink + jnp.sum(exp_weights, axis=2)
        mixed = jnp.dot(
            exp_weights.astype(jnp.bfloat16).reshape(row_count * heads, KBLK),
            values_block,
            preferred_element_type=jnp.float32,
        )
        weighted = weighted * shrink.reshape(row_count * heads, 1) + mixed
        return (new_max, row_sums, weighted)

    start_state = (
        jnp.full((row_count, heads), NEGATIVE, jnp.float32),
        jnp.zeros((row_count, heads), jnp.float32),
        jnp.zeros((row_count * heads, HD), jnp.float32),
    )
    running_max, row_sums, weighted = lax.fori_loop(
        block_low, block_high, forward_block, start_state
    )
    sums_safe = jnp.where(own_live[:, None], row_sums, 1.0)
    attended = (
        weighted.reshape(row_count, heads, HD) / sums_safe[:, :, None] * live_float[:, None, None]
    ).reshape(row_count, model_width)
    log_norm = running_max + jnp.log(sums_safe)
    attended_low = attended.astype(jnp.bfloat16)
    returned = lax.all_to_all(
        packed(attended_low, recv_slots), "seq", split_axis=0, concat_axis=0, tiled=True
    )
    attended_rows = unpacked(returned, send_slots)
    branch = jnp.dot(
        attended_rows, full_out, preferred_element_type=jnp.float32
    ) + full_outbias.astype(jnp.float32)
    middle = inputs_f32 + branch
    second_gain, second_shift, full_fc, full_fcbias, full_proj, full_projbias = (
        lax.all_gather(gain_second, "seq", axis=0, tiled=True),
        lax.all_gather(shift_second, "seq", axis=0, tiled=True),
        lax.all_gather(fc_weight, "seq", axis=0, tiled=True),
        lax.all_gather(fc_bias, "seq", axis=0, tiled=True),
        lax.all_gather(proj_weight, "seq", axis=0, tiled=True),
        lax.all_gather(proj_bias, "seq", axis=0, tiled=True),
    )
    normed2, norm2_pull = jax.vjp(
        layer_norm, middle, second_gain.astype(jnp.float32), second_shift.astype(jnp.float32)
    )
    normed2_low = normed2.astype(jnp.bfloat16)
    pre_act = jnp.dot(
        normed2_low, full_fc, preferred_element_type=jnp.float32
    ) + full_fcbias.astype(jnp.float32)
    activated, gelu_pull = jax.vjp(gelu_tanh, pre_act)
    activated_low = activated.astype(jnp.bfloat16)
    result = (
        middle
        + jnp.dot(activated_low, full_proj, preferred_element_type=jnp.float32)
        + full_projbias.astype(jnp.float32)
    )
    grad_low = out_grad[0]
    grad_f32 = grad_low.astype(jnp.float32)
    back_fc, back_proj = (
        lax.all_gather(fc_weight, "seq", axis=0, tiled=True),
        lax.all_gather(proj_weight, "seq", axis=0, tiled=True),
    )
    grad_act = jnp.einsum("rd,fd->rf", grad_low, back_proj, preferred_element_type=jnp.float32)
    (grad_pre,) = gelu_pull(grad_act)
    grad_pre_low = grad_pre.astype(jnp.bfloat16)
    dfc_bias = jnp.sum(grad_pre_low.astype(jnp.float32), axis=0)
    dfc_weight = jnp.einsum(
        "rd,rf->df", normed2_low, grad_pre_low, preferred_element_type=jnp.float32
    )
    grad_normed2 = jnp.einsum(
        "rf,df->rd", grad_pre_low, back_fc, preferred_element_type=jnp.float32
    )
    grad_mid_norm, dgain_second, dshift_second = norm2_pull(grad_normed2)
    grad_middle = grad_f32 + grad_mid_norm
    dproj_bias = jnp.sum(grad_f32, axis=0)
    dproj_weight = jnp.einsum(
        "rf,rd->fd", activated_low, grad_low, preferred_element_type=jnp.float32
    )
    mlp_gain, mlp_shift, mlp_fc, mlp_fcbias, mlp_proj, mlp_projbias = (
        lax.psum_scatter(
            dgain_second.astype(jnp.bfloat16), "seq", scatter_dimension=0, tiled=True
        ).astype(jnp.float32),
        lax.psum_scatter(
            dshift_second.astype(jnp.bfloat16), "seq", scatter_dimension=0, tiled=True
        ).astype(jnp.float32),
        lax.psum_scatter(
            dfc_weight.astype(jnp.bfloat16), "seq", scatter_dimension=0, tiled=True
        ).astype(jnp.float32),
        lax.psum_scatter(
            dfc_bias.astype(jnp.bfloat16), "seq", scatter_dimension=0, tiled=True
        ).astype(jnp.float32),
        lax.psum_scatter(
            dproj_weight.astype(jnp.bfloat16), "seq", scatter_dimension=0, tiled=True
        ).astype(jnp.float32),
        lax.psum_scatter(
            dproj_bias.astype(jnp.bfloat16), "seq", scatter_dimension=0, tiled=True
        ).astype(jnp.float32),
    )
    back_qkv, back_out = (
        lax.all_gather(qkv_weight, "seq", axis=0, tiled=True),
        lax.all_gather(out_weight, "seq", axis=0, tiled=True),
    )
    grad_branch = grad_middle.astype(jnp.bfloat16)
    dout_bias = jnp.sum(grad_branch.astype(jnp.float32), axis=0)
    dout_weight = jnp.einsum(
        "rd,re->de", attended_rows, grad_branch, preferred_element_type=jnp.float32
    )
    grad_attended = jnp.einsum(
        "re,de->rd", grad_branch, back_out, preferred_element_type=jnp.float32
    ).astype(jnp.bfloat16)
    grad_arrived = lax.all_to_all(
        packed(grad_attended, send_slots), "seq", split_axis=0, concat_axis=0, tiled=True
    )
    grad_places = unpacked(grad_arrived, recv_slots)
    grad_flat = grad_places.reshape(row_count * heads, HD)
    delta_rows = jnp.sum(
        grad_places.astype(jnp.float32).reshape(row_count, heads, HD)
        * attended.reshape(row_count, heads, HD),
        axis=2,
    )

    def backward_block(block_id, carry):
        grad_queries, grad_kv = carry
        kv_block = lax.dynamic_slice_in_dim(kv_places, block_id * KBLK, KBLK)
        keys_block = kv_block[:, :HD]
        values_block = kv_block[:, HD:]
        scores = block_scores(queries_flat, keys_block)
        allowed = block_mask(block_id)
        masked = jnp.where(allowed, scores, NEGATIVE)
        prob_rows = jnp.exp(masked - log_norm[:, :, None]) * allowed.astype(jnp.float32)
        grad_probs = jnp.einsum(
            "rd,kd->rk", grad_flat, values_block, preferred_element_type=jnp.float32
        ).reshape(row_count, heads, KBLK)
        grad_scores = (prob_rows * (grad_probs - delta_rows[:, :, None]) * scale).astype(
            jnp.bfloat16
        )
        grad_scores = grad_scores.reshape(row_count * heads, KBLK)
        grad_queries = grad_queries + jnp.dot(
            grad_scores, keys_block, preferred_element_type=jnp.float32
        )
        grad_keys = jnp.einsum(
            "rk,rd->kd", grad_scores, queries_flat, preferred_element_type=jnp.float32
        )
        prob_low = prob_rows.astype(jnp.bfloat16).reshape(row_count * heads, KBLK)
        grad_values = jnp.einsum(
            "rk,rd->kd", prob_low, grad_flat, preferred_element_type=jnp.float32
        )
        current = lax.dynamic_slice_in_dim(grad_kv, block_id * KBLK, KBLK)
        update = jnp.concatenate([grad_keys, grad_values], axis=1)
        grad_kv = lax.dynamic_update_slice_in_dim(grad_kv, current + update, block_id * KBLK, 0)
        return (grad_queries, grad_kv)

    back_state = (
        jnp.zeros((row_count * heads, HD), jnp.float32),
        jnp.zeros((window, 2 * HD), jnp.float32),
    )
    grad_queries, grad_kv = lax.fori_loop(block_low, block_high, backward_block, back_state)
    grad_query_low = grad_queries.astype(jnp.bfloat16).reshape(row_count, model_width)
    grad_returned = lax.all_to_all(
        packed(grad_query_low, recv_slots), "seq", split_axis=0, concat_axis=0, tiled=True
    )
    grad_query_rows = unpacked(grad_returned, send_slots)
    grad_kv_stored = grad_kv[places]
    grad_kv_rows = lax.psum_scatter(
        grad_kv_stored.astype(jnp.bfloat16), "seq", scatter_dimension=0, tiled=True
    )
    grad_qkv = jnp.concatenate([grad_query_rows, grad_kv_rows], axis=1)
    grad_qkv_float = grad_qkv.astype(jnp.float32)
    dqv_bias = jnp.concatenate(
        [
            jnp.sum(grad_qkv_float[:, :model_width], axis=0),
            jnp.sum(grad_qkv_float[:, model_width + HD :], axis=0),
        ]
    )
    dqkv_weight = jnp.einsum("rd,rc->dc", normed1_low, grad_qkv, preferred_element_type=jnp.float32)
    grad_normed1 = jnp.einsum("rc,dc->rd", grad_qkv, back_qkv, preferred_element_type=jnp.float32)
    grad_in_norm, dgain_first, dshift_first = norm1_pull(grad_normed1)
    input_grad = grad_middle + grad_in_norm
    attn_gain, attn_shift, attn_qkv, attn_qvbias, attn_out, attn_outbias = (
        lax.psum_scatter(
            dgain_first.astype(jnp.bfloat16), "seq", scatter_dimension=0, tiled=True
        ).astype(jnp.float32),
        lax.psum_scatter(
            dshift_first.astype(jnp.bfloat16), "seq", scatter_dimension=0, tiled=True
        ).astype(jnp.float32),
        lax.psum_scatter(
            dqkv_weight.astype(jnp.bfloat16), "seq", scatter_dimension=0, tiled=True
        ).astype(jnp.float32),
        lax.psum_scatter(
            dqv_bias.astype(jnp.bfloat16), "seq", scatter_dimension=0, tiled=True
        ).astype(jnp.float32),
        lax.psum_scatter(
            dout_weight.astype(jnp.bfloat16), "seq", scatter_dimension=0, tiled=True
        ).astype(jnp.float32),
        lax.psum_scatter(
            dout_bias.astype(jnp.bfloat16), "seq", scatter_dimension=0, tiled=True
        ).astype(jnp.float32),
    )
    totals = (
        lax.psum(attn_gain.astype(jnp.bfloat16), "rep").astype(jnp.float32),
        lax.psum(attn_shift.astype(jnp.bfloat16), "rep").astype(jnp.float32),
        lax.psum(attn_qkv.astype(jnp.bfloat16), "rep").astype(jnp.float32),
        lax.psum(attn_qvbias.astype(jnp.bfloat16), "rep").astype(jnp.float32),
        lax.psum(attn_out.astype(jnp.bfloat16), "rep").astype(jnp.float32),
        lax.psum(attn_outbias.astype(jnp.bfloat16), "rep").astype(jnp.float32),
        lax.psum(mlp_gain.astype(jnp.bfloat16), "rep").astype(jnp.float32),
        lax.psum(mlp_shift.astype(jnp.bfloat16), "rep").astype(jnp.float32),
        lax.psum(mlp_fc.astype(jnp.bfloat16), "rep").astype(jnp.float32),
        lax.psum(mlp_fcbias.astype(jnp.bfloat16), "rep").astype(jnp.float32),
        lax.psum(mlp_proj.astype(jnp.bfloat16), "rep").astype(jnp.float32),
        lax.psum(mlp_projbias.astype(jnp.bfloat16), "rep").astype(jnp.float32),
    )
    return (
        result.astype(jnp.bfloat16)[None],
        input_grad[None],
        totals[0],
        totals[1],
        totals[2],
        totals[3],
        totals[4],
        totals[5],
        totals[6],
        totals[7],
        totals[8],
        totals[9],
        totals[10],
        totals[11],
    )


def solution(mesh):
    placed = (
        P("rep", "seq", None),
        P("rep", "seq", None),
        P("rep", None),
        P("rep", None),
        P("seq"),
        P("seq"),
        P("seq", None),
        P("seq"),
        P("seq", None),
        P("seq"),
        P("seq"),
        P("seq"),
        P("seq", None),
        P("seq"),
        P("seq", None),
        P("seq"),
    )
    return jax.shard_map(
        shards,
        mesh=mesh,
        in_specs=placed,
        out_specs=(
            P("rep", "seq", None),
            P("rep", "seq", None),
            P("seq"),
            P("seq"),
            P("seq", None),
            P("seq"),
            P("seq", None),
            P("seq"),
            P("seq"),
            P("seq"),
            P("seq", None),
            P("seq"),
            P("seq", None),
            P("seq"),
        ),
        check_vma=False,
    )
```

profile of v0, /device:TPU:0, one launch (start us, length us, event | category | flops | bytes accessed | tf_op | source)
XLA Modules:
  0.0 3566.0 jit_solution(14426607719734576895)
XLA Ops:
  8.6 22.4 all-gather.1
  72.8 78.7 %all-gather.12.cloned.1.call-done = bf16[2048,2304]{1,0:T(8,128)(2,1)} async-done(((bf16[256,2304]{1,0:T(8,128)(2,1)}), bf16[2048,2304]{1,0:T(8,128)(2,1)}) %all-gather.12.cloned.1.call-update) | async-done | bytes 9437200 | tf_op jit(solution)/shard_map/all_gather | solution.py:102
  191.5 29.8 all-gather.14.cloned.1.call-done
  233.9 55.7 %while.29 = (s32[]{:T(128)}, f32[256,16]{1,0:T(8,128)S(1)}, f32[256,16]{1,0:T(8,128)}, f32[4096,128]{1,0:T(8,128)S(1)}, s32[]{:T(128)}, /*index=5*/s32[256]{0:T(...) while((s32[]{:T(128)}, f32[256,16]{1,0:T(8,128)S(1)}, ...), condition=%wide.region_11.12_spmd.clone, body=%wide.region_8.11_spmd.clone.sunk | while | flops 1094329088 | bytes 82730592 | solution.py:150
  300.4 46.5 %all-to-all-start.1 = ((bf16[8,64,2048]{2,1,0:T(8,128)(2,1)}), bf16[8,64,2048]{2,1,0:T(8,128)(2,1)}, u32[]{:S(2)}, u32[]{:S(2)}) async-start(bf16[8,64,2048]{2,1,0:T(8,128)(2,1)} %bitcast.191), calls=%async_computation.1 | async-start | bytes 4194304 | tf_op jit(solution)/shard_map/all_to_all | solution.py:159
  346.9 97.3 %all-gather.2 = bf16[8,1,256]{2,1,0:T(2,128)(2,1)S(1)} all-gather(bf16[1,1,256]{2,1,0:T(2,128)(2,1)S(1)} %reshape.621), channel_id=1, replica_groups=mesh['seq'=8,'rep'=4] {'seq'}, dimensions={0}, use_global_device_ids=true | all-gather | bytes 4608 | tf_op jit(solution)/shard_map/all_gather | solution.py:105
  444.2 55.3 %all_gather.53 = bf16[8192]{0:T(1024)(128)(2,1)S(1)} all-gather(bf16[1024]{0:T(1024)(128)(2,1)S(1)} %copy-done.62), channel_id=1, replica_groups=mesh['seq'=8,'rep'=4] {'seq'}, dimensions={0}, use_global_device_ids=true | all-gather | bytes 18432 | tf_op jit(solution)/shard_map/all_gather | solution.py:171
  499.5 28.5 all-gather.4
  528.1 32.0 all-gather.3
  573.6 428.8 %all-gather.18.cloned.1.call-done = bf16[2048,8192]{1,0:T(8,128)(2,1)} async-done(((bf16[256,8192]{1,0:T(8,128)(2,1)}), bf16[2048,8192]{1,0:T(8,128)(2,1)}) %all-gather.18.cloned.1.call-update) | async-done | bytes 33554448 | tf_op jit(solution)/shard_map/all_gather | solution.py:170
  1002.5 20.7 convolution_add_fusion.2
  1023.2 617.5 %all-gather.20.cloned.1.call-done = bf16[8192,2048]{1,0:T(8,128)(2,1)} async-done(((bf16[1024,2048]{1,0:T(8,128)(2,1)}), bf16[8192,2048]{1,0:T(8,128)(2,1)}) %all-gather.20.cloned.1.call-update) | async-done | bytes 33554448 | tf_op jit(solution)/shard_map/all_gather | solution.py:172
  1640.7 23.0 fusion.98
  1703.6 48.4 %all-to-all-done.2 = bf16[8,64,2048]{2,1,0:T(8,128)(2,1)} async-done(((bf16[8,64,2048]{2,1,0:T(8,128)(2,1)}), bf16[8,64,2048]{2,1,0:T(8,128)(2,1)}, u32[]{:S(2)}, u32[]{:S(2)}) %all-to-all-start.2) | async-done | bytes 2097184 | tf_op jit(solution)/shard_map/all_to_all | solution.py:243
  1765.3 50.2 %while.30 = (s32[]{:T(128)}, f32[4096,128]{1,0:T(8,128)S(1)}, f32[2048,256]{1,0:T(8,128)}, s32[]{:T(128)}, s32[256]{0:T(256)S(1)}, /*index=5*/s32[2048]{0:T(1024...) while((s32[]{:T(128)}, f32[4096,128]{1,0:T(8,128)S(1)}, ...), condition=%wide.wide.region_20.21_spmd.clone, body=%wide.wide.region_19.20_spmd.clone.sunk | while | flops 2704671488 | bytes 131774072 | solution.py:289
  1837.4 110.0 %all_to_all.20 = bf16[8,64,2048]{2,1,0:T(8,128)(2,1)S(1)} all-to-all(bf16[8,64,2048]{2,1,0:T(8,128)(2,1)} %bitcast.194), channel_id=1, replica_groups=mesh['seq'=8,'rep'=4] {'seq'}, dimensions={0} | all-to-all | bytes 4194304 | tf_op jit(solution)/shard_map/all_to_all | solution.py:291
  1993.7 19.8 all-gather.5
  2015.4 80.2 %reduce-scatter.10.cloned.1.call-done = bf16[256,2048]{1,0:T(8,128)(2,1)} async-done(((bf16[2048,2048]{1,0:T(8,128)(2,1)}), bf16[256,2048]{1,0:T(8,128)(2,1)}) %reduce-scatter.10.cloned.1.call-update) | async-done | bytes 1048592 | tf_op jit(solution)/shard_map/reduce_scatter | solution.py:324
  2095.6 166.1 %reduce-scatter.8.cloned.1.call-done = bf16[256,2304]{1,0:T(8,128)(2,1)} async-done(((bf16[2048,2304]{1,0:T(8,128)(2,1)}), bf16[256,2304]{1,0:T(8,128)(2,1)}) %reduce-scatter.8.cloned.1.call-update) | async-done | bytes 1179664 | tf_op jit(solution)/shard_map/reduce_scatter | solution.py:318
  2261.7 546.2 %reduce-scatter.12.cloned.1.call-done = bf16[256,8192]{1,0:T(8,128)(2,1)} async-done(((bf16[2048,8192]{1,0:T(8,128)(2,1)}), bf16[256,8192]{1,0:T(8,128)(2,1)}) %reduce-scatter.12.cloned.1.call-update) | async-done | bytes 4194320 | tf_op jit(solution)/shard_map/reduce_scatter | solution.py:218
  2807.8 545.8 %reduce-scatter.14.cloned.1.call-done = bf16[1024,2048]{1,0:T(8,128)(2,1)} async-done(((bf16[8192,2048]{1,0:T(8,128)(2,1)}), bf16[1024,2048]{1,0:T(8,128)(2,1)}) %reduce-scatter.14.cloned.1.call-update) | async-done | bytes 4194320 | tf_op jit(solution)/shard_map/reduce_scatter | solution.py:224
  3353.7 20.3 fusion.39
  3383.5 35.6 all-reduce.10
  3435.3 110.5 %all-reduce.15.cloned.1.call-done = (bf16[256,2304]{1,0:T(8,128)(2,1)}, bf16[256,2048]{1,0:T(8,128)(2,1)}, bf16[256,8192]{1,0:T(8,128)(2,1)}, bf16[1024,2048]{1,0:T(8,128)(2,1)}) async-done(((bf16[256,2304]{1,0:T(8,128)(2,1)}, bf16[256,2048]{1,0:T(8,128)(2,1)}, bf16[256,8192]{1,0:T(8,128)(2,1)}, bf16[1024,2048]{1,0:T(8,128)(2,1)}), (bf16[256,2304]{1,0:T(8,128)(2,1)}, bf16[256,2048]{1,0:T(8,128)(2,1)}, ...) | async-done | bytes 10616848 | tf_op jit(solution)/shard_map/psum | solution.py:334
  (331 shorter events, 370.3 us)
Async XLA Ops:
  7.2 144.3 %all-gather.12.cloned.1.call-start = ((), (), s32[]{:S(2)}) async-start(), calls=%async_computation.9 | async-start | bytes 10616832 | tf_op jit(solution)/shard_map/all_gather | solution.py:102
  7.9 213.4 %all-gather.14.cloned.1.call-start = ((), (), s32[]{:S(2)}) async-start(), calls=%async_computation.10 | async-start | bytes 1179648 | tf_op jit(solution)/shard_map/all_gather | solution.py:121
  31.1 126.9 %copy-start.32 = (f32[8,1,256]{2,1,0:T(1,128)}, f32[8,1,256]{2,1,0:T(1,128)S(1)}, u32[]{:S(2)}) copy-start(f32[8,1,256]{2,1,0:T(1,128)S(1)} %convert_element_type.266) | copy-start | bytes 24580
  48.1 109.8 %copy-start.25 = (f32[8,1,256]{2,1,0:T(1,128)}, f32[8,1,256]{2,1,0:T(1,128)S(1)}, u32[]{:S(2)}) copy-start(f32[8,1,256]{2,1,0:T(1,128)S(1)} %convert_element_type.265) | copy-start | bytes 24580
  158.7 406.7 %all-gather.16.cloned.1.call-start = ((), (), s32[]{:S(2)}) async-start(), calls=%async_computation.11 | async-start | bytes 9437184 | tf_op jit(solution)/shard_map/all_gather | solution.py:104
  159.4 843.1 %all-gather.18.cloned.1.call-start = ((), (), s32[]{:S(2)}) async-start(), calls=%async_computation.12 | async-start | bytes 37748736 | tf_op jit(solution)/shard_map/all_gather | solution.py:170
  160.0 1480.7 %all-gather.20.cloned.1.call-start = ((), (), s32[]{:S(2)}) async-start(), calls=%async_computation.13 | async-start | bytes 37748736 | tf_op jit(solution)/shard_map/all_gather | solution.py:172
  170.8 60.4 %all-to-all-start = ((bf16[8,64,2048]{2,1,0:T(8,128)(2,1)}), bf16[8,64,2048]{2,1,0:T(8,128)(2,1)S(1)}, u32[]{:S(2)}, u32[]{:S(2)}) async-start(bf16[8,64,2048]{2,1,0:T(8,128)(2,1)} %bitcast.190), calls=%async_computation | async-start | bytes 4194304 | tf_op jit(solution)/shard_map/all_to_all | solution.py:117
  300.4 143.8 %copy-start.62 = (bf16[1024]{0:T(1024)(128)(2,1)S(1)}, bf16[1024]{0:T(1024)(128)(2,1)}, u32[]{:S(2)}) copy-start(bf16[1024]{0:T(1024)(128)(2,1)} %param.33) | copy-start | bytes 6148
  300.4 199.1 %copy-start.64 = (bf16[256]{0:T(256)(128)(2,1)S(1)}, bf16[256]{0:T(256)(128)(2,1)}, u32[]{:S(2)}) copy-start(bf16[256]{0:T(256)(128)(2,1)} %param.31) | copy-start | bytes 1540
  300.4 227.6 %copy-start.65 = (bf16[256]{0:T(256)(128)(2,1)S(1)}, bf16[256]{0:T(256)(128)(2,1)}, u32[]{:S(2)}) copy-start(bf16[256]{0:T(256)(128)(2,1)} %param.30) | copy-start | bytes 1540
  300.4 259.7 %copy-start.61 = (s32[256]{0:T(256)S(1)}, s32[256]{0:T(256)}, u32[]{:S(2)}) copy-start(s32[256]{0:T(256)} %copy-done.60) | copy-start | bytes 3076
  300.4 259.7 %all-to-all-start.1 = ((bf16[8,64,2048]{2,1,0:T(8,128)(2,1)}), bf16[8,64,2048]{2,1,0:T(8,128)(2,1)}, u32[]{:S(2)}, u32[]{:S(2)}) async-start(bf16[8,64,2048]{2,1,0:T(8,128)(2,1)} %bitcast.191), calls=%async_computation.1 | async-start | bytes 4194304 | tf_op jit(solution)/shard_map/all_to_all | solution.py:159
  528.1 474.4 %copy-start.23 = (f32[8,1,256]{2,1,0:T(1,128)}, f32[8,1,256]{2,1,0:T(1,128)S(1)}, u32[]{:S(2)}) copy-start(f32[8,1,256]{2,1,0:T(1,128)S(1)} %convert_element_type.269) | copy-start | bytes 24580
  560.1 1122.1 %copy-start.21 = (f32[8,1,256]{2,1,0:T(1,128)}, f32[8,1,256]{2,1,0:T(1,128)S(1)}, u32[]{:S(2)}) copy-start(f32[8,1,256]{2,1,0:T(1,128)S(1)} %convert_element_type.268) | copy-start | bytes 24580
  572.0 1110.3 %copy-start.34 = (f32[256]{0:T(256)}, f32[256]{0:T(256)S(1)}, u32[]{:S(2)}) copy-start(f32[256]{0:T(256)S(1)} %broadcast_multiply_fusion) | copy-start | bytes 3076
  573.6 1108.6 %copy-start.40 = (f32[256]{0:T(256)}, f32[256]{0:T(256)S(1)}, u32[]{:S(2)}) copy-start(f32[256]{0:T(256)S(1)} %fusion.82) | copy-start | bytes 3076
  1698.7 53.3 %all-to-all-start.2 = ((bf16[8,64,2048]{2,1,0:T(8,128)(2,1)}), bf16[8,64,2048]{2,1,0:T(8,128)(2,1)}, u32[]{:S(2)}, u32[]{:S(2)}) async-start(bf16[8,64,2048]{2,1,0:T(8,128)(2,1)} %bitcast.192), calls=%async_computation.2 | async-start | bytes 4194304 | tf_op jit(solution)/shard_map/all_to_all | solution.py:243
  1703.4 245.6 %reduce-scatter.6.cloned.1.call-start = ((), (), s32[]{:S(2)}) async-start(), calls=%async_computation.14 | async-start | bytes 1179648 | tf_op jit(solution)/shard_map/reduce_scatter | solution.py:296
  1825.8 269.8 %reduce-scatter.10.cloned.1.call-start = ((), (), s32[]{:S(2)}) async-start(), calls=%async_computation.16 | async-start | bytes 9437184 | tf_op jit(solution)/shard_map/reduce_scatter | solution.py:324
  1832.9 428.8 %reduce-scatter.8.cloned.1.call-start = ((), (), s32[]{:S(2)}) async-start(), calls=%async_computation.15 | async-start | bytes 10616832 | tf_op jit(solution)/shard_map/reduce_scatter | solution.py:318
  1955.6 852.3 %reduce-scatter.12.cloned.1.call-start = ((), (), s32[]{:S(2)}) async-start(), calls=%async_computation.17 | async-start | bytes 37748736 | tf_op jit(solution)/shard_map/reduce_scatter | solution.py:218
  1973.4 1380.2 %reduce-scatter.14.cloned.1.call-start = ((), (), s32[]{:S(2)}) async-start(), calls=%async_computation.18 | async-start | bytes 37748736 | tf_op jit(solution)/shard_map/reduce_scatter | solution.py:224
  1992.1 1553.8 %all-reduce.15.cloned.1.call-start = ((), (), s32[]{:S(2)}) async-start(), calls=%async_computation.19 | async-start | bytes 21233664 | tf_op jit(solution)/shard_map/psum | solution.py:334
  (57 other events, 728.6 us)
Sparse Core Ops, SparseCore 0:
  10.2 141.2 all-gather.11
  158.8 62.4 all-gather.13
  223.4 122.1 all-gather.15
  347.0 655.4 all-gather.17
  1003.9 636.7 all-gather.19
  1825.9 117.0 reduce-scatter.5
  1947.6 147.8 reduce-scatter.9
  2099.2 162.4 reduce-scatter.7
  2265.4 542.3 reduce-scatter.11
  2811.5 542.1 reduce-scatter.13
  3356.5 189.3 all-reduce.14
where the time goes:
time: 3580 us; the launch traced here: 3570 us
  waiting for transfers between devices  2650 us (74%)
  blocking collectives  444 us (12%)
  matrix products  190 us (5%)
  local copies, waits for them, and re-layouts  122 us (3%)
  other arithmetic  68.1 us (2%)
  starting transfers between devices  55.4 us (2%)
    all_gather x1, waiting for transfers between devices, shards(): lax.all_gather(proj_weight, 'seq', axis=0, tiled=True)  617 us
    reduce_scatter x1, waiting for transfers between devices, shards(): lax.psum_scatter(dfc_weight.astype(jnp.bfloat16), 'seq', scatter_dimensio...  546 us
    reduce_scatter x1, waiting for transfers between devices, shards(): lax.psum_scatter(dproj_weight.astype(jnp.bfloat16), 'seq', scatter_dimens...  546 us
    all_gather x1, waiting for transfers between devices, shards(): lax.all_gather(fc_weight, 'seq', axis=0, tiled=True)  429 us
    reduce_scatter x1, waiting for transfers between devices, shards(): lax.psum_scatter(dqkv_weight.astype(jnp.bfloat16), 'seq', scatter_dimensi...  166 us
    psum x1, waiting for transfers between devices, shards(): lax.psum(attn_qkv.astype(jnp.bfloat16), 'rep').astype(jnp.float32)  111 us
    all_to_all x1, blocking collectives, shards(): lax.all_to_all(packed(grad_query_low, recv_slots), 'seq', split_axis=0, c...  110 us
    all_gather x1, blocking collectives, shards(): lax.all_gather(out_bias, 'seq', axis=0, tiled=True)  97.3 us
  transfers between devices with their start and end apart: 14, of which 10 were waited for; matrix products, arithmetic and copies ran while one was open for 6% of the time, Pallas kernels for 0%

commit v1 on v0

v1 whole, which is shorter than its diff:
```python
import functools
import math

import jax
import jax.numpy as jnp
from jax import lax
from jax.experimental import pallas as pl
from jax.experimental.pallas import tpu as pltpu
from jax.sharding import Mesh
from jax.sharding import PartitionSpec as P

HD = 128
EPSILON = 1e-05
NEGATIVE = -1e30
SCALE = 1.0 / math.sqrt(HD)
LOG2E = math.log2(math.e)
GELU_C = math.sqrt(2.0 / math.pi)
SEQ = ("z", "y")
REP = ("x", "c")
PLANE = ("y", "x", "c")
ALL = ("z", "y", "x", "c")
BF16 = jnp.bfloat16
F32 = jnp.float32
HEADS_STEP = 2


def dot(left, right, dims):
    return lax.dot_general(left, right, (dims, ((), ())), preferred_element_type=F32)


NN = ((1,), (0,))
NT = ((1,), (1,))
TN = ((0,), (0,))


def attention_bias(seg_own, seg_ctx, padding_id, rows, ctx):
    t = lax.broadcasted_iota(jnp.int32, (rows, ctx), 0)
    u = lax.broadcasted_iota(jnp.int32, (rows, ctx), 1)
    allowed = (seg_own == seg_ctx) & (u <= t + (ctx - rows)) & (seg_own != padding_id)
    return jnp.where(allowed, 0.0, NEGATIVE).astype(F32)


def forward_kernel(padding_id, q_ref, kv_ref, own_ref, ctx_ref, low_ref, att_ref, norm_ref, bias):
    rows, ctx = bias.shape

    @pl.when(pl.program_id(0) == 0)
    def _():
        bias[...] = attention_bias(own_ref[...], ctx_ref[...], padding_id, rows, ctx)

    live = own_ref[...] != padding_id
    keys = kv_ref[:, :HD]
    values = kv_ref[:, HD:]
    for head in range(HEADS_STEP):
        lanes = slice(head * HD, (head + 1) * HD)
        scores = dot(q_ref[:, lanes], keys, NT) * (SCALE * LOG2E) + bias[...]
        top = jnp.max(scores, axis=1, keepdims=True)
        weights = jnp.exp2(scores - top)
        sums = jnp.sum(weights, axis=1, keepdims=True)
        mixed = dot(weights.astype(BF16), values, NN)
        attended = jnp.where(live, mixed / sums, 0.0)
        att_ref[:, lanes] = attended
        low_ref[:, lanes] = attended.astype(BF16)
        norm = jnp.where(live, top + jnp.log2(sums), 0.0)
        norm_ref[:, lanes] = jnp.broadcast_to(norm, (rows, HD))


def attention_forward(queries, kv_ctx, seg_own, seg_ctx, padding_id):
    rows, width = queries.shape
    ctx = kv_ctx.shape[0]
    step = HEADS_STEP * HD
    tile = pl.BlockSpec((rows, step), lambda h: (0, h))
    return pl.pallas_call(
        functools.partial(forward_kernel, padding_id),
        grid=(width // step,),
        in_specs=[
            tile,
            pl.BlockSpec((ctx, 2 * HD), lambda h: (0, 0)),
            pl.BlockSpec((rows, 1), lambda h: (0, 0)),
            pl.BlockSpec((1, ctx), lambda h: (0, 0)),
        ],
        out_specs=[tile, tile, tile],
        out_shape=[
            jax.ShapeDtypeStruct((rows, width), BF16),
            jax.ShapeDtypeStruct((rows, width), F32),
            jax.ShapeDtypeStruct((rows, width), F32),
        ],
        scratch_shapes=[pltpu.VMEM((rows, ctx), F32)],
        compiler_params=pltpu.CompilerParams(vmem_limit_bytes=40 * 1024 * 1024),
        cost_estimate=pl.CostEstimate(
            flops=4 * rows * ctx * width,
            bytes_accessed=12 * rows * width,
            transcendentals=rows * ctx * width // HD,
        ),
        name="attention_forward",
    )(queries, kv_ctx, seg_own, seg_ctx)


def backward_kernel(
    padding_id, q_ref, g_ref, att_ref, norm_ref, kv_ref, own_ref, ctx_ref, dq_ref, dkv_ref, bias
):
    rows, ctx = bias.shape

    @pl.when(pl.program_id(0) == 0)
    def _():
        bias[...] = attention_bias(own_ref[...], ctx_ref[...], padding_id, rows, ctx)
        dkv_ref[...] = jnp.zeros_like(dkv_ref)

    keys = kv_ref[:, :HD]
    values = kv_ref[:, HD:]
    for head in range(HEADS_STEP):
        lanes = slice(head * HD, (head + 1) * HD)
        q = q_ref[:, lanes]
        g = g_ref[:, lanes]
        delta = jnp.sum(g.astype(F32) * att_ref[:, lanes], axis=1, keepdims=True)
        norm = norm_ref[:, head * HD : head * HD + 1]
        scores = dot(q, keys, NT) * (SCALE * LOG2E) + bias[...]
        prob = jnp.exp2(scores - norm)
        grad_prob = dot(g, values, NT)
        grad_scores = (prob * (grad_prob - delta) * SCALE).astype(BF16)
        dq_ref[:, lanes] = dot(grad_scores, keys, NN).astype(BF16)
        dkv_ref[:, :HD] += dot(grad_scores, q, TN)
        dkv_ref[:, HD:] += dot(prob.astype(BF16), g, TN)


def attention_backward(queries, grads, attended, norms, kv_ctx, seg_own, seg_ctx, padding_id):
    rows, width = queries.shape
    ctx = kv_ctx.shape[0]
    step = HEADS_STEP * HD
    tile = pl.BlockSpec((rows, step), lambda h: (0, h))
    whole = pl.BlockSpec((ctx, 2 * HD), lambda h: (0, 0))
    return pl.pallas_call(
        functools.partial(backward_kernel, padding_id),
        grid=(width // step,),
        in_specs=[
            tile,
            tile,
            tile,
            tile,
            whole,
            pl.BlockSpec((rows, 1), lambda h: (0, 0)),
            pl.BlockSpec((1, ctx), lambda h: (0, 0)),
        ],
        out_specs=[tile, whole],
        out_shape=[
            jax.ShapeDtypeStruct((rows, width), BF16),
            jax.ShapeDtypeStruct((ctx, 2 * HD), F32),
        ],
        scratch_shapes=[pltpu.VMEM((rows, ctx), F32)],
        compiler_params=pltpu.CompilerParams(vmem_limit_bytes=48 * 1024 * 1024),
        cost_estimate=pl.CostEstimate(
            flops=10 * rows * ctx * width,
            bytes_accessed=14 * rows * width,
            transcendentals=rows * ctx * width // HD,
        ),
        name="attention_backward",
    )(queries, grads, attended, norms, kv_ctx, seg_own, seg_ctx)


def norm_parts(values):
    center = values - jnp.mean(values, axis=-1, keepdims=True)
    spread = jnp.mean(center * center, axis=-1, keepdims=True)
    rstd = lax.rsqrt(spread + EPSILON)
    return center * rstd, rstd


def norm_back(grad, unit, rstd, gain):
    scaled = grad * gain
    mean_g = jnp.mean(scaled, axis=-1, keepdims=True)
    mean_gu = jnp.mean(scaled * unit, axis=-1, keepdims=True)
    return rstd * (scaled - mean_g - unit * mean_gu)


def gelu_pair(v):
    inner = jnp.tanh(GELU_C * (v + 0.044715 * v * v * v))
    value = 0.5 * v * (1.0 + inner)
    slope = 0.5 * (1.0 + inner) + 0.5 * v * (1.0 - inner * inner) * GELU_C * (
        1.0 + 3.0 * 0.044715 * v * v
    )
    return value, slope


def gather_plane(block):
    return lax.all_gather(block, PLANE, axis=0, tiled=True)


def scatter_plane(partial):
    return lax.psum_scatter(partial, PLANE, scatter_dimension=0, tiled=True)


def shards(
    hidden_in,
    out_grad,
    segment_ids,
    row_position,
    gain_first,
    shift_first,
    qkv_weight,
    qv_bias,
    out_weight,
    out_bias,
    gain_second,
    shift_second,
    fc_weight,
    fc_bias,
    proj_weight,
    proj_bias,
):
    zs, ys, xs, cs = (lax.axis_size(a) for a in ALL)
    reps = xs * cs
    plane = ys * reps
    seqs = zs * ys
    z_at = lax.axis_index("z")
    y_at = lax.axis_index("y")
    q_at = lax.axis_index("x") * cs + lax.axis_index("c")
    f_at = y_at * reps + q_at
    seq_at = z_at * ys + y_at
    rows = hidden_in.shape[1]
    width = hidden_in.shape[2]
    window = rows * seqs
    capacity = 2 * rows // seqs
    slots = seqs * capacity
    halo = max(1, seqs // 4)
    ctx = (halo + 1) * rows
    padding_id = max(8, window // 256) - 1
    qkv_cols = qkv_weight.shape[1]
    ff = fc_weight.shape[1]
    ff_block = ff // seqs
    ff_unit = ff_block // reps
    ff_own = zs * ff_unit

    places = row_position[0]
    segments = segment_ids[0]
    targets = (places // rows).reshape(seqs, rows)
    earlier = (
        lax.broadcasted_iota(jnp.int32, (rows, rows), 1)
        < lax.broadcasted_iota(jnp.int32, (rows, rows), 0)
    )
    same = (targets[:, :, None] == targets[:, None, :]) & earlier[None]
    ranks = jnp.sum(same.astype(jnp.int32), axis=2).reshape(window)
    first_row = seq_at * rows
    own_places_stored = lax.dynamic_slice_in_dim(places, first_row, rows)
    own_ranks = lax.dynamic_slice_in_dim(ranks, first_row, rows)
    send_slots = own_places_stored // rows * capacity + own_ranks
    arrive_slots = jnp.arange(window, dtype=jnp.int32) // rows * capacity + ranks
    own_places = first_row + jnp.arange(rows, dtype=jnp.int32)
    recv_slots = jnp.sum(
        jnp.where(places[None, :] == own_places[:, None], arrive_slots[None, :], 0), axis=1
    )
    slot_ids = jnp.arange(slots, dtype=jnp.int32)
    pick_send = (send_slots[:, None] == slot_ids[None, :]).astype(BF16)
    pick_recv = (recv_slots[:, None] == slot_ids[None, :]).astype(BF16)

    def exchange(values, pick_out, pick_in):
        packed = dot(pick_out, values, TN).astype(BF16).reshape(seqs, capacity, values.shape[1])
        moved = lax.all_to_all(packed, SEQ, split_axis=0, concat_axis=0, tiled=True)
        return dot(pick_in, moved.reshape(slots, values.shape[1]), NN)

    def to_places(values):
        return exchange(values, pick_send, pick_recv)

    def to_stored(values):
        return exchange(values, pick_recv, pick_send)

    small = jnp.concatenate(
        [gain_first, shift_first, qv_bias, out_bias, gain_second, shift_second, fc_bias, proj_bias]
    )
    small_all = lax.all_gather(small, SEQ, axis=0, tiled=True).reshape(seqs, -1).astype(F32)
    parts = []
    at = 0
    for item in (
        gain_first,
        shift_first,
        qv_bias,
        out_bias,
        gain_second,
        shift_second,
        fc_bias,
        proj_bias,
    ):
        parts.append(small_all[:, at : at + item.shape[0]].reshape(-1))
        at += item.shape[0]
    gain1, shift1, qv_full, out_shift, gain2, shift2, fc_shift, proj_shift = parts
    fc_shift_own = lax.dynamic_slice(
        fc_shift.reshape(zs, ys, reps, ff_unit), (0, y_at, q_at, 0), (zs, 1, 1, ff_unit)
    ).reshape(ff_own)

    def quarter(weight, axis):
        size = weight.shape[axis] // reps
        return lax.dynamic_slice_in_dim(weight, q_at * size, size, axis)

    full_qkv = lax.all_gather(quarter(qkv_weight, 0), ALL, axis=0, tiled=True)
    full_out = lax.all_gather(quarter(out_weight, 0), ALL, axis=0, tiled=True)
    proj_own = lax.all_gather(quarter(proj_weight, 0), "z", axis=0, tiled=True)
    fc_view = fc_weight.reshape(width // seqs, zs, ys, reps, ff_unit)
    fc_quarter = lax.dynamic_slice_in_dim(fc_view, q_at, 1, 3)[:, :, :, 0]
    fc_send = fc_quarter.transpose(2, 0, 1, 3).reshape(ys, width // seqs, ff_own)
    fc_pair = lax.all_to_all(fc_send, "y", split_axis=0, concat_axis=0, tiled=True)
    fc_own = lax.all_gather(
        fc_pair.reshape(ys * (width // seqs), ff_own), "z", axis=0, tiled=True
    )

    inputs = to_places(hidden_in[0])
    unit1, rstd1 = norm_parts(inputs)
    normed1 = (unit1 * gain1 + shift1).astype(BF16)
    projected = dot(normed1, full_qkv, NN)
    queries = (projected[:, :width] + qv_full[:width]).astype(BF16)
    kv_shift = jnp.concatenate([jnp.zeros((HD,), F32), qv_full[width:]])
    kv_own = (projected[:, width:] + kv_shift).astype(BF16)
    blocks = []
    for back in range(halo, 0, -1):
        pairs = [(i, i + back) for i in range(seqs - back)]
        blocks.append(lax.ppermute(kv_own, SEQ, pairs))
    kv_ctx = jnp.concatenate(blocks + [kv_own], axis=0)
    seg_own = lax.dynamic_slice_in_dim(segments, first_row, rows)[:, None]
    seg_padded = jnp.concatenate([jnp.full((halo * rows,), -1, jnp.int32), segments])
    seg_ctx = lax.dynamic_slice_in_dim(seg_padded, first_row, ctx)[None, :]
    attended_low, attended, norms = attention_forward(
        queries, kv_ctx, seg_own, seg_ctx, padding_id
    )
    middle = inputs + (dot(attended_low, full_out, NN) + out_shift)

    unit2, rstd2 = norm_parts(middle)
    normed2 = (unit2 * gain2 + shift2).astype(BF16)
    grad_f32 = to_places(out_grad[0])
    grad_low = grad_f32.astype(BF16)
    grad_all = gather_plane(grad_low)
    normed2_all = gather_plane(normed2)
    pre_act = dot(normed2_all, fc_own, NN) + fc_shift_own
    act, slope = gelu_pair(pre_act)
    act_low = act.astype(BF16)
    mlp_out = scatter_plane(dot(act_low, proj_own, NN).astype(BF16))
    result = (middle + mlp_out.astype(F32) + proj_shift).astype(BF16)
    hidden_out = to_stored(result).astype(BF16)
    grad_pre = (dot(grad_all, proj_own, NT) * slope).astype(BF16)
    grad_normed2 = scatter_plane(dot(grad_pre, fc_own, NT).astype(BF16)).astype(F32)
    dfc_bias_own = jnp.sum(grad_pre.astype(F32), axis=0)
    dproj_own = dot(act_low, grad_all, TN).astype(BF16)
    dfc_own = dot(normed2_all, grad_pre, TN).astype(BF16)
    dgain2 = jnp.sum(grad_normed2 * unit2, axis=0)
    dshift2 = jnp.sum(grad_normed2, axis=0)
    dproj_bias = jnp.sum(grad_f32, axis=0)
    grad_middle = grad_f32 + norm_back(grad_normed2, unit2, rstd2, gain2)

    grad_branch = grad_middle.astype(BF16)
    dout_bias = jnp.sum(grad_branch.astype(F32), axis=0)
    grad_attended = dot(grad_branch, full_out, NT).astype(BF16)
    dq, dkv_ctx = attention_backward(
        queries, grad_attended, attended, norms, kv_ctx, seg_own, seg_ctx, padding_id
    )
    dkv = dkv_ctx[halo * rows :]
    for back in range(1, halo + 1):
        pairs = [(i + back, i) for i in range(seqs - back)]
        term = dkv_ctx[(halo - back) * rows : (halo - back + 1) * rows].astype(BF16)
        dkv = dkv + lax.ppermute(term, SEQ, pairs).astype(F32)
    grad_qkv = jnp.concatenate([dq, dkv.astype(BF16)], axis=1)
    grad_normed1 = dot(grad_qkv, full_qkv, NT)
    dgain1 = jnp.sum(grad_normed1 * unit1, axis=0)
    dshift1 = jnp.sum(grad_normed1, axis=0)
    grad_in = grad_middle + norm_back(grad_normed1, unit1, rstd1, gain1)
    input_grad = to_stored(grad_in.astype(BF16))
    grad_qkv_f32 = grad_qkv.astype(F32)
    dqv_bias = jnp.concatenate(
        [jnp.sum(grad_qkv_f32[:, :width], axis=0), jnp.sum(grad_qkv_f32[:, width + HD :], axis=0)]
    )

    def columns_of_plane(values):
        cols = values.shape[1] // plane
        sent = values.reshape(rows, plane, cols).transpose(1, 0, 2)
        return lax.all_to_all(sent, PLANE, split_axis=0, concat_axis=0, tiled=True).reshape(
            plane * rows, cols
        )

    normed1_all = gather_plane(normed1)
    attended_all = gather_plane(attended_low)
    dout_own = dot(attended_all, columns_of_plane(grad_branch), TN).astype(BF16)
    dqkv_own = dot(normed1_all, columns_of_plane(grad_qkv), TN).astype(BF16)

    def over_z(partial):
        return lax.psum_scatter(partial, "z", scatter_dimension=0, tiled=True)

    def by_rows(partial):
        cols = partial.shape[1]
        mine = lax.all_to_all(
            partial.reshape(ys, -1, cols), "y", split_axis=0, concat_axis=0, tiled=True
        )
        return lax.all_gather(mine, REP, axis=0, tiled=False).reshape(reps, ys, -1, cols)

    dproj_weight = lax.all_gather(over_z(dproj_own), REP, axis=0, tiled=True).astype(F32)
    dfc_rows = by_rows(over_z(dfc_own)).reshape(reps, ys, width // seqs, zs, ff_unit)
    dfc_weight = dfc_rows.transpose(2, 3, 1, 0, 4).reshape(width // seqs, ff).astype(F32)
    dout_rows = by_rows(over_z(dout_own))
    dout_weight = dout_rows.transpose(2, 1, 0, 3).reshape(width // seqs, width).astype(F32)
    dqkv_rows = by_rows(over_z(dqkv_own))
    dqkv_weight = dqkv_rows.transpose(2, 1, 0, 3).reshape(width // seqs, qkv_cols).astype(F32)

    dfc_bias = lax.dynamic_update_slice(
        jnp.zeros((zs, ys, reps, ff_unit), F32),
        dfc_bias_own.reshape(zs, 1, 1, ff_unit),
        (0, y_at, q_at, 0),
    ).reshape(ff)
    mids = (dout_bias, dgain2, dshift2, dfc_bias, dproj_bias)
    lasts = (dgain1, dshift1, dqv_bias)

    def reduce_small(items):
        total = lax.psum(jnp.concatenate(items), ALL)
        outs, at = [], 0
        for item in items:
            size = item.shape[0] // seqs
            outs.append(lax.dynamic_slice_in_dim(total, at + seq_at * size, size))
            at += item.shape[0]
        return outs

    dout_bias, dgain2, dshift2, dfc_bias, dproj_bias = reduce_small(mids)
    dgain1, dshift1, dqv_bias = reduce_small(lasts)
    return (
        hidden_out[None],
        input_grad[None],
        dgain1,
        dshift1,
        dqkv_weight,
        dqv_bias,
        dout_weight,
        dout_bias,
        dgain2,
        dshift2,
        dfc_weight,
        dfc_bias,
        dproj_weight,
        dproj_bias,
    )


def solution(mesh):
    seqs, reps = mesh.shape["seq"], mesh.shape["rep"]
    grid = Mesh(mesh.devices.reshape(4, seqs // 4, reps // 2, 2), ALL)
    wide = P(REP, SEQ, None)
    table = P(REP, None)
    vector = P(SEQ)
    matrix = P(SEQ, None)
    return jax.shard_map(
        shards,
        mesh=grid,
        in_specs=(
            wide,
            wide,
            table,
            table,
            vector,
            vector,
            matrix,
            vector,
            matrix,
            vector,
            vector,
            vector,
            matrix,
            vector,
            matrix,
            vector,
        ),
        out_specs=(
            wide,
            wide,
            vector,
            vector,
            matrix,
            vector,
            matrix,
            vector,
            vector,
            vector,
            matrix,
            vector,
            matrix,
            vector,
        ),
        check_vma=False,
    )
```

time: 3580 us -> 1350 us (0.38)
  waiting for transfers between devices: 2650 us -> 728 us
  blocking collectives: 444 us -> 288 us
  local copies, waits for them, and re-layouts: 122 us -> 73.8 us
  other arithmetic: 68.1 us -> 22.1 us
    reduce_scatter x5 -> x6, waiting for transfers between devices: 1340 us -> 287 us  [the longest x4 178 us: over_z(): return lax.psum_scatter(partial, 'z', scatter_dimension=0, tiled=True)]
    all_gather x5 -> x12, waiting for transfers between devices: 1150 us -> 290 us  [the longest x4 167 us: gather_plane(): return lax.all_gather(block, PLANE, axis=0, tiled=True)]
    all_gather x7 -> x0, blocking collectives: 272 us -> none  [the longest x1 97.3 us: shards(): lax.all_gather(out_bias, 'seq', axis=0, tiled=True)]
    unnamed x2 -> x1, blocking collectives: 55.3 us -> 104 us
    dot_general x19 -> x20, matrix products: 190 us -> 157 us  [dot(): lax.dot_general(left, right, (dims, ((), ())), preferred_element_type=F32)]
    all_to_all x1 -> x3, blocking collectives: 110 us -> 143 us  [the longest x1 105 us: exchange(): moved = lax.all_to_all(packed, SEQ, split_axis=0, concat_axis=0, tiled=True)]
  transfers between devices with their start and end apart: 14 -> 30, of which waited for: 10 -> 21; matrix products, arithmetic and copies ran while one was open for 6% -> 15% of each run, Pallas kernels for 0% -> 2%
where the time goes in v1:
time: 1350 us; the launch traced here: 1340 us
  waiting for transfers between devices  728 us (54%)
  blocking collectives  288 us (21%)
  matrix products  157 us (12%)
  local copies, waits for them, and re-layouts  73.8 us (5%)
  starting transfers between devices  36.5 us (3%)
  other arithmetic  22.1 us (2%)
  Pallas kernels  21.5 us (2%)
  between operations  16 us (1%)
    reduce_scatter x4, waiting for transfers between devices, over_z(): return lax.psum_scatter(partial, 'z', scatter_dimension=0, tiled=True)  178 us
    all_gather x4, waiting for transfers between devices, gather_plane(): return lax.all_gather(block, PLANE, axis=0, tiled=True)  167 us
    dot_general x20, matrix products, dot(): lax.dot_general(left, right, (dims, ((), ())), preferred_element_type=F32)  157 us
    reduce_scatter x2, waiting for transfers between devices, scatter_plane(): return lax.psum_scatter(partial, PLANE, scatter_dimension=0, tiled=True)  109 us
    all_to_all x1, blocking collectives, exchange(): moved = lax.all_to_all(packed, SEQ, split_axis=0, concat_axis=0, tiled=True)  105 us
    unnamed x1, blocking collectives  104 us
    psum x1, waiting for transfers between devices, reduce_small(): total = lax.psum(jnp.concatenate(items), ALL)  100 us
    all_gather x1, waiting for transfers between devices, shards(): proj_own = lax.all_gather(quarter(proj_weight, 0), 'z', axis=0, tiled=True)  68.3 us
  transfers between devices with their start and end apart: 30, of which 21 were waited for; matrix products, arithmetic and copies ran while one was open for 15% of the time, Pallas kernels for 2%

profile of v1, /device:TPU:0, one launch (start us, length us, event | category | flops | bytes accessed | tf_op | source)
XLA Modules:
  0.0 1342.7 jit_solution(9406320479091767060)
XLA Ops:
  45.3 103.5 %all-reduce.2 = bf16[22656]{0:T(1024)(128)(2,1)S(1)} all-reduce(bf16[22656]{0:T(1024)(128)(2,1)S(1)} %dynamic-update-slice), channel_id=1, replica_groups=mesh['z'=4,'y'=2,'x'=2,'c'=2] {'z','y'}, use_global_device_ids=true, to_apply=%add.2 | all-reduce | flops 22656 | bytes 90624
  182.0 28.4 %all-gather.18.cloned.1.call-done = bf16[2048,2048]{1,0:T(8,128)(2,1)} async-done(((bf16[64,2048]{1,0:T(8,128)(2,1)}), bf16[2048,2048]{1,0:T(8,128)(2,1)}) %all-gather.18.cloned.1.call-update) | async-done | bytes 8388624 | tf_op jit(solution)/shard_map/all_gather | solution.py:292
  222.6 104.9 %all_to_all.50 = bf16[8,64,2048]{2,1,0:T(8,128)(2,1)S(1)} all-to-all(bf16[8,64,2048]{2,1,0:T(8,128)(2,1)S(1)} %bitcast.116), channel_id=1, replica_groups=mesh['z'=4,'y'=2,'x'=2,'c'=2] {'z','y'}, dimensions={0} | all-to-all | bytes 4194304 | tf_op jit(solution)/shard_map/all_to_all | solution.py:255
  335.8 55.2 %all-gather.20.cloned.1.call-done = bf16[2048,2048]{1,0:T(8,128)(2,1)} async-done(((bf16[256,2048]{1,0:T(8,128)(2,1)}), bf16[2048,2048]{1,0:T(8,128)(2,1)}) %all-gather.20.cloned.1.call-update) | async-done | bytes 8388624 | tf_op jit(solution)/shard_map/all_gather | solution.py:183
  391.0 14.5 %fusion.55 = f32[2048,1024]{1,0:T(8,128)} fusion(bf16[2048,2048]{1,0:T(8,128)(2,1)} %all-gather.20.cloned.1.call-done, bf16[2048,1024]{1,0:T(8,128)(2,1)} %all-gather.22.cloned.1.call-done), kind=kOutput, calls=%fused_computation.146 | convolution fusion | flops 8589934592 | bytes 20971520 | tf_op jit(solution)/shard_map/dot_general | solution.py:28
  405.5 68.3 %all-gather.24.cloned.1.call-done = bf16[1024,2048]{1,0:T(8,128)(2,1)} async-done(((bf16[256,2048]{1,0:T(8,128)(2,1)}), bf16[1024,2048]{1,0:T(8,128)(2,1)}) %all-gather.24.cloned.1.call-update) | async-done | bytes 4194320 | tf_op jit(solution)/shard_map/all_gather | solution.py:293
  473.8 54.7 %all-gather.26.cloned.1.call-done = bf16[2048,2048]{1,0:T(8,128)(2,1)} async-done(((bf16[256,2048]{1,0:T(8,128)(2,1)}), bf16[2048,2048]{1,0:T(8,128)(2,1)}) %all-gather.26.cloned.1.call-update) | async-done | bytes 8388624 | tf_op jit(solution)/shard_map/all_gather | solution.py:183
  528.5 20.4 %convert_reduce_fusion = (f32[1024]{0:T(1024)}, bf16[2048,1024]{1,0:T(8,128)(2,1)S(1)}) fusion(f32[2048,1024]{1,0:T(8,128)} %fusion.55, f32[1024]{0:T(1024)S(1)} %bitcast.148, bf16[2048,2048]{1,0:T(8,128)(2,1)} %all-gather.26.cloned.1.call-done, bf16[1024,2048]{1,0:T(8,128)(2,1)} %all-gather.24.cloned.1.call-done), kind=kOutput, calls=%fused_computation.9 | convolution fusion | flops 8636070912 | bytes 25174016 | tf_op jit(solution)/shard_map/dot_general | solution.py:28
  563.8 17.1 %convolution_convert_fusion.2 = bf16[1024,2048]{1,0:T(8,128)(2,1)} fusion(bf16[2048,2048]{1,0:T(8,128)(2,1)} %all-gather.26.cloned.1.call-done, f32[2048,1024]{1,0:T(8,128)} %fusion.55, f32[1024]{0:T(1024)S(1)} %bitcast.149), kind=kOutput, calls=%fused_computation.13 | convolution fusion | flops 8613003264 | bytes 20975616 | tf_op jit(solution)/shard_map/dot_general | solution.py:28
  581.0 14.2 %convolution_convert_fusion.3 = bf16[2048,1024]{1,0:T(8,128)(2,1)} fusion(bf16[2048,2048]{1,0:T(8,128)(2,1)} %all-gather.20.cloned.1.call-done, bf16[2048,1024]{1,0:T(8,128)(2,1)} %copy-done.55), kind=kOutput, calls=%fused_computation.14 | convolution fusion | flops 8592031744 | bytes 16777216 | tf_op jit(solution)/shard_map/dot_general | solution.py:28
  595.2 38.5 %reduce-scatter.9.cloned.1.call-done = bf16[256,2048]{1,0:T(8,128)(2,1)} async-done(((bf16[2048,2048]{1,0:T(8,128)(2,1)}), bf16[256,2048]{1,0:T(8,128)(2,1)}) %reduce-scatter.9.cloned.1.call-update) | async-done | bytes 1048592 | tf_op jit(solution)/shard_map/reduce_scatter | solution.py:187
  644.8 57.2 %all-gather.30.cloned.1.call-done = bf16[2048,2048]{1,0:T(8,128)(2,1)} async-done(((bf16[256,2048]{1,0:T(8,128)(2,1)}), bf16[2048,2048]{1,0:T(8,128)(2,1)}) %all-gather.30.cloned.1.call-update) | async-done | bytes 8388624 | tf_op jit(solution)/shard_map/all_gather | solution.py:183
  708.9 16.6 %convolution_convert_fusion.1 = bf16[2048,2048]{1,0:T(8,128)(2,1)} fusion(bf16[1024,2048]{1,0:T(8,128)(2,1)} %all-gather.24.cloned.1.call-done, f32[2048,1024]{1,0:T(8,128)} %fusion.55, f32[1024]{0:T(1024)S(1)} %bitcast.150), kind=kOutput, calls=%fused_computation.12 | convolution fusion | flops 8615100416 | bytes 20975616 | tf_op jit(solution)/shard_map/dot_general | solution.py:28
  759.1 19.4 %all_to_all.51 = bf16[8,256,288]{1,2,0:T(8,128)(2,1)S(1)} all-to-all(bf16[8,256,288]{1,2,0:T(8,128)(2,1)S(1)} %bitcast.118), channel_id=1, replica_groups=mesh['z'=4,'y'=2,'x'=2,'c'=2] {'y','x','c'}, dimensions={0} | all-to-all | bytes 2359296 | tf_op jit(solution)/shard_map/all_to_all | solution.py:369
  786.7 53.6 %reduce-scatter.17.cloned.1.call-done = bf16[256,2048]{1,0:T(8,128)(2,1)} async-done(((bf16[1024,2048]{1,0:T(8,128)(2,1)}), bf16[256,2048]{1,0:T(8,128)(2,1)}) %reduce-scatter.17.cloned.1.call-update) | async-done | bytes 1048592 | tf_op jit(solution)/shard_map/reduce_scatter | solution.py:379
  840.4 79.5 %reduce-scatter.15.cloned.1.call-done = bf16[512,1024]{1,0:T(8,128)(2,1)} async-done(((bf16[2048,1024]{1,0:T(8,128)(2,1)}), bf16[512,1024]{1,0:T(8,128)(2,1)}) %reduce-scatter.15.cloned.1.call-update) | async-done | bytes 1048592 | tf_op jit(solution)/shard_map/reduce_scatter | solution.py:379
  920.0 18.4 %all_to_all.52 = bf16[2,256,1024]{2,1,0:T(8,128)(2,1)} all-to-all(bf16[2,256,1024]{2,1,0:T(8,128)(2,1)} %bitcast.125), channel_id=1, replica_groups=mesh['z'=4,'y'=2,'x'=2,'c'=2] {'y'}, dimensions={0} | all-to-all | bytes 2097152 | tf_op jit(solution)/shard_map/all_to_all | solution.py:383
  938.4 12.1 reduce-scatter.13.cloned.1.call-done
  953.9 70.6 %reduce-scatter.7.cloned.1.call-done = bf16[256,2048]{1,0:T(8,128)(2,1)} async-done(((bf16[2048,2048]{1,0:T(8,128)(2,1)}), bf16[256,2048]{1,0:T(8,128)(2,1)}) %reduce-scatter.7.cloned.1.call-update) | async-done | bytes 1048592 | tf_op jit(solution)/shard_map/reduce_scatter | solution.py:187
  1041.9 32.3 %reduce-scatter.11.cloned.1.call-done = bf16[512,288]{0,1:T(8,128)(2,1)} async-done(((bf16[2048,288]{0,1:T(8,128)(2,1)}), bf16[512,288]{0,1:T(8,128)(2,1)}) %reduce-scatter.11.cloned.1.call-update) | async-done | bytes 294928 | tf_op jit(solution)/shard_map/reduce_scatter | solution.py:379
  1075.9 24.5 %all-to-all-done.2 = bf16[8,64,2048]{2,1,0:T(8,128)(2,1)} async-done(((bf16[8,64,2048]{2,1,0:T(8,128)(2,1)}), bf16[8,64,2048]{2,1,0:T(8,128)(2,1)}, u32[]{:S(2)}, u32[]{:S(2)}) %all-to-all-start.2) | async-done | bytes 2097184 | tf_op jit(solution)/shard_map/all_to_all | solution.py:255
  1115.6 100.0 %all-reduce.5.cloned.1.call-done = f32[16384]{0:T(1024)} async-done(((f32[16384]{0:T(1024)}), f32[16384]{0:T(1024)}) %all-reduce.5.cloned.1.call-update) | async-done | bytes 65552 | tf_op jit(solution)/shard_map/psum | solution.py:405
  1218.4 41.5 %psum.14 = f32[6272]{0:T(1024)S(1)} all-reduce(f32[6272]{0:T(1024)S(1)} %pad_maximum_fusion.2), channel_id=1, replica_groups=mesh['z'=4,'y'=2,'x'=2,'c'=2] {'z','y','x','c'}, use_global_device_ids=true, to_apply=%region_16.17 | all-reduce | flops 6272 | bytes 50176 | tf_op jit(solution)/shard_map/psum | solution.py:405
  1268.4 20.4 %all-gather.38.cloned.1.call-done = bf16[8,256,1024]{2,1,0:T(8,128)(2,1)} async-done(((bf16[2,256,1024]{2,1,0:T(8,128)(2,1)}), bf16[8,256,1024]{2,1,0:T(8,128)(2,1)}) %all-gather.38.cloned.1.call-update) | async-done | bytes 4194320 | tf_op jit(solution)/shard_map/all_gather | solution.py:386
  (287 shorter events, 260.8 us)
Async XLA Ops:
  7.2 147.3 %all-gather.16.cloned.1.call-start = ((), (), s32[]{:S(2)}) async-start(), calls=%async_computation.16 | async-start | bytes 9732096 | tf_op jit(solution)/shard_map/all_gather | solution.py:291
  9.2 201.2 %all-gather.18.cloned.1.call-start = ((), (), s32[]{:S(2)}) async-start(), calls=%async_computation.17 | async-start | bytes 8650752 | tf_op jit(solution)/shard_map/all_gather | solution.py:292
  38.9 112.9 %all-to-all-start = ((bf16[8,64,2048]{2,1,0:T(8,128)(2,1)}), bf16[8,64,2048]{2,1,0:T(8,128)(2,1)S(1)}, u32[]{:S(2)}, u32[]{:S(2)}) async-start(bf16[8,64,2048]{2,1,0:T(8,128)(2,1)} %bitcast.113), calls=%async_computation | async-start | bytes 4194304 | tf_op jit(solution)/shard_map/all_to_all | solution.py:255
  43.5 292.3 %all-gather.22.cloned.1.call-start = ((), (), s32[]{:S(2)}) async-start(), calls=%async_computation.19 | async-start | bytes 5242880 | tf_op jit(solution)/shard_map/all_gather | solution.py:298
  150.4 240.6 %all-gather.20.cloned.1.call-start = ((), (), s32[]{:S(2)}) async-start(), calls=%async_computation.18 | async-start | bytes 9437184 | tf_op jit(solution)/shard_map/all_gather | solution.py:183
  218.9 254.9 %all-gather.24.cloned.1.call-start = ((), (), s32[]{:S(2)}) async-start(), calls=%async_computation.20 | async-start | bytes 5242880 | tf_op jit(solution)/shard_map/all_gather | solution.py:293
  221.4 307.1 %all-gather.26.cloned.1.call-start = ((), (), s32[]{:S(2)}) async-start(), calls=%async_computation.22 | async-start | bytes 9437184 | tf_op jit(solution)/shard_map/all_gather | solution.py:183
  329.9 303.8 %reduce-scatter.9.cloned.1.call-start = ((), (), s32[]{:S(2)}) async-start(), calls=%async_computation.23 | async-start | bytes 9437184 | tf_op jit(solution)/shard_map/reduce_scatter | solution.py:187
  562.3 139.7 %all-gather.30.cloned.1.call-start = ((), (), s32[]{:S(2)}) async-start(), calls=%async_computation.26 | async-start | bytes 9437184 | tf_op jit(solution)/shard_map/all_gather | solution.py:183
  563.1 215.6 %all-gather.28.cloned.1.call-start = ((), (), s32[]{:S(2)}) async-start(), calls=%async_computation.24 | async-start | bytes 9437184 | tf_op jit(solution)/shard_map/all_gather | solution.py:183
  563.8 276.6 %reduce-scatter.17.cloned.1.call-start = ((), (), s32[]{:S(2)}) async-start(), calls=%async_computation.30 | async-start | bytes 5242880 | tf_op jit(solution)/shard_map/reduce_scatter | solution.py:379
  580.9 339.0 %reduce-scatter.15.cloned.1.call-start = ((), (), s32[]{:S(2)}) async-start(), calls=%async_computation.29 | async-start | bytes 5242880 | tf_op jit(solution)/shard_map/reduce_scatter | solution.py:379
  641.1 60.9 %all-to-all-start.7 = ((bf16[8,256,256]{2,1,0:T(8,128)(2,1)}), bf16[8,256,256]{2,1,0:T(8,128)(2,1)S(1)}, u32[]{:S(2)}, u32[]{:S(2)}) async-start(bf16[8,256,256]{2,1,0:T(8,128)(2,1)} %bitcast.107), calls=%async_computation.10 | async-start | bytes 2097152 | tf_op jit(solution)/shard_map/all_to_all | solution.py:369
  644.7 305.8 %reduce-scatter.13.cloned.1.call-start = ((), (), s32[]{:S(2)}) async-start(), calls=%async_computation.27 | async-start | bytes 1310720 | tf_op jit(solution)/shard_map/reduce_scatter | solution.py:379
  708.9 315.6 %reduce-scatter.7.cloned.1.call-start = ((), (), s32[]{:S(2)}) async-start(), calls=%async_computation.21 | async-start | bytes 9437184 | tf_op jit(solution)/shard_map/reduce_scatter | solution.py:187
  725.6 348.6 %reduce-scatter.11.cloned.1.call-start = ((), (), s32[]{:S(2)}) async-start(), calls=%async_computation.25 | async-start | bytes 1474560 | tf_op jit(solution)/shard_map/reduce_scatter | solution.py:379
  785.8 429.8 %all-reduce.5.cloned.1.call-start = ((), (), s32[]{:S(2)}) async-start(), calls=%async_computation.28 | async-start | bytes 131072 | tf_op jit(solution)/shard_map/psum | solution.py:405
  786.7 474.6 %all-gather.32.cloned.1.call-start = ((), (), s32[]{:S(2)}) async-start(), calls=%async_computation.31 | async-start | bytes 5242880 | tf_op jit(solution)/shard_map/all_gather | solution.py:388
  840.4 448.5 %all-gather.38.cloned.1.call-start = ((), (), s32[]{:S(2)}) async-start(), calls=%async_computation.34 | async-start | bytes 5242880 | tf_op jit(solution)/shard_map/all_gather | solution.py:386
  950.5 77.4 %all-to-all-start.8 = ((bf16[2,256,256]{2,1,0:T(8,128)(2,1)}), bf16[2,256,256]{2,1,0:T(8,128)(2,1)S(1)}, u32[]{:S(2)}, u32[]{:S(2)}) async-start(bf16[2,256,256]{2,1,0:T(8,128)(2,1)} %bitcast.128), calls=%async_computation.12 | async-start | bytes 524288 | tf_op jit(solution)/shard_map/all_to_all | solution.py:383
  1027.9 72.5 %all-to-all-start.2 = ((bf16[8,64,2048]{2,1,0:T(8,128)(2,1)}), bf16[8,64,2048]{2,1,0:T(8,128)(2,1)}, u32[]{:S(2)}, u32[]{:S(2)}) async-start(bf16[8,64,2048]{2,1,0:T(8,128)(2,1)} %bitcast.114), calls=%async_computation.3 | async-start | bytes 4194304 | tf_op jit(solution)/shard_map/all_to_all | solution.py:255
  1109.6 214.2 %all-to-all-start.4 = ((bf16[8,64,2048]{2,1,0:T(8,128)(2,1)}), bf16[8,64,2048]{2,1,0:T(8,128)(2,1)}, u32[]{:S(2)}, u32[]{:S(2)}) async-start(bf16[8,64,2048]{2,1,0:T(8,128)(2,1)} %bitcast.111), calls=%async_computation.6 | async-start | bytes 4194304 | tf_op jit(solution)/shard_map/all_to_all | solution.py:255
  1114.3 213.3 %all-gather.36.cloned.1.call-start = ((), (), s32[]{:S(2)}) async-start(), calls=%async_computation.33 | async-start | bytes 1310720 | tf_op jit(solution)/shard_map/all_gather | solution.py:386
  1114.8 217.6 %all-gather.34.cloned.1.call-start = ((), (), s32[]{:S(2)}) async-start(), calls=%async_computation.32 | async-start | bytes 1474560 | tf_op jit(solution)/shard_map/all_gather | solution.py:386
  (63 other events, 2159.7 us)
Sparse Core Ops, SparseCore 0:
  11.5 118.9 all-gather.15
  133.9 76.4 all-gather.17
  211.9 123.8 all-gather.21
  338.1 52.8 all-gather.19
  393.0 80.7 all-gather.23
  475.6 52.9 all-gather.25
  562.4 71.2 reduce-scatter.8
  636.4 65.6 all-gather.29
  704.1 57.1 all-gather.27
  763.5 76.7 reduce-scatter.16
  842.7 77.2 reduce-scatter.14
  922.8 27.6 reduce-scatter.12
  954.5 69.9 reduce-scatter.6
  1027.4 46.8 reduce-scatter.10
  1080.6 134.9 all-reduce.4
  1217.1 35.6 all-gather.31
  1254.3 34.5 all-gather.37
  1290.3 16.7 all-gather.35
  1308.7 17.4 all-gather.33

commit v2 on v1

--- a/solution.py
+++ b/solution.py
@@ -1,4 +1,5 @@
 import functools
+import itertools
 import math
 
 import jax
@@ -179,12 +180,177 @@
     return value, slope
 
 
+def swap(block, axis):
+    return lax.ppermute(block, axis, [(0, 1), (1, 0)])
+
+
+def pair(block, axis):
+    if lax.axis_size(axis) != 2:
+        return lax.all_gather(block, axis, axis=0, tiled=False)
+    other = swap(block, axis)
+    first = lax.axis_index(axis) == 0
+    return jnp.stack([jnp.where(first, block, other), jnp.where(first, other, block)])
+
+
+def small_plane():
+    return lax.axis_size("y") == 2
+
+
+def plane_pieces(block):
+    if not small_plane():
+        return [lax.all_gather(block, PLANE, axis=0, tiled=True)]
+    half = block.shape[0] // 2
+    top, low = block[:half], block[half:]
+    top_x, low_y = swap(top, "x"), swap(low, "y")
+    top_y, low_x = swap(top, "y"), swap(low, "x")
+    top_xy, low_yx = swap(top_x, "y"), swap(low_y, "x")
+    near = [top, top_y, top_x, top_xy, low, low_x, low_y, low_yx]
+    return near + [swap(item, "c") for item in near]
+
+
 def gather_plane(block):
-    return lax.all_gather(block, PLANE, axis=0, tiled=True)
-
-
-def scatter_plane(partial):
-    return lax.psum_scatter(partial, PLANE, scatter_dimension=0, tiled=True)
+    return jnp.concatenate(plane_pieces(block), axis=0)
+
+
+def scatter_plane(partial, rows, hold=None):
+    total = rows * lax.axis_size("y") * lax.axis_size("x") * lax.axis_size("c")
+    if not small_plane():
+        return lax.psum_scatter(
+            partial(0, total).astype(BF16), PLANE, scatter_dimension=0, tiled=True
+        ).astype(F32)
+    side = total // 2
+    got = swap(partial(side, side).astype(BF16), "c")
+    both = (partial(0, side) + got.astype(F32)).astype(BF16)
+    if hold is not None:
+        both, _ = together(both, hold)
+    top, low = both[: side // 2], both[side // 2 :]
+    got_top, got_low = swap(top[rows:], "x"), swap(low[rows:], "y")
+    top = (top[:rows].astype(F32) + got_top.astype(F32)).astype(BF16)
+    low = (low[:rows].astype(F32) + got_low.astype(F32)).astype(BF16)
+    half = rows // 2
+    got_top, got_low = swap(top[half:], "y"), swap(low[half:], "x")
+    return jnp.concatenate(
+        [
+            top[:half].astype(F32) + got_top.astype(F32),
+            low[:half].astype(F32) + got_low.astype(F32),
+        ],
+        axis=0,
+    )
+
+
+def shift(block, axis, by):
+    count = math.prod(lax.axis_size(a) for a in ([axis] if isinstance(axis, str) else axis))
+    return lax.ppermute(block, axis, [(i, (i + by) % count) for i in range(count)])
+
+
+def place_kernel(count, parts, offsets, *refs):
+    out = refs[count]
+    for i in range(count):
+        rows = refs[i].shape[0] // parts
+        for j in range(parts):
+            start = pl.multiple_of(offsets[i * parts + j], rows)
+            out[pl.ds(start, rows), :] = refs[i][j * rows : (j + 1) * rows, :]
+
+
+def place_rows(pieces, parts, offsets):
+    count = len(pieces)
+    rows, width = pieces[0].shape
+    return pl.pallas_call(
+        functools.partial(place_kernel, count, parts),
+        grid_spec=pltpu.PrefetchScalarGridSpec(
+            num_scalar_prefetch=1,
+            grid=(1,),
+            in_specs=[pl.BlockSpec((rows, width), lambda i, at: (0, 0))] * count,
+            out_specs=pl.BlockSpec((count * rows, width), lambda i, at: (0, 0)),
+        ),
+        out_shape=jax.ShapeDtypeStruct((count * rows, width), pieces[0].dtype),
+        compiler_params=pltpu.CompilerParams(vmem_limit_bytes=56 * 1024 * 1024),
+        cost_estimate=pl.CostEstimate(
+            flops=0, bytes_accessed=4 * count * rows * width, transcendentals=0
+        ),
+        name="place_rows",
+    )(offsets, *pieces)
+
+
+def assemble_kernel(count, slices, by_column, rolled, offsets, *refs):
+    outs = refs[count:]
+    if rolled is not None:
+        total = jnp.zeros((refs[0].shape[0], 2 * HD), F32)
+    for i in range(count):
+        for row, rows, first, cols, target, base in slices:
+            values = refs[i][row : row + rows, first : first + cols].astype(F32)
+            if by_column:
+                start = pl.multiple_of(offsets[i] + base, HD)
+                outs[target][:, pl.ds(start, cols)] = values
+            else:
+                start = pl.multiple_of(offsets[i], rows)
+                outs[target][pl.ds(start, rows), base : base + cols] = values
+        if rolled is not None:
+            first, wide, target, at = rolled
+            narrow = refs[i][:, first : first + wide].astype(F32)
+            padded = jnp.concatenate(
+                [narrow, jnp.zeros((narrow.shape[0], 2 * HD - wide), F32)], axis=1
+            )
+            total = total + pltpu.roll(padded, offsets[i] * wide // slices[0][3], 1)
+    if rolled is not None:
+        outs[target][:, at : at + 2 * HD] = total
+
+
+def assemble(pieces, slices, shapes, offsets, by_column=False, rolled=None):
+    count = len(pieces)
+    rows, width = pieces[0].shape
+    return pl.pallas_call(
+        functools.partial(assemble_kernel, count, slices, by_column, rolled),
+        grid_spec=pltpu.PrefetchScalarGridSpec(
+            num_scalar_prefetch=1,
+            grid=(1,),
+            in_specs=[pl.BlockSpec((rows, width), lambda i, at: (0, 0))] * count,
+            out_specs=[pl.BlockSpec(shape, lambda i, at: (0, 0)) for shape in shapes],
+        ),
+        out_shape=[jax.ShapeDtypeStruct(shape, F32) for shape in shapes],
+        compiler_params=pltpu.CompilerParams(vmem_limit_bytes=56 * 1024 * 1024),
+        cost_estimate=pl.CostEstimate(
+            flops=0, bytes_accessed=6 * count * rows * width, transcendentals=0
+        ),
+        name="assemble_rows",
+    )(offsets, *pieces)
+
+
+def together(*values):
+    return lax.optimization_barrier(values)
+
+
+def spread_near(column):
+    side = column.shape[0] // 2
+    near = []
+    for part in range(2):
+        own = column[part * side : (part + 1) * side]
+        one, two = ("x", "y") if part == 0 else ("y", "x")
+        near += [own, swap(own, one), swap(own, two)]
+    return near
+
+
+def spread_far(near):
+    zs = lax.axis_size("z")
+    y, x, c = (lax.axis_index(a) for a in PLANE)
+    rows = near[0].shape[0] // (zs // 2)
+    pieces, offsets = [], []
+    for part in range(2):
+        one, two = ("x", "y") if part == 0 else ("y", "x")
+        own, by_one, by_two = near[3 * part : 3 * part + 3]
+        for item, at_one, at_two in (
+            (own, 0, 0),
+            (by_one, 1, 0),
+            (by_two, 0, 1),
+            (swap(by_one, two), 1, 1),
+        ):
+            dx, dy = (at_one, at_two) if one == "x" else (at_two, at_one)
+            for dc in range(2):
+                pieces.append(swap(item, "c") if dc else item)
+                source = ((y ^ dy) * 2 + (x ^ dx)) * 2 + (c ^ dc)
+                for z in range(zs // 2):
+                    offsets.append(((part * (zs // 2) + z) * 8 + source) * rows)
+    return place_rows(pieces, zs // 2, jnp.stack(offsets).astype(jnp.int32))
 
 
 def shards(
@@ -209,24 +375,39 @@
     reps = xs * cs
     plane = ys * reps
     seqs = zs * ys
-    z_at = lax.axis_index("z")
-    y_at = lax.axis_index("y")
-    q_at = lax.axis_index("x") * cs + lax.axis_index("c")
+    z_at, y_at, x_at, c_at = (lax.axis_index(a) for a in ALL)
+    q_at = x_at * cs + c_at
     f_at = y_at * reps + q_at
     seq_at = z_at * ys + y_at
     rows = hidden_in.shape[1]
     width = hidden_in.shape[2]
     window = rows * seqs
     capacity = 2 * rows // seqs
-    slots = seqs * capacity
     halo = max(1, seqs // 4)
     ctx = (halo + 1) * rows
     padding_id = max(8, window // 256) - 1
     qkv_cols = qkv_weight.shape[1]
     ff = fc_weight.shape[1]
-    ff_block = ff // seqs
-    ff_unit = ff_block // reps
+    ff_unit = ff // seqs // reps
     ff_own = zs * ff_unit
+    shard = width // seqs
+
+    def fc_columns(y):
+        picked = []
+        for z in range(zs):
+            start = ((z * ys + y) * reps + q_at) * ff_unit
+            picked.append(lax.dynamic_slice_in_dim(fc_weight, start, ff_unit, 1))
+        return jnp.concatenate(picked, axis=1)
+
+    if ys == 2:
+        fc_mine, fc_other = fc_columns(y_at), swap(fc_columns(1 - y_at), "y")
+        fc_pair = jnp.concatenate(
+            [jnp.where(y_at == 0, fc_mine, fc_other), jnp.where(y_at == 0, fc_other, fc_mine)]
+        )
+    else:
+        fc_pair = lax.all_to_all(
+            jnp.stack([fc_columns(y) for y in range(ys)]), "y", 0, 0, tiled=True
+        ).reshape(ys * shard, ff_own)
 
     places = row_position[0]
     segments = segment_ids[0]
@@ -238,9 +419,8 @@
     same = (targets[:, :, None] == targets[:, None, :]) & earlier[None]
     ranks = jnp.sum(same.astype(jnp.int32), axis=2).reshape(window)
     first_row = seq_at * rows
-    own_places_stored = lax.dynamic_slice_in_dim(places, first_row, rows)
-    own_ranks = lax.dynamic_slice_in_dim(ranks, first_row, rows)
-    send_slots = own_places_stored // rows * capacity + own_ranks
+    slots = seqs * capacity
+    send_slots = lax.dynamic_slice_in_dim(places // rows * capacity + ranks, first_row, rows)
     arrive_slots = jnp.arange(window, dtype=jnp.int32) // rows * capacity + ranks
     own_places = first_row + jnp.arange(rows, dtype=jnp.int32)
     recv_slots = jnp.sum(
@@ -250,6 +430,27 @@
     pick_send = (send_slots[:, None] == slot_ids[None, :]).astype(BF16)
     pick_recv = (recv_slots[:, None] == slot_ids[None, :]).astype(BF16)
 
+    def exchange_first(values):
+        wide = capacity + extra
+        wide_ids = jnp.arange(seqs * wide, dtype=jnp.int32)
+        send_wide = send_slots // capacity * wide + send_slots % capacity
+        recv_wide = recv_slots // capacity * wide + recv_slots % capacity
+        pick_rows = (send_wide[:, None] == wide_ids[None, :]).astype(BF16)
+        pick_small = (wide_ids % wide - capacity)[None, :] == jnp.arange(extra)[:, None]
+        packed = dot(
+            jnp.concatenate([pick_rows, pick_small.astype(BF16)], axis=0),
+            jnp.concatenate([values, small_rows], axis=0),
+            TN,
+        )
+        packed = packed.astype(BF16).reshape(seqs, wide, width)
+        moved = lax.all_to_all(packed, SEQ, split_axis=0, concat_axis=0, tiled=True)
+        return moved, recv_wide, wide_ids
+
+    def arrive_first(moved, recv_wide, wide_ids):
+        pick_wide = (recv_wide[:, None] == wide_ids[None, :]).astype(BF16)
+        every = moved[:, capacity:].reshape(seqs, extra * width)[:, : small.shape[0]]
+        return dot(pick_wide, moved.reshape(wide_ids.shape[0], width), NN), every.astype(F32)
+
     def exchange(values, pick_out, pick_in):
         packed = dot(pick_out, values, TN).astype(BF16).reshape(seqs, capacity, values.shape[1])
         moved = lax.all_to_all(packed, SEQ, split_axis=0, concat_axis=0, tiled=True)
@@ -261,13 +462,7 @@
     def to_stored(values):
         return exchange(values, pick_recv, pick_send)
 
-    small = jnp.concatenate(
-        [gain_first, shift_first, qv_bias, out_bias, gain_second, shift_second, fc_bias, proj_bias]
-    )
-    small_all = lax.all_gather(small, SEQ, axis=0, tiled=True).reshape(seqs, -1).astype(F32)
-    parts = []
-    at = 0
-    for item in (
+    vectors = (
         gain_first,
         shift_first,
         qv_bias,
@@ -276,30 +471,59 @@
         shift_second,
         fc_bias,
         proj_bias,
-    ):
-        parts.append(small_all[:, at : at + item.shape[0]].reshape(-1))
+    )
+    small = jnp.concatenate(vectors)
+    extra = -(-small.shape[0] // (8 * width)) * 8
+    small_rows = jnp.pad(small, (0, extra * width - small.shape[0])).reshape(extra, width)
+
+    def quarter(weight):
+        size = weight.shape[0] // reps
+        return lax.dynamic_slice_in_dim(weight, q_at * size, size, 0)
+
+    proj_rows = quarter(proj_weight)
+    parts = [slice(p * ff_own, (p + 1) * ff_own) for p in range(width // ff_own)]
+    fc_rows = ys * shard
+    units_part = jnp.concatenate([fc_pair] + [proj_rows[:, part] for part in parts], axis=0)
+    with jax.named_scope("attention_weights"):
+        if small_plane():
+            columns = lax.all_gather(
+                jnp.concatenate([quarter(qkv_weight), quarter(out_weight)], axis=1),
+                "z",
+                axis=0,
+                tiled=True,
+            )
+        else:
+            columns = lax.all_gather(quarter(qkv_weight), ALL, axis=0, tiled=True)
+    with jax.named_scope("hidden_to_places"):
+        moved, *picks = exchange_first(hidden_in[0])
+    units_part, grad_stored, columns, moved = together(
+        units_part, out_grad[0], columns, moved
+    )
+    with jax.named_scope("units_gather"):
+        hidden_units = lax.all_gather(units_part, "z", axis=0, tiled=False)
+
+    with jax.named_scope("hidden_to_places"):
+        inputs, small_all = arrive_first(moved, *picks)
+    if small_plane():
+        qkv_near = spread_near(columns[:, :qkv_cols])
+        out_column, *qkv_near = together(columns[:, qkv_cols:], *qkv_near)
+        with jax.named_scope("qkv_gather"):
+            full_qkv = spread_far(qkv_near)
+        with jax.named_scope("out_gather"):
+            full_out = spread_far(spread_near(out_column))
+    else:
+        full_qkv = columns
+        full_out = lax.all_gather(quarter(out_weight), ALL, axis=0, tiled=True)
+    wholes = []
+    at = 0
+    for item in vectors:
+        wholes.append(small_all[:, at : at + item.shape[0]].reshape(-1))
         at += item.shape[0]
-    gain1, shift1, qv_full, out_shift, gain2, shift2, fc_shift, proj_shift = parts
+    gain1, shift1, qv_full, out_shift, gain2, shift2, fc_shift, proj_shift = wholes
     fc_shift_own = lax.dynamic_slice(
         fc_shift.reshape(zs, ys, reps, ff_unit), (0, y_at, q_at, 0), (zs, 1, 1, ff_unit)
     ).reshape(ff_own)
 
-    def quarter(weight, axis):
-        size = weight.shape[axis] // reps
-        return lax.dynamic_slice_in_dim(weight, q_at * size, size, axis)
-
-    full_qkv = lax.all_gather(quarter(qkv_weight, 0), ALL, axis=0, tiled=True)
-    full_out = lax.all_gather(quarter(out_weight, 0), ALL, axis=0, tiled=True)
-    proj_own = lax.all_gather(quarter(proj_weight, 0), "z", axis=0, tiled=True)
-    fc_view = fc_weight.reshape(width // seqs, zs, ys, reps, ff_unit)
-    fc_quarter = lax.dynamic_slice_in_dim(fc_view, q_at, 1, 3)[:, :, :, 0]
-    fc_send = fc_quarter.transpose(2, 0, 1, 3).reshape(ys, width // seqs, ff_own)
-    fc_pair = lax.all_to_all(fc_send, "y", split_axis=0, concat_axis=0, tiled=True)
-    fc_own = lax.all_gather(
-        fc_pair.reshape(ys * (width // seqs), ff_own), "z", axis=0, tiled=True
-    )
-
-    inputs = to_places(hidden_in[0])
     unit1, rstd1 = norm_parts(inputs)
     normed1 = (unit1 * gain1 + shift1).astype(BF16)
     projected = dot(normed1, full_qkv, NN)
@@ -317,25 +541,52 @@
     attended_low, attended, norms = attention_forward(
         queries, kv_ctx, seg_own, seg_ctx, padding_id
     )
+    with jax.named_scope("grad_to_places"):
+        grad_f32 = to_places(grad_stored)
+    attended_low, grad_f32 = together(attended_low, grad_f32)
+    grad_low = grad_f32.astype(BF16)
+    with jax.named_scope("grad_gather"):
+        grad_all = gather_plane(grad_low)
     middle = inputs + (dot(attended_low, full_out, NN) + out_shift)
 
     unit2, rstd2 = norm_parts(middle)
     normed2 = (unit2 * gain2 + shift2).astype(BF16)
-    grad_f32 = to_places(out_grad[0])
-    grad_low = grad_f32.astype(BF16)
-    grad_all = gather_plane(grad_low)
-    normed2_all = gather_plane(normed2)
+    with jax.named_scope("normed2_gather"):
+        normed2_all = gather_plane(normed2)
+    with jax.named_scope("both_gather"):
+        both_low, normed2_all = together(
+            jnp.concatenate([normed1, attended_low], axis=1), normed2_all
+        )
+        both_all = lax.all_gather(both_low, PLANE, axis=0, tiled=True)
+    fc_own = hidden_units[:, :fc_rows].reshape(width, ff_own)
+    proj_parts = [
+        hidden_units[:, fc_rows + p * ff_unit : fc_rows + (p + 1) * ff_unit].reshape(ff_own, ff_own)
+        for p in range(len(parts))
+    ]
+
     pre_act = dot(normed2_all, fc_own, NN) + fc_shift_own
     act, slope = gelu_pair(pre_act)
     act_low = act.astype(BF16)
-    mlp_out = scatter_plane(dot(act_low, proj_own, NN).astype(BF16))
-    result = (middle + mlp_out.astype(F32) + proj_shift).astype(BF16)
-    hidden_out = to_stored(result).astype(BF16)
-    grad_pre = (dot(grad_all, proj_own, NT) * slope).astype(BF16)
-    grad_normed2 = scatter_plane(dot(grad_pre, fc_own, NT).astype(BF16)).astype(F32)
+    grad_act = sum(dot(grad_all[:, part], own, NT) for part, own in zip(parts, proj_parts))
+    grad_pre = (grad_act * slope).astype(BF16)
     dfc_bias_own = jnp.sum(grad_pre.astype(F32), axis=0)
-    dproj_own = dot(act_low, grad_all, TN).astype(BF16)
-    dfc_own = dot(normed2_all, grad_pre, TN).astype(BF16)
+
+    def over_z(partial):
+        return lax.psum_scatter(partial, "z", scatter_dimension=0, tiled=True)
+
+    unit_terms = [dot(normed2_all, grad_pre, TN).reshape(zs, fc_rows, ff_own)]
+    for part in parts:
+        unit_terms.append(dot(act_low, grad_all[:, part], TN).reshape(zs, ff_unit, ff_own))
+    unit_terms = jnp.concatenate(unit_terms, axis=1).astype(BF16).reshape(-1, ff_own)
+    unit_terms, both_all = together(unit_terms, both_all)
+    normed1_all, attended_all = both_all[:, :width], both_all[:, width:]
+    with jax.named_scope("grad_normed2_scatter"):
+        grad_normed2 = scatter_plane(
+            lambda first, count: dot(grad_pre[first : first + count], fc_own, NT),
+            rows,
+            unit_terms,
+        )
+    units = over_z(unit_terms)
     dgain2 = jnp.sum(grad_normed2 * unit2, axis=0)
     dshift2 = jnp.sum(grad_normed2, axis=0)
     dproj_bias = jnp.sum(grad_f32, axis=0)
@@ -347,6 +598,17 @@
     dq, dkv_ctx = attention_backward(
         queries, grad_attended, attended, norms, kv_ctx, seg_own, seg_ctx, padding_id
     )
+    act_late, dq = together(act_low, dq)
+    with jax.named_scope("mlp_out_scatter"):
+        mlp_out = scatter_plane(
+            lambda first, count: jnp.concatenate(
+                [dot(act_late[first : first + count], own, NN) for own in proj_parts], axis=1
+            ),
+            rows,
+        )
+    result = (middle + mlp_out + proj_shift).astype(BF16)
+    with jax.named_scope("result_to_stored"):
+        hidden_out = to_stored(result).astype(BF16)
     dkv = dkv_ctx[halo * rows :]
     for back in range(1, halo + 1):
         pairs = [(i + back, i) for i in range(seqs - back)]
@@ -357,41 +619,101 @@
     dgain1 = jnp.sum(grad_normed1 * unit1, axis=0)
     dshift1 = jnp.sum(grad_normed1, axis=0)
     grad_in = grad_middle + norm_back(grad_normed1, unit1, rstd1, gain1)
-    input_grad = to_stored(grad_in.astype(BF16))
+    with jax.named_scope("input_grad_to_stored"):
+        input_grad = to_stored(grad_in.astype(BF16))
     grad_qkv_f32 = grad_qkv.astype(F32)
     dqv_bias = jnp.concatenate(
         [jnp.sum(grad_qkv_f32[:, :width], axis=0), jnp.sum(grad_qkv_f32[:, width + HD :], axis=0)]
     )
 
     def columns_of_plane(values):
-        cols = values.shape[1] // plane
-        sent = values.reshape(rows, plane, cols).transpose(1, 0, 2)
+        parts = [values[:, :width].reshape(rows, plane, width // plane)]
+        if values.shape[1] > width:
+            parts.append(values[:, width:].reshape(rows, plane, -1))
+        sent = jnp.concatenate(parts, axis=2).transpose(1, 0, 2)
+        cols = sent.shape[2]
         return lax.all_to_all(sent, PLANE, split_axis=0, concat_axis=0, tiled=True).reshape(
             plane * rows, cols
         )
 
-    normed1_all = gather_plane(normed1)
-    attended_all = gather_plane(attended_low)
     dout_own = dot(attended_all, columns_of_plane(grad_branch), TN).astype(BF16)
     dqkv_own = dot(normed1_all, columns_of_plane(grad_qkv), TN).astype(BF16)
 
-    def over_z(partial):
-        return lax.psum_scatter(partial, "z", scatter_dimension=0, tiled=True)
-
-    def by_rows(partial):
+    first_row_y = y_at * shard
+    flipped = (1 - y_at) * shard
+
+    def rows_of_y(partial):
         cols = partial.shape[1]
-        mine = lax.all_to_all(
-            partial.reshape(ys, -1, cols), "y", split_axis=0, concat_axis=0, tiled=True
+        if ys == 2:
+            kept = lax.dynamic_slice_in_dim(partial, first_row_y, shard, 0)
+            return [kept, swap(lax.dynamic_slice_in_dim(partial, flipped, shard, 0), "y")]
+        moved = lax.all_to_all(
+            partial.reshape(ys, shard, cols), "y", split_axis=0, concat_axis=0, tiled=True
         )
-        return lax.all_gather(mine, REP, axis=0, tiled=False).reshape(reps, ys, -1, cols)
-
-    dproj_weight = lax.all_gather(over_z(dproj_own), REP, axis=0, tiled=True).astype(F32)
-    dfc_rows = by_rows(over_z(dfc_own)).reshape(reps, ys, width // seqs, zs, ff_unit)
-    dfc_weight = dfc_rows.transpose(2, 3, 1, 0, 4).reshape(width // seqs, ff).astype(F32)
-    dout_rows = by_rows(over_z(dout_own))
-    dout_weight = dout_rows.transpose(2, 1, 0, 3).reshape(width // seqs, width).astype(F32)
-    dqkv_rows = by_rows(over_z(dqkv_own))
-    dqkv_weight = dqkv_rows.transpose(2, 1, 0, 3).reshape(width // seqs, qkv_cols).astype(F32)
+        return [moved[y] for y in range(ys)]
+
+    def near_rep(pieces):
+        return pieces + [swap(item, "x") for item in pieces]
+
+    def far_rep(pieces):
+        return pieces + [swap(item, "c") for item in pieces]
+
+    def sources(count):
+        found = []
+        for dc, dx, dy in itertools.product(range(2), range(2), range(count)):
+            y = (y_at ^ dy) if ys == 2 else dy
+            found.append((y * reps if count > 1 else 0) + (x_at ^ dx) * cs + (c_at ^ dc))
+        return jnp.stack(found).astype(jnp.int32)
+
+    proj_near = near_rep([units[fc_rows:]])
+    fc_near = near_rep(rows_of_y(units[:fc_rows]))
+    head_terms, input_grad, hidden_out, proj_near, fc_near = together(
+        jnp.concatenate([dqkv_own, dout_own], axis=1), input_grad, hidden_out, proj_near, fc_near
+    )
+    with jax.named_scope("proj_grad_rows"):
+        proj_pieces = far_rep(proj_near)
+        dproj_weight = assemble(
+            proj_pieces,
+            [(p * ff_unit, ff_unit, 0, ff_own, 0, p * ff_own) for p in range(len(parts))],
+            [(ff // seqs, width)],
+            sources(1) * ff_unit,
+        )[0]
+    with jax.named_scope("fc_grad_rows"):
+        fc_pieces = far_rep(fc_near)
+        if small_plane():
+            dfc_weight = assemble(
+                fc_pieces,
+                [(0, shard, z * ff_unit, ff_unit, 0, z * plane * ff_unit) for z in range(zs)],
+                [(shard, ff)],
+                sources(ys) * ff_unit,
+                by_column=True,
+            )[0]
+        else:
+            stacked = jnp.stack(fc_pieces).reshape(plane, shard, zs, ff_unit)
+            order = jnp.argsort(sources(ys))
+            dfc_weight = (
+                stacked[order].transpose(1, 2, 0, 3).reshape(shard, ff).astype(F32)
+            )
+    with jax.named_scope("attention_grad_rows"):
+        heads = over_z(head_terms)
+        head_pieces = far_rep(near_rep(rows_of_y(heads)))
+        q_cols, kv_cols = width // plane, 2 * HD // plane
+        if small_plane():
+            dqkv_weight, dout_weight = assemble(
+                head_pieces,
+                [(0, shard, 0, q_cols, 0, 0), (0, shard, q_cols + kv_cols, q_cols, 1, 0)],
+                [(shard, qkv_cols), (shard, width)],
+                sources(ys) * q_cols,
+                by_column=True,
+                rolled=(q_cols, kv_cols, 0, width),
+            )
+        else:
+            stacked = jnp.stack(head_pieces)[jnp.argsort(sources(ys))].transpose(1, 0, 2)
+            stacked = stacked.astype(F32)
+            dq_cols = stacked[:, :, :q_cols].reshape(shard, width)
+            dkv_cols = stacked[:, :, q_cols : q_cols + kv_cols].reshape(shard, 2 * HD)
+            dqkv_weight = jnp.concatenate([dq_cols, dkv_cols], axis=1)
+            dout_weight = stacked[:, :, q_cols + kv_cols :].reshape(shard, width)
 
     dfc_bias = lax.dynamic_update_slice(
         jnp.zeros((zs, ys, reps, ff_unit), F32),
@@ -402,7 +724,14 @@
     lasts = (dgain1, dshift1, dqv_bias)
 
     def reduce_small(items):
-        total = lax.psum(jnp.concatenate(items), ALL)
+        total = jnp.concatenate(items).reshape(-1, HD)
+        if small_plane():
+            for axis in ("c", "x", "y"):
+                total = total + swap(total, axis)
+            total = sum([shift(total, "z", away) for away in range(1, zs)], total)
+        else:
+            total = lax.psum(total, ALL)
+        total = total.reshape(-1)
         outs, at = [], 0
         for item in items:
             size = item.shape[0] // seqs

time: 1350 us -> 917 us (0.68)
  waiting for transfers between devices: 728 us -> 410 us
  blocking collectives: 288 us -> 0 us
  starting transfers between devices: 36.5 us -> 126 us
  Pallas kernels: 21.5 us -> 56.8 us
  local copies, waits for them, and re-layouts: 73.8 us -> 98.7 us
  other arithmetic: 22.1 us -> 43.5 us
    ppermute x0 -> x96, waiting for transfers between devices: none -> 296 us  [the longest x90 273 us: swap(): return lax.ppermute(block, axis, [(0, 1), (1, 0)])]
    all_gather x12 -> x3, waiting for transfers between devices: 290 us -> 55 us  [the longest x1 54.9 us: shards(): lax.all_gather(jnp.concatenate([quarter(qkv_weight), quarter(out_weight)]...]
    reduce_scatter x4 -> x2, waiting for transfers between devices: 178 us -> 18.3 us  [over_z(): return lax.psum_scatter(partial, 'z', scatter_dimension=0, tiled=True)]
    all_to_all x3 -> x0, blocking collectives: 143 us -> none  [the longest x1 105 us: exchange(): moved = lax.all_to_all(packed, SEQ, split_axis=0, concat_axis=0, tiled=True)]
    reduce_scatter x2 -> x0, waiting for transfers between devices: 109 us -> none  [scatter_plane(): return lax.psum_scatter(partial, PLANE, scatter_dimension=0, tiled=True)]
    unnamed x1 -> x0, blocking collectives: 104 us -> none
    psum x1 -> x0, waiting for transfers between devices: 100 us -> none  [reduce_small(): total = lax.psum(jnp.concatenate(items), ALL)]
    ppermute x0 -> x96, starting transfers between devices: none -> 76 us  [the longest x90 70.5 us: swap(): return lax.ppermute(block, axis, [(0, 1), (1, 0)])]
  transfers between devices with their start and end apart: 30 -> 111, of which waited for: 21 -> 45; matrix products, arithmetic and copies ran while one was open for 15% -> 28% of each run, Pallas kernels for 2% -> 6%
where the time goes in v2:
time: 917 us; the launch traced here: 906 us
  waiting for transfers between devices  410 us (45%)
  matrix products  155 us (17%)
  starting transfers between devices  126 us (14%)
  local copies, waits for them, and re-layouts  98.7 us (11%)
  Pallas kernels  56.8 us (6%)
  other arithmetic  43.5 us (5%)
  between operations  15.7 us (2%)
    ppermute x90, waiting for transfers between devices, swap(): return lax.ppermute(block, axis, [(0, 1), (1, 0)])  273 us
    dot_general x26, matrix products, dot(): lax.dot_general(left, right, (dims, ((), ())), preferred_element_type=F32)  155 us
    ppermute x90, starting transfers between devices, swap(): return lax.ppermute(block, axis, [(0, 1), (1, 0)])  70.5 us
    all_gather x1, waiting for transfers between devices, shards(): lax.all_gather(jnp.concatenate([quarter(qkv_weight), quarter(out_weight)]...  54.9 us
    unnamed x209, local copies, waits for them, and re-layouts  53.6 us
    ppermute x2, waiting for transfers between devices, shards(): dkv = dkv + lax.ppermute(term, SEQ, pairs).astype(F32)  23.5 us
    ppermute x6, waiting for transfers between devices, shift(): lax.ppermute(block, axis, [(i, (i + by) % count) for i in range(count)])  23.5 us
    pallas_call x3, Pallas kernels, assemble(): pl.pallas_call(functools.partial(assemble_kernel, count, slices, by_colum...  18.9 us
  transfers between devices with their start and end apart: 111, of which 45 were waited for; matrix products, arithmetic and copies ran while one was open for 28% of the time, Pallas kernels for 6%

profile of v2, /device:TPU:0, one launch (start us, length us, event | category | flops | bytes accessed | tf_op | source)
XLA Modules:
  0.0 905.9 jit_solution(17779785177702530015)
XLA Ops:
  38.5 21.6 %collective-permute-done = bf16[256,1024]{1,0:T(8,128)(2,1)S(1)} collective-permute-done((bf16[256,1024]{1,0:T(8,128)(2,1)S(1)}, bf16[256,1024]{1,0:T(8,128)(2,1)S(1)}, u32[]{:S(2)}, u32[]{:S(2)}) %collective-permute-start) | collective-permute-done | bytes 524320 | tf_op jit(solution)/shard_map/ppermute | solution.py:184
  63.8 54.9 %all-gather.5.cloned.1.call-done = bf16[256,4352]{1,0:T(8,128)(2,1)} async-done(((bf16[64,4352]{1,0:T(8,128)(2,1)}), bf16[256,4352]{1,0:T(8,128)(2,1)}) %all-gather.5.cloned.1.call-update) | async-done | bytes 2228240 | tf_op jit(solution)/shard_map/attention_weights/all_gather | solution.py:489
  138.7 12.0 %collective-permute-done.2.refs_4_ = bf16[128,2304]{1,0:T(8,128)(2,1)} collective-permute-done((bf16[128,2304]{1,0:T(8,128)(2,1)}, bf16[128,2304]{1,0:T(8,128)(2,1)}, u32[]{:S(2)}, u32[]{:S(2)}) %collective-permute-start.2) | collective-permute-done | bytes 589856 | tf_op jit(solution)/shard_map/ppermute | solution.py:184
  150.7 13.6 %collective-permute-done.3.refs_10_ = bf16[128,2304]{1,0:T(8,128)(2,1)} collective-permute-done((bf16[128,2304]{1,0:T(8,128)(2,1)}, bf16[128,2304]{1,0:T(8,128)(2,1)}, u32[]{:S(2)}, u32[]{:S(2)}) %collective-permute-start.3) | collective-permute-done | bytes 589856 | tf_op jit(solution)/shard_map/ppermute | solution.py:184
  170.4 16.1 %collective-permute-done.8.refs_6_ = bf16[128,2304]{1,0:T(8,128)(2,1)} collective-permute-done((bf16[128,2304]{1,0:T(8,128)(2,1)}, bf16[128,2304]{1,0:T(8,128)(2,1)}, u32[]{:S(2)}, u32[]{:S(2)}) %collective-permute-start.8) | collective-permute-done | bytes 589856 | tf_op jit(solution)/shard_map/qkv_gather/ppermute | solution.py:184
  204.4 9.8 %collective-permute-done.25.refs_10_ = bf16[128,2048]{1,0:T(8,128)(2,1)} collective-permute-done((bf16[128,2048]{1,0:T(8,128)(2,1)S(1)}, bf16[128,2048]{1,0:T(8,128)(2,1)}, u32[]{:S(2)}, u32[]{:S(2)}) %collective-permute-start.25) | collective-permute-done | bytes 524320 | tf_op jit(solution)/shard_map/out_gather/ppermute | solution.py:184
  234.3 9.0 attention_forward.1
  275.3 9.3 %collective-permute-done.32 = bf16[128,2048]{1,0:T(8,128)(2,1)} collective-permute-done((bf16[128,2048]{1,0:T(8,128)(2,1)}, bf16[128,2048]{1,0:T(8,128)(2,1)}, u32[]{:S(2)}, u32[]{:S(2)}) %collective-permute-start.32) | collective-permute-done | bytes 524320 | tf_op jit(solution)/shard_map/normed2_gather/ppermute | solution.py:184
  299.6 10.9 %collective-permute-done.33 = bf16[128,2048]{1,0:T(8,128)(2,1)} collective-permute-done((bf16[128,2048]{1,0:T(8,128)(2,1)}, bf16[128,2048]{1,0:T(8,128)(2,1)}, u32[]{:S(2)}, u32[]{:S(2)}) %collective-permute-start.33) | collective-permute-done | bytes 524320 | tf_op jit(solution)/shard_map/normed2_gather/ppermute | solution.py:184
  340.3 9.8 %collective-permute-done.46 = bf16[128,2048]{1,0:T(8,128)(2,1)} collective-permute-done((bf16[128,2048]{1,0:T(8,128)(2,1)}, bf16[128,2048]{1,0:T(8,128)(2,1)}, u32[]{:S(2)}, u32[]{:S(2)}) %collective-permute-start.46) | collective-permute-done | bytes 524320 | tf_op jit(solution)/shard_map/grad_gather/ppermute | solution.py:184
  357.2 13.8 %collective-permute-done.49 = bf16[128,2048]{1,0:T(8,128)(2,1)S(1)} collective-permute-done((bf16[128,2048]{1,0:T(8,128)(2,1)}, bf16[128,2048]{1,0:T(8,128)(2,1)S(1)}, u32[]{:S(2)}, u32[]{:S(2)}) %collective-permute-start.49) | collective-permute-done | bytes 524320 | tf_op jit(solution)/shard_map/grad_gather/ppermute | solution.py:184
  371.1 21.2 %collective-permute-done.47 = bf16[128,2048]{1,0:T(8,128)(2,1)S(1)} collective-permute-done((bf16[128,2048]{1,0:T(8,128)(2,1)}, bf16[128,2048]{1,0:T(8,128)(2,1)S(1)}, u32[]{:S(2)}, u32[]{:S(2)}) %collective-permute-start.47) | collective-permute-done | bytes 524320 | tf_op jit(solution)/shard_map/grad_gather/ppermute | solution.py:184
  427.8 15.3 %multiply_convert_fusion = (bf16[2048,1024]{1,0:T(8,128)(2,1)}, f32[2048,1024]{1,0:T(8,128)}) fusion(f32[1024]{0:T(1024)S(1)} %bitcast.205, bf16[2048,2048]{1,0:T(8,128)(2,1)} %constant_dynamic-update-slice_fusion, bf16[2048,1024]{1,0:T(8,128)(2,1)S(1)} %bitcast.161), kind=kOutput, calls=%fused_computation.18 | convolution fusion | flops 8610906112 | bytes 25169920 | tf_op jit(solution)/shard_map/dot_general | solution.py:29
  443.2 13.7 %convert_reduce_fusion = (f32[1024]{0:T(1024)S(1)}, bf16[2048,1024]{1,0:T(8,128)(2,1)}) fusion(f32[2048,1024]{1,0:T(8,128)} %get-tuple-element.163, f32[1024]{0:T(1024)S(1)} %bitcast.206, f32[2048,1024]{1,0:T(8,128)} %fusion.14, bf16[1024,1024]{1,0:T(8,128)(2,1)S(1)} %bitcast.168, bf16[2048,2048]{1,0:T(8,128)(2,1)S(1)} %copy-done.69), kind=kOutput, calls=%fused_computation.12 | convolution fusion | flops 4343200768 | bytes 27271168 | tf_op jit(solution)/shard_map/dot_general | solution.py:29
  478.0 11.2 %convolution_convert_fusion.1 = bf16[2048,1024]{1,0:T(8,128)(2,1)S(1)} fusion(bf16[2048,2048]{1,0:T(8,128)(2,1)S(1)} %bitcast.200, bf16[2048,1024]{1,0:T(8,128)(2,1)} %get-tuple-element.166), kind=kOutput, calls=%fused_computation.21 | convolution fusion | flops 8592031744 | bytes 16777216 | tf_op jit(solution)/shard_map/dot_general | solution.py:29
  507.5 22.9 %collective-permute-done.60 = bf16[256,2048]{1,0:T(8,128)(2,1)S(1)} collective-permute-done((bf16[256,2048]{1,0:T(8,128)(2,1)}, bf16[256,2048]{1,0:T(8,128)(2,1)S(1)}, u32[]{:S(2)}, u32[]{:S(2)}) %collective-permute-start.60) | collective-permute-done | bytes 1048608 | tf_op jit(solution)/shard_map/grad_normed2_scatter/ppermute | solution.py:184
  537.6 9.9 %collective-permute-done.63 = bf16[128,2048]{1,0:T(8,128)(2,1)S(1)} collective-permute-done((bf16[128,2048]{1,0:T(8,128)(2,1)S(1)}, bf16[128,2048]{1,0:T(8,128)(2,1)S(1)}, u32[]{:S(2)}, u32[]{:S(2)}) %collective-permute-start.63) | collective-permute-done | bytes 524320 | tf_op jit(solution)/shard_map/grad_normed2_scatter/ppermute | solution.py:184
  556.2 12.2 %attention_backward.1 = (bf16[256,2048]{1,0:T(8,128)(2,1)S(1)}, f32[768,256]{1,0:T(8,128)S(1)}) custom-call(bf16[256,2048]{1,0:T(8,128)(2,1)S(1)} %copy-done.3, bf16[256,2048]{1,0:T(8,128)(2,1)S(1)} %convolution_convert_fusion.7.g_ref, f32[256,2048]{1,0:T(8,128)} %copy-done.10, f32[256,2048]{1,0:T(8,128)} %copy-done.11, bf16[768,256]{1,0:T(8,128)(2,1)S(1)} %copy-done.5, ...), custom_call_target="tpu_custom_call" | custom-call | flops 4026531840 | bytes 7340032 | tf_op jit(solution)/shard_map/attention_backward/pallas_call | solution.py:132
  595.6 23.5 %collective-permute-done.65 = bf16[256,256]{1,0:T(8,128)(2,1)S(1)} collective-permute-done((bf16[256,256]{1,0:T(8,128)(2,1)S(1)}, bf16[256,256]{1,0:T(8,128)(2,1)S(1)}, u32[]{:S(2)}, u32[]{:S(2)}) %collective-permute-start.65) | collective-permute-done | bytes 131104 | tf_op jit(solution)/shard_map/ppermute | solution.py:616
  630.3 12.4 %all-to-all-start.2 = ((bf16[8,256,288]{1,2,0:T(8,128)(2,1)}), bf16[8,256,288]{1,2,0:T(8,128)(2,1)}, u32[]{:S(2)}, u32[]{:S(2)}) async-start(bf16[8,256,288]{1,2,0:T(8,128)(2,1)} %maximum_bitcast_fusion), calls=%async_computation.2 | async-start | bytes 2359296 | tf_op jit(solution)/shard_map/all_to_all | solution.py:635
  671.2 21.0 %collective-permute-done.67 = bf16[256,2048]{1,0:T(8,128)(2,1)S(1)} collective-permute-done((bf16[256,2048]{1,0:T(8,128)(2,1)S(1)}, bf16[256,2048]{1,0:T(8,128)(2,1)S(1)}, u32[]{:S(2)}, u32[]{:S(2)}) %collective-permute-start.67) | collective-permute-done | bytes 1048608 | tf_op jit(solution)/shard_map/mlp_out_scatter/ppermute | solution.py:184
  692.2 15.1 %collective-permute-done.69 = bf16[256,2048]{1,0:T(8,128)(2,1)S(1)} collective-permute-done((bf16[256,2048]{1,0:T(8,128)(2,1)S(1)}, bf16[256,2048]{1,0:T(8,128)(2,1)S(1)}, u32[]{:S(2)}, u32[]{:S(2)}) %collective-permute-start.69) | collective-permute-done | bytes 1048608 | tf_op jit(solution)/shard_map/mlp_out_scatter/ppermute | solution.py:184
  827.6 9.3 %collective-permute-done.92 = f32[128,128]{1,0:T(8,128)S(1)} collective-permute-done((f32[128,128]{1,0:T(8,128)S(1)}, f32[128,128]{1,0:T(8,128)S(1)}, u32[]{:S(2)}, u32[]{:S(2)}) %collective-permute-start.92) | collective-permute-done | bytes 65568 | tf_op jit(solution)/shard_map/ppermute | solution.py:243
  837.1 18.3 %reduce-scatter.5.cloned.1.call-done = bf16[512,544]{1,0:T(8,128)(2,1)} async-done(((bf16[2048,544]{1,0:T(8,128)(2,1)}), bf16[512,544]{1,0:T(8,128)(2,1)}) %reduce-scatter.5.cloned.1.call-update) | async-done | bytes 557072 | tf_op jit(solution)/shard_map/attention_grad_rows/reduce_scatter | solution.py:575
  (566 shorter events, 503.5 us)
Async XLA Ops:
  22.0 96.9 %all-to-all-start = ((bf16[8,72,2048]{2,1,0:T(8,128)(2,1)}), bf16[8,72,2048]{2,1,0:T(8,128)(2,1)S(1)}, u32[]{:S(2)}, u32[]{:S(2)}) async-start(bf16[8,72,2048]{2,1,0:T(8,128)(2,1)} %bitcast.166), calls=%async_computation | async-start | bytes 4718592 | tf_op jit(solution)/shard_map/hidden_to_places/all_to_all | solution.py:446
  29.3 89.5 %all-gather.5.cloned.1.call-start = ((), (), s32[]{:S(2)}) async-start(), calls=%async_computation.8 | async-start | bytes 2785280 | tf_op jit(solution)/shard_map/attention_weights/all_gather | solution.py:489
  125.1 39.2 %collective-permute-start.3 = (bf16[128,2304]{1,0:T(8,128)(2,1)}, bf16[128,2304]{1,0:T(8,128)(2,1)}, u32[]{:S(2)}, u32[]{:S(2)}) collective-permute-start(bf16[128,2304]{1,0:T(8,128)(2,1)} %get-tuple-element.55.refs_8_), channel_id=1, source_target_pairs={{0,4},{4,0},{1,5},{5,1},{2,6},{6,2},{3,7},{7,3},{8,12},{12,8},{9,1... | collective-permute-start | bytes 1769480 | tf_op jit(solution)/shard_map/ppermute | solution.py:184
  125.7 38.7 %collective-permute-start.4 = (bf16[128,2304]{1,0:T(8,128)(2,1)}, bf16[128,2304]{1,0:T(8,128)(2,1)}, u32[]{:S(2)}, u32[]{:S(2)}) collective-permute-start(bf16[128,2304]{1,0:T(8,128)(2,1)} %get-tuple-element.55.refs_8_), channel_id=1, source_target_pairs={{0,2},{2,0},{1,3},{3,1},{4,6},{6,4},{5,7},{7,5},{8,10},{10,8},{9,1... | collective-permute-start | bytes 1769480 | tf_op jit(solution)/shard_map/ppermute | solution.py:184
  129.2 127.9 %all-to-all-start.1 = ((bf16[8,64,2048]{2,1,0:T(8,128)(2,1)}), bf16[8,64,2048]{2,1,0:T(8,128)(2,1)}, u32[]{:S(2)}, u32[]{:S(2)}) async-start(bf16[8,64,2048]{2,1,0:T(8,128)(2,1)} %bitcast.158), calls=%async_computation.1 | async-start | bytes 4194304 | tf_op jit(solution)/shard_map/grad_to_places/all_to_all | solution.py:456
  133.6 277.4 %all-gather.9.cloned.1.call-start = ((), (), s32[]{:S(2)}) async-start(), calls=%async_computation.12 | async-start | bytes 10485760 | tf_op jit(solution)/shard_map/units_gather/all_gather | solution.py:503
  134.4 367.1 %all-gather.7.cloned.1.call-start = ((), (), s32[]{:S(2)}) async-start(), calls=%async_computation.9 | async-start | bytes 18874368 | tf_op jit(solution)/shard_map/both_gather/all_gather | solution.py:560
  332.8 412.9 %reduce-scatter.3.cloned.1.call-start = ((), (), s32[]{:S(2)}) async-start(), calls=%async_computation.10 | async-start | bytes 10485760 | tf_op jit(solution)/shard_map/reduce_scatter | solution.py:575
  350.0 42.2 %collective-permute-start.47 = (bf16[128,2048]{1,0:T(8,128)(2,1)}, bf16[128,2048]{1,0:T(8,128)(2,1)S(1)}, u32[]{:S(2)}, u32[]{:S(2)}) collective-permute-start(bf16[128,2048]{1,0:T(8,128)(2,1)} %collective-permute-done.46), channel_id=1, source_target_pairs={{0,4},{4,0},{1,5},{5,1},{2,6},{6,2},{3,7},{7,3},{8,12},{12,8},{9,1... | collective-permute-start | bytes 1572872 | tf_op jit(solution)/shard_map/grad_gather/ppermute | solution.py:184
  351.4 42.5 %collective-permute-start.48 = (bf16[128,2048]{1,0:T(8,128)(2,1)}, bf16[128,2048]{1,0:T(8,128)(2,1)S(1)}, u32[]{:S(2)}, u32[]{:S(2)}) collective-permute-start(bf16[128,2048]{1,0:T(8,128)(2,1)} %get-tuple-element.132), channel_id=1, source_target_pairs={{0,2},{2,0},{1,3},{3,1},{4,6},{6,4},{5,7},{7,5},{8,10},{10,8},{9,1... | collective-permute-start | bytes 1572872 | tf_op jit(solution)/shard_map/grad_gather/ppermute | solution.py:184
  352.9 50.3 %collective-permute-start.51 = (bf16[128,2048]{1,0:T(8,128)(2,1)}, bf16[128,2048]{1,0:T(8,128)(2,1)S(1)}, u32[]{:S(2)}, u32[]{:S(2)}) collective-permute-start(bf16[128,2048]{1,0:T(8,128)(2,1)} %get-tuple-element.134), channel_id=1, source_target_pairs={{0,1},{1,0},{2,3},{3,2},{4,5},{5,4},{6,7},{7,6},{8,9},{9,8},{10,11... | collective-permute-start | bytes 1572872 | tf_op jit(solution)/shard_map/grad_gather/ppermute | solution.py:184
  352.9 54.8 %collective-permute-start.55 = (bf16[128,2048]{1,0:T(8,128)(2,1)}, bf16[128,2048]{1,0:T(8,128)(2,1)S(1)}, u32[]{:S(2)}, u32[]{:S(2)}) collective-permute-start(bf16[128,2048]{1,0:T(8,128)(2,1)} %get-tuple-element.132), channel_id=1, source_target_pairs={{0,1},{1,0},{2,3},{3,2},{4,5},{5,4},{6,7},{7,6},{8,9},{9,8},{10,11... | collective-permute-start | bytes 1572872 | tf_op jit(solution)/shard_map/grad_gather/ppermute | solution.py:184
  577.3 70.4 %collective-permute-start.66 = (bf16[1024,2048]{1,0:T(8,128)(2,1)}, bf16[1024,2048]{1,0:T(8,128)(2,1)}, u32[]{:S(2)}, u32[]{:S(2)}) collective-permute-start(bf16[1024,2048]{1,0:T(8,128)(2,1)} %pad_maximum_fusion.1), channel_id=1, source_target_pairs={{0,1},{1,0},{2,3},{3,2},{4,5},{5,4},{6,7},{7,6},{8,9},{9,8},{10,11... | collective-permute-start | bytes 12582920 | tf_op jit(solution)/shard_map/mlp_out_scatter/ppermute | solution.py:184
  577.3 41.8 %collective-permute-start.65 = (bf16[256,256]{1,0:T(8,128)(2,1)S(1)}, bf16[256,256]{1,0:T(8,128)(2,1)S(1)}, u32[]{:S(2)}, u32[]{:S(2)}) collective-permute-start(bf16[256,256]{1,0:T(8,128)(2,1)S(1)} %get-tuple-element.142), channel_id=1, source_target_pairs={{8,0},{12,4},{16,8},{20,12},{24,16},{28,20},{9,1},{13,5},{17,9},{2... | collective-permute-start | bytes 393224 | tf_op jit(solution)/shard_map/ppermute | solution.py:616
  578.6 40.5 %collective-permute-start.64 = (bf16[256,256]{1,0:T(8,128)(2,1)S(1)}, bf16[256,256]{1,0:T(8,128)(2,1)S(1)}, u32[]{:S(2)}, u32[]{:S(2)}) collective-permute-start(bf16[256,256]{1,0:T(8,128)(2,1)S(1)} %get-tuple-element.141), channel_id=1, source_target_pairs={{4,0},{8,4},{12,8},{16,12},{20,16},{24,20},{28,24},{5,1},{9,5},{13... | collective-permute-start | bytes 393224 | tf_op jit(solution)/shard_map/ppermute | solution.py:616
  590.1 40.3 %all-to-all-start.3 = ((bf16[8,256,256]{2,1,0:T(8,128)(2,1)}), bf16[8,256,256]{2,1,0:T(8,128)(2,1)}, u32[]{:S(2)}, u32[]{:S(2)}) async-start(bf16[8,256,256]{2,1,0:T(8,128)(2,1)} %bitcast.150), calls=%async_computation.3 | async-start | bytes 2097152 | tf_op jit(solution)/shard_map/all_to_all | solution.py:635
  659.6 70.5 %all-to-all-start.4 = ((bf16[8,64,2048]{2,1,0:T(8,128)(2,1)}), bf16[8,64,2048]{2,1,0:T(8,128)(2,1)S(1)}, u32[]{:S(2)}, u32[]{:S(2)}) async-start(bf16[8,64,2048]{2,1,0:T(8,128)(2,1)} %bitcast.55), calls=%async_computation.4 | async-start | bytes 4194304 | tf_op jit(solution)/shard_map/input_grad_to_stored/all_to_all | solution.py:456
  669.2 38.1 %collective-permute-start.69 = (bf16[256,2048]{1,0:T(8,128)(2,1)S(1)}, bf16[256,2048]{1,0:T(8,128)(2,1)S(1)}, u32[]{:S(2)}, u32[]{:S(2)}) collective-permute-start(bf16[256,2048]{1,0:T(8,128)(2,1)S(1)} %get-tuple-element.103), channel_id=1, source_target_pairs={{0,4},{4,0},{1,5},{5,1},{2,6},{6,2},{3,7},{7,3},{8,12},{12,8},{9,1... | collective-permute-start | bytes 3145736 | tf_op jit(solution)/shard_map/mlp_out_scatter/ppermute | solution.py:184
  730.1 54.4 %all-to-all-start.5 = ((bf16[8,64,2048]{2,1,0:T(8,128)(2,1)}), bf16[8,64,2048]{2,1,0:T(8,128)(2,1)}, u32[]{:S(2)}, u32[]{:S(2)}) async-start(bf16[8,64,2048]{2,1,0:T(8,128)(2,1)} %bitcast.159), calls=%async_computation.5 | async-start | bytes 4194304 | tf_op jit(solution)/shard_map/result_to_stored/all_to_all | solution.py:456
  736.0 119.4 %reduce-scatter.5.cloned.1.call-start = ((), (), s32[]{:S(2)}) async-start(), calls=%async_computation.11 | async-start | bytes 3276800 | tf_op jit(solution)/shard_map/attention_grad_rows/reduce_scatter | solution.py:575
  748.6 39.3 %collective-permute-start.71 = (bf16[512,1024]{1,0:T(8,128)(2,1)}, bf16[512,1024]{1,0:T(8,128)(2,1)}, u32[]{:S(2)}, u32[]{:S(2)}) collective-permute-start(bf16[512,1024]{1,0:T(8,128)(2,1)} %get-tuple-element.84.refs_0_), channel_id=1, source_target_pairs={{0,2},{2,0},{1,3},{3,1},{4,6},{6,4},{5,7},{7,5},{8,10},{10,8},{9,1... | collective-permute-start | bytes 3145736 | tf_op jit(solution)/shard_map/ppermute | solution.py:184
  799.7 57.0 %collective-permute-start.94 = (bf16[256,1024]{1,0:T(8,128)(2,1)S(1)}, bf16[256,1024]{1,0:T(8,128)(2,1)S(1)}, u32[]{:S(2)}, u32[]{:S(2)}) collective-permute-start(bf16[256,1024]{1,0:T(8,128)(2,1)S(1)} %copy-done.26), channel_id=1, source_target_pairs={{0,1},{1,0},{2,3},{3,2},{4,5},{5,4},{6,7},{7,6},{8,9},{9,8},{10,11... | collective-permute-start | bytes 1572872 | tf_op jit(solution)/shard_map/fc_grad_rows/ppermute | solution.py:184
  799.7 57.4 %collective-permute-start.95 = (bf16[256,1024]{1,0:T(8,128)(2,1)}, bf16[256,1024]{1,0:T(8,128)(2,1)S(1)}, u32[]{:S(2)}, u32[]{:S(2)}) collective-permute-start(bf16[256,1024]{1,0:T(8,128)(2,1)} %collective-permute-done.72.refs_1_), channel_id=1, source_target_pairs={{0,1},{1,0},{2,3},{3,2},{4,5},{5,4},{6,7},{7,6},{8,9},{9,8},{10,11... | collective-permute-start | bytes 1572872 | tf_op jit(solution)/shard_map/fc_grad_rows/ppermute | solution.py:184
  803.5 66.9 %collective-permute-start.98 = (bf16[512,1024]{1,0:T(8,128)(2,1)}, bf16[512,1024]{1,0:T(8,128)(2,1)S(1)}, u32[]{:S(2)}, u32[]{:S(2)}) collective-permute-start(bf16[512,1024]{1,0:T(8,128)(2,1)} %get-tuple-element.84.refs_0_), channel_id=1, source_target_pairs={{0,1},{1,0},{2,3},{3,2},{4,5},{5,4},{6,7},{7,6},{8,9},{9,8},{10,11... | collective-permute-start | bytes 3145736 | tf_op jit(solution)/shard_map/proj_grad_rows/ppermute | solution.py:184
  (171 other events, 3134.6 us)
Sparse Core Ops, SparseCore 0:
  32.3 86.4 all-gather.4
  136.0 180.3 all-gather.8
  333.0 123.3 all-gather.6
  507.6 192.4 reduce-scatter.2
  796.0 59.3 reduce-scatter.4

commit v3 on v2

--- a/solution.py
+++ b/solution.py
@@ -208,8 +208,33 @@
     return near + [swap(item, "c") for item in near]
 
 
+def join_kernel(count, *refs):
+    rows = refs[0].shape[0]
+    for i in range(count):
+        refs[count][i * rows : (i + 1) * rows, :] = refs[i][...]
+
+
+def join_rows(pieces):
+    count = len(pieces)
+    if count == 1:
+        return pieces[0]
+    rows, width = pieces[0].shape
+    return pl.pallas_call(
+        functools.partial(join_kernel, count),
+        grid=(1,),
+        in_specs=[pl.BlockSpec((rows, width), lambda i: (0, 0))] * count,
+        out_specs=pl.BlockSpec((count * rows, width), lambda i: (0, 0)),
+        out_shape=jax.ShapeDtypeStruct((count * rows, width), pieces[0].dtype),
+        compiler_params=pltpu.CompilerParams(vmem_limit_bytes=56 * 1024 * 1024),
+        cost_estimate=pl.CostEstimate(
+            flops=0, bytes_accessed=4 * count * rows * width, transcendentals=0
+        ),
+        name="join_rows",
+    )(*pieces)
+
+
 def gather_plane(block):
-    return jnp.concatenate(plane_pieces(block), axis=0)
+    return join_rows(plane_pieces(block))
 
 
 def scatter_plane(partial, rows, hold=None):
@@ -217,7 +242,7 @@
     if not small_plane():
         return lax.psum_scatter(
             partial(0, total).astype(BF16), PLANE, scatter_dimension=0, tiled=True
-        ).astype(F32)
+        ).astype(F32), hold
     side = total // 2
     got = swap(partial(side, side).astype(BF16), "c")
     both = (partial(0, side) + got.astype(F32)).astype(BF16)
@@ -229,13 +254,14 @@
     low = (low[:rows].astype(F32) + got_low.astype(F32)).astype(BF16)
     half = rows // 2
     got_top, got_low = swap(top[half:], "y"), swap(low[half:], "x")
-    return jnp.concatenate(
+    sums = jnp.concatenate(
         [
             top[:half].astype(F32) + got_top.astype(F32),
             low[:half].astype(F32) + got_low.astype(F32),
         ],
         axis=0,
     )
+    return sums, got_low
 
 
 def shift(block, axis, by):
@@ -486,16 +512,16 @@
     units_part = jnp.concatenate([fc_pair] + [proj_rows[:, part] for part in parts], axis=0)
     with jax.named_scope("attention_weights"):
         if small_plane():
-            columns = lax.all_gather(
+            stored, quarters = together(
+                hidden_in[0],
                 jnp.concatenate([quarter(qkv_weight), quarter(out_weight)], axis=1),
-                "z",
-                axis=0,
-                tiled=True,
             )
+            columns = lax.all_gather(quarters, "z", axis=0, tiled=True)
         else:
+            stored = hidden_in[0]
             columns = lax.all_gather(quarter(qkv_weight), ALL, axis=0, tiled=True)
     with jax.named_scope("hidden_to_places"):
-        moved, *picks = exchange_first(hidden_in[0])
+        moved, *picks = exchange_first(stored)
     units_part, grad_stored, columns, moved = together(
         units_part, out_grad[0], columns, moved
     )
@@ -535,18 +561,19 @@
         pairs = [(i, i + back) for i in range(seqs - back)]
         blocks.append(lax.ppermute(kv_own, SEQ, pairs))
     kv_ctx = jnp.concatenate(blocks + [kv_own], axis=0)
+    with jax.named_scope("grad_to_places"):
+        grad_f32 = to_places(grad_stored)
+    queries, grad_f32 = together(queries, grad_f32)
     seg_own = lax.dynamic_slice_in_dim(segments, first_row, rows)[:, None]
     seg_padded = jnp.concatenate([jnp.full((halo * rows,), -1, jnp.int32), segments])
     seg_ctx = lax.dynamic_slice_in_dim(seg_padded, first_row, ctx)[None, :]
     attended_low, attended, norms = attention_forward(
         queries, kv_ctx, seg_own, seg_ctx, padding_id
     )
-    with jax.named_scope("grad_to_places"):
-        grad_f32 = to_places(grad_stored)
-    attended_low, grad_f32 = together(attended_low, grad_f32)
     grad_low = grad_f32.astype(BF16)
     with jax.named_scope("grad_gather"):
         grad_all = gather_plane(grad_low)
+    attended_low, grad_all = together(attended_low, grad_all)
     middle = inputs + (dot(attended_low, full_out, NN) + out_shift)
 
     unit2, rstd2 = norm_parts(middle)
@@ -578,15 +605,23 @@
     for part in parts:
         unit_terms.append(dot(act_low, grad_all[:, part], TN).reshape(zs, ff_unit, ff_own))
     unit_terms = jnp.concatenate(unit_terms, axis=1).astype(BF16).reshape(-1, ff_own)
-    unit_terms, both_all = together(unit_terms, both_all)
+    unit_terms, both_all, act_late = together(unit_terms, both_all, act_low)
     normed1_all, attended_all = both_all[:, :width], both_all[:, width:]
     with jax.named_scope("grad_normed2_scatter"):
-        grad_normed2 = scatter_plane(
+        grad_normed2, scattered = scatter_plane(
             lambda first, count: dot(grad_pre[first : first + count], fc_own, NT),
             rows,
             unit_terms,
         )
     units = over_z(unit_terms)
+    with jax.named_scope("mlp_out_scatter"):
+        mlp_out, _ = scatter_plane(
+            lambda first, count: jnp.concatenate(
+                [dot(act_late[first : first + count], own, NN) for own in proj_parts], axis=1
+            ),
+            rows,
+            scattered,
+        )
     dgain2 = jnp.sum(grad_normed2 * unit2, axis=0)
     dshift2 = jnp.sum(grad_normed2, axis=0)
     dproj_bias = jnp.sum(grad_f32, axis=0)
@@ -598,14 +633,6 @@
     dq, dkv_ctx = attention_backward(
         queries, grad_attended, attended, norms, kv_ctx, seg_own, seg_ctx, padding_id
     )
-    act_late, dq = together(act_low, dq)
-    with jax.named_scope("mlp_out_scatter"):
-        mlp_out = scatter_plane(
-            lambda first, count: jnp.concatenate(
-                [dot(act_late[first : first + count], own, NN) for own in proj_parts], axis=1
-            ),
-            rows,
-        )
     result = (middle + mlp_out + proj_shift).astype(BF16)
     with jax.named_scope("result_to_stored"):
         hidden_out = to_stored(result).astype(BF16)
@@ -694,8 +721,38 @@
             dfc_weight = (
                 stacked[order].transpose(1, 2, 0, 3).reshape(shard, ff).astype(F32)
             )
+    dfc_bias = lax.dynamic_update_slice(
+        jnp.zeros((zs, ys, reps, ff_unit), F32),
+        dfc_bias_own.reshape(zs, 1, 1, ff_unit),
+        (0, y_at, q_at, 0),
+    ).reshape(ff)
+    mids = (dout_bias, dgain2, dshift2, dfc_bias, dproj_bias)
+    lasts = (dgain1, dshift1, dqv_bias)
+
+    def reduce_small(items):
+        total = jnp.concatenate(items).reshape(-1, HD)
+        if small_plane():
+            for axis in ("c", "x", "y"):
+                total = total + swap(total, axis)
+            total = sum([shift(total, "z", away) for away in range(1, zs)], total)
+        else:
+            total = lax.psum(total, ALL)
+        total = total.reshape(-1)
+        outs, at = [], 0
+        for item in items:
+            size = item.shape[0] // seqs
+            outs.append(lax.dynamic_slice_in_dim(total, at + seq_at * size, size))
+            at += item.shape[0]
+        return outs
+
+    mids = reduce_small(mids)
+    lasts = reduce_small(lasts)
     with jax.named_scope("attention_grad_rows"):
-        heads = over_z(head_terms)
+        heads, dfc_weight, dproj_weight, mids, lasts = together(
+            over_z(head_terms), dfc_weight, dproj_weight, mids, lasts
+        )
+        dout_bias, dgain2, dshift2, dfc_bias, dproj_bias = mids
+        dgain1, dshift1, dqv_bias = lasts
         head_pieces = far_rep(near_rep(rows_of_y(heads)))
         q_cols, kv_cols = width // plane, 2 * HD // plane
         if small_plane():
@@ -715,32 +772,6 @@
             dqkv_weight = jnp.concatenate([dq_cols, dkv_cols], axis=1)
             dout_weight = stacked[:, :, q_cols + kv_cols :].reshape(shard, width)
 
-    dfc_bias = lax.dynamic_update_slice(
-        jnp.zeros((zs, ys, reps, ff_unit), F32),
-        dfc_bias_own.reshape(zs, 1, 1, ff_unit),
-        (0, y_at, q_at, 0),
-    ).reshape(ff)
-    mids = (dout_bias, dgain2, dshift2, dfc_bias, dproj_bias)
-    lasts = (dgain1, dshift1, dqv_bias)
-
-    def reduce_small(items):
-        total = jnp.concatenate(items).reshape(-1, HD)
-        if small_plane():
-            for axis in ("c", "x", "y"):
-                total = total + swap(total, axis)
-            total = sum([shift(total, "z", away) for away in range(1, zs)], total)
-        else:
-            total = lax.psum(total, ALL)
-        total = total.reshape(-1)
-        outs, at = [], 0
-        for item in items:
-            size = item.shape[0] // seqs
-            outs.append(lax.dynamic_slice_in_dim(total, at + seq_at * size, size))
-            at += item.shape[0]
-        return outs
-
-    dout_bias, dgain2, dshift2, dfc_bias, dproj_bias = reduce_small(mids)
-    dgain1, dshift1, dqv_bias = reduce_small(lasts)
     return (
         hidden_out[None],
         input_grad[None],

time: 917 us -> 826 us (0.901)
  local copies, waits for them, and re-layouts: 98.7 us -> 47.9 us
  waiting for transfers between devices: 410 us -> 386 us
  starting transfers between devices: 126 us -> 110 us
  Pallas kernels: 56.8 us -> 71.7 us
    unnamed x209 -> x245, local copies, waits for them, and re-layouts: 53.6 us -> 14.5 us
    reduce_scatter x2, waiting for transfers between devices: 18.3 us -> 3 us  [over_z(): return lax.psum_scatter(partial, 'z', scatter_dimension=0, tiled=True)]
    pallas_call x0 -> x2, Pallas kernels: none -> 15.1 us  [join_rows(): pl.pallas_call(functools.partial(join_kernel, count), grid=(1,), in_specs...]
    ppermute x2, waiting for transfers between devices: 23.5 us -> 9.09 us  [shards(): dkv = dkv + lax.ppermute(term, SEQ, pairs).astype(F32)]
    all_gather x1, waiting for transfers between devices: 0.02 us -> 14.2 us  [shards(): both_all = lax.all_gather(both_low, PLANE, axis=0, tiled=True)]
    ppermute x6, waiting for transfers between devices: 23.5 us -> 10.3 us  [shift(): lax.ppermute(block, axis, [(i, (i + by) % count) for i in range(count)])]
    all_to_all x3, waiting for transfers between devices: 8.9 us -> 19.7 us  [exchange(): moved = lax.all_to_all(packed, SEQ, split_axis=0, concat_axis=0, tiled=True)]
  transfers between devices with their start and end apart: 111 -> 111, of which waited for: 45 -> 55; matrix products, arithmetic and copies ran while one was open for 28% -> 26% of each run, Pallas kernels for 6% -> 8%
where the time goes in v3:
time: 826 us; the launch traced here: 820 us
  waiting for transfers between devices  386 us (47%)
  matrix products  151 us (18%)
  starting transfers between devices  110 us (13%)
  Pallas kernels  71.7 us (9%)
  local copies, waits for them, and re-layouts  47.9 us (6%)
  other arithmetic  37.6 us (5%)
  between operations  16.1 us (2%)
    ppermute x90, waiting for transfers between devices, swap(): return lax.ppermute(block, axis, [(0, 1), (1, 0)])  265 us
    dot_general x26, matrix products, dot(): lax.dot_general(left, right, (dims, ((), ())), preferred_element_type=F32)  151 us
    ppermute x90, starting transfers between devices, swap(): return lax.ppermute(block, axis, [(0, 1), (1, 0)])  61.5 us
    all_gather x1, waiting for transfers between devices, shards(): columns = lax.all_gather(quarters, 'z', axis=0, tiled=True)  55.1 us
    all_to_all x3, waiting for transfers between devices, exchange(): moved = lax.all_to_all(packed, SEQ, split_axis=0, concat_axis=0, tiled=True)  19.7 us
    pallas_call x3, Pallas kernels, assemble(): pl.pallas_call(functools.partial(assemble_kernel, count, slices, by_colum...  19 us
  transfers between devices with their start and end apart: 111, of which 55 were waited for; matrix products, arithmetic and copies ran while one was open for 26% of the time, Pallas kernels for 8%

profile of v3, /device:TPU:0, one launch (start us, length us, event | category | flops | bytes accessed | tf_op | source)
XLA Modules:
  0.0 819.7 jit_solution(11056898016536979280)
XLA Ops:
  32.0 22.7 %collective-permute-done = bf16[256,1024]{1,0:T(8,128)(2,1)S(1)} collective-permute-done((bf16[256,1024]{1,0:T(8,128)(2,1)S(1)}, bf16[256,1024]{1,0:T(8,128)(2,1)S(1)}, u32[]{:S(2)}, u32[]{:S(2)}) %collective-permute-start) | collective-permute-done | bytes 524320 | tf_op jit(solution)/shard_map/ppermute | solution.py:184
  58.3 55.1 %all-gather.5.cloned.1.call-done = bf16[256,4352]{1,0:T(8,128)(2,1)} async-done(((bf16[64,4352]{1,0:T(8,128)(2,1)}), bf16[256,4352]{1,0:T(8,128)(2,1)}) %all-gather.5.cloned.1.call-update) | async-done | bytes 2228240 | tf_op jit(solution)/shard_map/attention_weights/all_gather | solution.py:519
  135.2 21.4 %collective-permute-done.3.refs_10_ = bf16[128,2304]{1,0:T(8,128)(2,1)} collective-permute-done((bf16[128,2304]{1,0:T(8,128)(2,1)}, bf16[128,2304]{1,0:T(8,128)(2,1)}, u32[]{:S(2)}, u32[]{:S(2)}) %collective-permute-start.3) | collective-permute-done | bytes 589856 | tf_op jit(solution)/shard_map/ppermute | solution.py:184
  167.5 10.4 %collective-permute-done.8.refs_6_ = bf16[128,2304]{1,0:T(8,128)(2,1)} collective-permute-done((bf16[128,2304]{1,0:T(8,128)(2,1)}, bf16[128,2304]{1,0:T(8,128)(2,1)}, u32[]{:S(2)}, u32[]{:S(2)}) %collective-permute-start.8) | collective-permute-done | bytes 589856 | tf_op jit(solution)/shard_map/qkv_gather/ppermute | solution.py:184
  199.8 9.5 %collective-permute-done.39.refs_10_ = bf16[128,2048]{1,0:T(8,128)(2,1)} collective-permute-done((bf16[128,2048]{1,0:T(8,128)(2,1)S(1)}, bf16[128,2048]{1,0:T(8,128)(2,1)}, u32[]{:S(2)}, u32[]{:S(2)}) %collective-permute-start.39) | collective-permute-done | bytes 524320 | tf_op jit(solution)/shard_map/out_gather/ppermute | solution.py:184
  214.7 9.3 %collective-permute-done.36.refs_6_ = bf16[128,2048]{1,0:T(8,128)(2,1)} collective-permute-done((bf16[128,2048]{1,0:T(8,128)(2,1)}, bf16[128,2048]{1,0:T(8,128)(2,1)}, u32[]{:S(2)}, u32[]{:S(2)}) %collective-permute-start.36) | collective-permute-done | bytes 524320 | tf_op jit(solution)/shard_map/out_gather/ppermute | solution.py:184
  225.4 8.8 %all-to-all-done.1 = bf16[8,64,2048]{2,1,0:T(8,128)(2,1)} async-done(((bf16[8,64,2048]{2,1,0:T(8,128)(2,1)}), bf16[8,64,2048]{2,1,0:T(8,128)(2,1)}, u32[]{:S(2)}, u32[]{:S(2)}) %all-to-all-start.1) | async-done | bytes 2097184 | tf_op jit(solution)/shard_map/grad_to_places/all_to_all | solution.py:482
  258.3 11.1 %collective-permute-done.17.refs_1_ = bf16[128,2048]{1,0:T(8,128)(2,1)S(1)} collective-permute-done((bf16[128,2048]{1,0:T(8,128)(2,1)S(1)}, bf16[128,2048]{1,0:T(8,128)(2,1)S(1)}, u32[]{:S(2)}, u32[]{:S(2)}) %collective-permute-start.17) | collective-permute-done | bytes 524320 | tf_op jit(solution)/shard_map/grad_gather/ppermute | solution.py:184
  292.9 9.0 %attention_forward.1 = (bf16[256,2048]{1,0:T(8,128)(2,1)S(1)}, f32[256,2048]{1,0:T(8,128)S(1)}, f32[256,2048]{1,0:T(8,128)S(1)}) custom-call(bf16[256,2048]{1,0:T(8,128)(2,1)S(1)} %fusion.31.q_ref, bf16[768,256]{1,0:T(8,128)(2,1)S(1)} %pad_maximum_fusion.11.kv_ref, s32[256,1]{1,0:T(8,128)S(1)} %copy.72.own_ref, s32[1,768]{1,0:T(1,128)S(1)} %broadcast_in_dim.25.ctx_ref), custom_call_target="tpu_custom_call" | custom-call | flops 1610612736 | bytes 6291456 | tf_op jit(solution)/shard_map/attention_forward/pallas_call | solution.py:73
  322.6 10.7 %collective-permute-done.46.refs_2_ = bf16[128,2048]{1,0:T(8,128)(2,1)S(1)} collective-permute-done((bf16[128,2048]{1,0:T(8,128)(2,1)S(1)}, bf16[128,2048]{1,0:T(8,128)(2,1)S(1)}, u32[]{:S(2)}, u32[]{:S(2)}) %collective-permute-start.46) | collective-permute-done | bytes 524320 | tf_op jit(solution)/shard_map/normed2_gather/ppermute | solution.py:184
  334.8 11.2 %collective-permute-done.45.refs_1_ = bf16[128,2048]{1,0:T(8,128)(2,1)S(1)} collective-permute-done((bf16[128,2048]{1,0:T(8,128)(2,1)S(1)}, bf16[128,2048]{1,0:T(8,128)(2,1)S(1)}, u32[]{:S(2)}, u32[]{:S(2)}) %collective-permute-start.45) | collective-permute-done | bytes 524320 | tf_op jit(solution)/shard_map/normed2_gather/ppermute | solution.py:184
  347.3 8.8 %collective-permute-done.47.refs_3_ = bf16[128,2048]{1,0:T(8,128)(2,1)} collective-permute-done((bf16[128,2048]{1,0:T(8,128)(2,1)S(1)}, bf16[128,2048]{1,0:T(8,128)(2,1)}, u32[]{:S(2)}, u32[]{:S(2)}) %collective-permute-start.47) | collective-permute-done | bytes 524320 | tf_op jit(solution)/shard_map/normed2_gather/ppermute | solution.py:184
  375.6 12.1 %fusion.17 = f32[2048,1024]{1,0:T(8,128)} fusion(bf16[1024,1024]{1,0:T(8,128)(2,1)S(1)} %bitcast.175, bf16[2048,2048]{1,0:T(8,128)(2,1)} %join_rows.2), kind=kOutput, calls=%fused_computation.27 | convolution fusion | flops 4294967296 | bytes 14680064 | tf_op jit(solution)/shard_map/dot_general | solution.py:29
  387.8 13.2 %multiply_convert_fusion = (bf16[2048,1024]{1,0:T(8,128)(2,1)}, f32[2048,1024]{1,0:T(8,128)}) fusion(f32[1024]{0:T(1024)S(1)} %bitcast.210, bf16[2048,2048]{1,0:T(8,128)(2,1)S(1)} %bitcast.161, bf16[2048,1024]{1,0:T(8,128)(2,1)S(1)} %bitcast.167), kind=kOutput, calls=%fused_computation.18 | convolution fusion | flops 8610906112 | bytes 25169920 | tf_op jit(solution)/shard_map/dot_general | solution.py:29
  401.0 13.5 %convert_reduce_fusion = (f32[1024]{0:T(1024)S(1)}, bf16[2048,1024]{1,0:T(8,128)(2,1)}) fusion(f32[2048,1024]{1,0:T(8,128)} %get-tuple-element.191, f32[1024]{0:T(1024)S(1)} %bitcast.211, f32[2048,1024]{1,0:T(8,128)} %fusion.17, bf16[1024,1024]{1,0:T(8,128)(2,1)S(1)} %bitcast.178, bf16[2048,2048]{1,0:T(8,128)(2,1)S(1)} %bitcast.159), kind=kOutput, calls=%fused_computation.12 | convolution fusion | flops 4343200768 | bytes 27271168 | tf_op jit(solution)/shard_map/dot_general | solution.py:29
  433.3 11.2 %convolution_convert_fusion.1 = bf16[2048,1024]{1,0:T(8,128)(2,1)S(1)} fusion(bf16[2048,2048]{1,0:T(8,128)(2,1)S(1)} %bitcast.163, bf16[2048,1024]{1,0:T(8,128)(2,1)} %get-tuple-element.194), kind=kOutput, calls=%fused_computation.21 | convolution fusion | flops 8592031744 | bytes 16777216 | tf_op jit(solution)/shard_map/dot_general | solution.py:29
  448.6 14.2 %all-gather.7.cloned.1.call-done = bf16[2048,4096]{1,0:T(8,128)(2,1)} async-done(((bf16[256,4096]{1,0:T(8,128)(2,1)}), bf16[2048,4096]{1,0:T(8,128)(2,1)}) %all-gather.7.cloned.1.call-update) | async-done | bytes 16777232 | tf_op jit(solution)/shard_map/both_gather/all_gather | solution.py:587
  480.3 16.7 %collective-permute-done.60 = bf16[256,2048]{1,0:T(8,128)(2,1)S(1)} collective-permute-done((bf16[256,2048]{1,0:T(8,128)(2,1)S(1)}, bf16[256,2048]{1,0:T(8,128)(2,1)S(1)}, u32[]{:S(2)}, u32[]{:S(2)}) %collective-permute-start.60) | collective-permute-done | bytes 1048608 | tf_op jit(solution)/shard_map/grad_normed2_scatter/ppermute | solution.py:184
  523.8 12.1 %attention_backward.1 = (bf16[256,2048]{1,0:T(8,128)(2,1)S(1)}, f32[768,256]{1,0:T(8,128)S(1)}) custom-call(bf16[256,2048]{1,0:T(8,128)(2,1)S(1)} %copy-done.3, bf16[256,2048]{1,0:T(8,128)(2,1)S(1)} %convolution_convert_fusion.7.g_ref, f32[256,2048]{1,0:T(8,128)} %copy-done.10, f32[256,2048]{1,0:T(8,128)} %copy-done.11, bf16[768,256]{1,0:T(8,128)(2,1)S(1)} %copy-done.5, ...), custom_call_target="tpu_custom_call" | custom-call | flops 4026531840 | bytes 7340032 | tf_op jit(solution)/shard_map/attention_backward/pallas_call | solution.py:132
  549.6 9.1 %collective-permute-done.65 = bf16[256,256]{1,0:T(8,128)(2,1)S(1)} collective-permute-done((bf16[256,256]{1,0:T(8,128)(2,1)S(1)}, bf16[256,256]{1,0:T(8,128)(2,1)S(1)}, u32[]{:S(2)}, u32[]{:S(2)}) %collective-permute-start.65) | collective-permute-done | bytes 131104 | tf_op jit(solution)/shard_map/ppermute | solution.py:643
  599.2 21.4 %collective-permute-done.67 = bf16[256,2048]{1,0:T(8,128)(2,1)S(1)} collective-permute-done((bf16[256,2048]{1,0:T(8,128)(2,1)S(1)}, bf16[256,2048]{1,0:T(8,128)(2,1)S(1)}, u32[]{:S(2)}, u32[]{:S(2)}) %collective-permute-start.67) | collective-permute-done | bytes 1048608 | tf_op jit(solution)/shard_map/mlp_out_scatter/ppermute | solution.py:184
  620.6 13.1 %collective-permute-done.69 = bf16[256,2048]{1,0:T(8,128)(2,1)S(1)} collective-permute-done((bf16[256,2048]{1,0:T(8,128)(2,1)S(1)}, bf16[256,2048]{1,0:T(8,128)(2,1)S(1)}, u32[]{:S(2)}, u32[]{:S(2)}) %collective-permute-start.69) | collective-permute-done | bytes 1048608 | tf_op jit(solution)/shard_map/mlp_out_scatter/ppermute | solution.py:184
  640.6 12.4 %collective-permute-done.68 = bf16[128,2048]{1,0:T(8,128)(2,1)S(1)} collective-permute-done((bf16[128,2048]{1,0:T(8,128)(2,1)S(1)}, bf16[128,2048]{1,0:T(8,128)(2,1)S(1)}, u32[]{:S(2)}, u32[]{:S(2)}) %collective-permute-start.68) | collective-permute-done | bytes 524320 | tf_op jit(solution)/shard_map/mlp_out_scatter/ppermute | solution.py:184
  718.6 9.5 %collective-permute-done.74.refs_3_ = bf16[256,1024]{1,0:T(8,128)(2,1)} collective-permute-done((bf16[256,1024]{1,0:T(8,128)(2,1)}, bf16[256,1024]{1,0:T(8,128)(2,1)}, u32[]{:S(2)}, u32[]{:S(2)}) %collective-permute-start.74) | collective-permute-done | bytes 524320 | tf_op jit(solution)/shard_map/ppermute | solution.py:184
  (604 shorter events, 457.0 us)
Async XLA Ops:
  16.6 97.0 %all-to-all-start = ((bf16[8,72,2048]{2,1,0:T(8,128)(2,1)}), bf16[8,72,2048]{2,1,0:T(8,128)(2,1)S(1)}, u32[]{:S(2)}, u32[]{:S(2)}) async-start(bf16[8,72,2048]{2,1,0:T(8,128)(2,1)} %bitcast.173), calls=%async_computation | async-start | bytes 4718592 | tf_op jit(solution)/shard_map/hidden_to_places/all_to_all | solution.py:472
  23.9 89.5 %all-gather.5.cloned.1.call-start = ((), (), s32[]{:S(2)}) async-start(), calls=%async_computation.8 | async-start | bytes 2785280 | tf_op jit(solution)/shard_map/attention_weights/all_gather | solution.py:519
  24.7 344.5 %all-gather.9.cloned.1.call-start = ((), (), s32[]{:S(2)}) async-start(), calls=%async_computation.12 | async-start | bytes 10485760 | tf_op jit(solution)/shard_map/units_gather/all_gather | solution.py:529
  26.9 27.8 %collective-permute-start = (bf16[256,1024]{1,0:T(8,128)(2,1)S(1)}, bf16[256,1024]{1,0:T(8,128)(2,1)S(1)}, u32[]{:S(2)}, u32[]{:S(2)}) collective-permute-start(bf16[256,1024]{1,0:T(8,128)(2,1)S(1)} %pad_maximum_fusion.10), channel_id=1, source_target_pairs={{0,4},{4,0},{1,5},{5,1},{2,6},{6,2},{3,7},{7,3},{8,12},{12,8},{9,1... | collective-permute-start | bytes 1572872 | tf_op jit(solution)/shard_map/ppermute | solution.py:184
  118.8 37.8 %collective-permute-start.3 = (bf16[128,2304]{1,0:T(8,128)(2,1)}, bf16[128,2304]{1,0:T(8,128)(2,1)}, u32[]{:S(2)}, u32[]{:S(2)}) collective-permute-start(bf16[128,2304]{1,0:T(8,128)(2,1)} %get-tuple-element.72.refs_8_), channel_id=1, source_target_pairs={{0,4},{4,0},{1,5},{5,1},{2,6},{6,2},{3,7},{7,3},{8,12},{12,8},{9,1... | collective-permute-start | bytes 1769480 | tf_op jit(solution)/shard_map/ppermute | solution.py:184
  119.4 37.2 %collective-permute-start.4 = (bf16[128,2304]{1,0:T(8,128)(2,1)}, bf16[128,2304]{1,0:T(8,128)(2,1)}, u32[]{:S(2)}, u32[]{:S(2)}) collective-permute-start(bf16[128,2304]{1,0:T(8,128)(2,1)} %get-tuple-element.72.refs_8_), channel_id=1, source_target_pairs={{0,2},{2,0},{1,3},{3,1},{4,6},{6,4},{5,7},{7,5},{8,10},{10,8},{9,1... | collective-permute-start | bytes 1769480 | tf_op jit(solution)/shard_map/ppermute | solution.py:184
  122.3 111.9 %all-to-all-start.1 = ((bf16[8,64,2048]{2,1,0:T(8,128)(2,1)}), bf16[8,64,2048]{2,1,0:T(8,128)(2,1)}, u32[]{:S(2)}, u32[]{:S(2)}) async-start(bf16[8,64,2048]{2,1,0:T(8,128)(2,1)} %bitcast.164), calls=%async_computation.1 | async-start | bytes 4194304 | tf_op jit(solution)/shard_map/grad_to_places/all_to_all | solution.py:482
  126.7 336.1 %all-gather.7.cloned.1.call-start = ((), (), s32[]{:S(2)}) async-start(), calls=%async_computation.9 | async-start | bytes 18874368 | tf_op jit(solution)/shard_map/both_gather/all_gather | solution.py:587
  181.8 30.1 %collective-permute-start.34 = (bf16[128,2048]{1,0:T(8,128)(2,1)S(1)}, bf16[128,2048]{1,0:T(8,128)(2,1)}, u32[]{:S(2)}, u32[]{:S(2)}) collective-permute-start(bf16[128,2048]{1,0:T(8,128)(2,1)S(1)} %get-tuple-element.162.refs_0_), channel_id=1, source_target_pairs={{0,4},{4,0},{1,5},{5,1},{2,6},{6,2},{3,7},{7,3},{8,12},{12,8},{9,1... | collective-permute-start | bytes 1572872 | tf_op jit(solution)/shard_map/out_gather/ppermute | solution.py:184
  181.8 27.5 %collective-permute-start.39 = (bf16[128,2048]{1,0:T(8,128)(2,1)S(1)}, bf16[128,2048]{1,0:T(8,128)(2,1)}, u32[]{:S(2)}, u32[]{:S(2)}) collective-permute-start(bf16[128,2048]{1,0:T(8,128)(2,1)S(1)} %get-tuple-element.161.refs_8_), channel_id=1, source_target_pairs={{0,4},{4,0},{1,5},{5,1},{2,6},{6,2},{3,7},{7,3},{8,12},{12,8},{9,1... | collective-permute-start | bytes 1572872 | tf_op jit(solution)/shard_map/out_gather/ppermute | solution.py:184
  183.8 29.0 %collective-permute-start.41 = (bf16[128,2048]{1,0:T(8,128)(2,1)S(1)}, bf16[128,2048]{1,0:T(8,128)(2,1)}, u32[]{:S(2)}, u32[]{:S(2)}) collective-permute-start(bf16[128,2048]{1,0:T(8,128)(2,1)S(1)} %get-tuple-element.161.refs_8_), channel_id=1, source_target_pairs={{0,2},{2,0},{1,3},{3,1},{4,6},{6,4},{5,7},{7,5},{8,10},{10,8},{9,1... | collective-permute-start | bytes 1572872 | tf_op jit(solution)/shard_map/out_gather/ppermute | solution.py:184
  184.4 28.6 %collective-permute-start.31 = (bf16[128,2048]{1,0:T(8,128)(2,1)S(1)}, bf16[128,2048]{1,0:T(8,128)(2,1)S(1)}, u32[]{:S(2)}, u32[]{:S(2)}) collective-permute-start(bf16[128,2048]{1,0:T(8,128)(2,1)S(1)} %get-tuple-element.162.refs_0_), channel_id=1, source_target_pairs={{0,1},{1,0},{2,3},{3,2},{4,5},{5,4},{6,7},{7,6},{8,9},{9,8},{10,11... | collective-permute-start | bytes 1572872 | tf_op jit(solution)/shard_map/out_gather/ppermute | solution.py:184
  270.9 32.3 %collective-permute-start.25 = (bf16[128,2048]{1,0:T(8,128)(2,1)}, bf16[128,2048]{1,0:T(8,128)(2,1)}, u32[]{:S(2)}, u32[]{:S(2)}) collective-permute-start(bf16[128,2048]{1,0:T(8,128)(2,1)} %collective-permute-done.18.refs_2_), channel_id=1, source_target_pairs={{0,1},{1,0},{2,3},{3,2},{4,5},{5,4},{6,7},{7,6},{8,9},{9,8},{10,11... | collective-permute-start | bytes 1572872 | tf_op jit(solution)/shard_map/grad_gather/ppermute | solution.py:184
  271.4 31.8 %collective-permute-start.29 = (bf16[128,2048]{1,0:T(8,128)(2,1)}, bf16[128,2048]{1,0:T(8,128)(2,1)}, u32[]{:S(2)}, u32[]{:S(2)}) collective-permute-start(bf16[128,2048]{1,0:T(8,128)(2,1)} %collective-permute-done.21.refs_6_), channel_id=1, source_target_pairs={{0,1},{1,0},{2,3},{3,2},{4,5},{5,4},{6,7},{7,6},{8,9},{9,8},{10,11... | collective-permute-start | bytes 1572872 | tf_op jit(solution)/shard_map/grad_gather/ppermute | solution.py:184
  368.2 306.9 %reduce-scatter.3.cloned.1.call-start = ((), (), s32[]{:S(2)}) async-start(), calls=%async_computation.10 | async-start | bytes 10485760 | tf_op jit(solution)/shard_map/reduce_scatter | solution.py:602
  423.1 39.7 %collective-permute-start.59 = (bf16[1024,2048]{1,0:T(8,128)(2,1)}, bf16[1024,2048]{1,0:T(8,128)(2,1)}, u32[]{:S(2)}, u32[]{:S(2)}) collective-permute-start(bf16[1024,2048]{1,0:T(8,128)(2,1)} %convolution_convert_fusion), channel_id=1, source_target_pairs={{0,1},{1,0},{2,3},{3,2},{4,5},{5,4},{6,7},{7,6},{8,9},{9,8},{10,11... | collective-permute-start | bytes 12582920 | tf_op jit(solution)/shard_map/grad_normed2_scatter/ppermute | solution.py:184
  507.3 71.7 %collective-permute-start.66 = (bf16[1024,2048]{1,0:T(8,128)(2,1)}, bf16[1024,2048]{1,0:T(8,128)(2,1)}, u32[]{:S(2)}, u32[]{:S(2)}) collective-permute-start(bf16[1024,2048]{1,0:T(8,128)(2,1)} %pad_maximum_fusion.1), channel_id=1, source_target_pairs={{0,1},{1,0},{2,3},{3,2},{4,5},{5,4},{6,7},{7,6},{8,9},{9,8},{10,11... | collective-permute-start | bytes 12582920 | tf_op jit(solution)/shard_map/mlp_out_scatter/ppermute | solution.py:184
  590.9 69.0 %all-to-all-start.4 = ((bf16[8,64,2048]{2,1,0:T(8,128)(2,1)}), bf16[8,64,2048]{2,1,0:T(8,128)(2,1)S(1)}, u32[]{:S(2)}, u32[]{:S(2)}) async-start(bf16[8,64,2048]{2,1,0:T(8,128)(2,1)} %bitcast.55), calls=%async_computation.4 | async-start | bytes 4194304 | tf_op jit(solution)/shard_map/input_grad_to_stored/all_to_all | solution.py:482
  597.2 36.4 %collective-permute-start.69 = (bf16[256,2048]{1,0:T(8,128)(2,1)S(1)}, bf16[256,2048]{1,0:T(8,128)(2,1)S(1)}, u32[]{:S(2)}, u32[]{:S(2)}) collective-permute-start(bf16[256,2048]{1,0:T(8,128)(2,1)S(1)} %get-tuple-element.133), channel_id=1, source_target_pairs={{0,4},{4,0},{1,5},{5,1},{2,6},{6,2},{3,7},{7,3},{8,12},{12,8},{9,1... | collective-permute-start | bytes 3145736 | tf_op jit(solution)/shard_map/mlp_out_scatter/ppermute | solution.py:184
  659.9 53.8 %all-to-all-start.5 = ((bf16[8,64,2048]{2,1,0:T(8,128)(2,1)}), bf16[8,64,2048]{2,1,0:T(8,128)(2,1)}, u32[]{:S(2)}, u32[]{:S(2)}) async-start(bf16[8,64,2048]{2,1,0:T(8,128)(2,1)} %bitcast.165), calls=%async_computation.5 | async-start | bytes 4194304 | tf_op jit(solution)/shard_map/result_to_stored/all_to_all | solution.py:482
  665.6 120.9 %reduce-scatter.5.cloned.1.call-start = ((), (), s32[]{:S(2)}) async-start(), calls=%async_computation.11 | async-start | bytes 3276800 | tf_op jit(solution)/shard_map/attention_grad_rows/reduce_scatter | solution.py:602
  680.9 47.1 %collective-permute-start.71 = (bf16[512,1024]{1,0:T(8,128)(2,1)}, bf16[512,1024]{1,0:T(8,128)(2,1)}, u32[]{:S(2)}, u32[]{:S(2)}) collective-permute-start(bf16[512,1024]{1,0:T(8,128)(2,1)} %get-tuple-element.101.refs_0_), channel_id=1, source_target_pairs={{0,2},{2,0},{1,3},{3,1},{4,6},{6,4},{5,7},{7,5},{8,10},{10,8},{9,1... | collective-permute-start | bytes 3145736 | tf_op jit(solution)/shard_map/ppermute | solution.py:184
  739.6 35.0 %collective-permute-start.79 = (bf16[512,1024]{1,0:T(8,128)(2,1)}, bf16[512,1024]{1,0:T(8,128)(2,1)S(1)}, u32[]{:S(2)}, u32[]{:S(2)}) collective-permute-start(bf16[512,1024]{1,0:T(8,128)(2,1)} %get-tuple-element.101.refs_0_), channel_id=1, source_target_pairs={{0,1},{1,0},{2,3},{3,2},{4,5},{5,4},{6,7},{7,6},{8,9},{9,8},{10,11... | collective-permute-start | bytes 3145736 | tf_op jit(solution)/shard_map/proj_grad_rows/ppermute | solution.py:184
  739.6 35.0 %collective-permute-start.80 = (bf16[512,1024]{1,0:T(8,128)(2,1)}, bf16[512,1024]{1,0:T(8,128)(2,1)S(1)}, u32[]{:S(2)}, u32[]{:S(2)}) collective-permute-start(bf16[512,1024]{1,0:T(8,128)(2,1)} %collective-permute-done.71.refs_1_), channel_id=1, source_target_pairs={{0,1},{1,0},{2,3},{3,2},{4,5},{5,4},{6,7},{7,6},{8,9},{9,8},{10,11... | collective-permute-start | bytes 3145736 | tf_op jit(solution)/shard_map/proj_grad_rows/ppermute | solution.py:184
  (203 other events, 3337.9 us)
Sparse Core Ops, SparseCore 0:
  26.9 86.4 all-gather.4
  115.0 192.2 all-gather.8
  368.4 94.3 all-gather.6
  465.5 166.3 reduce-scatter.2
  728.2 58.2 reduce-scatter.4

commit v4 on v3

--- a/solution.py
+++ b/solution.py
@@ -608,34 +608,31 @@
     unit_terms, both_all, act_late = together(unit_terms, both_all, act_low)
     normed1_all, attended_all = both_all[:, :width], both_all[:, width:]
     with jax.named_scope("grad_normed2_scatter"):
-        grad_normed2, scattered = scatter_plane(
+        grad_normed2, _ = scatter_plane(
             lambda first, count: dot(grad_pre[first : first + count], fc_own, NT),
             rows,
             unit_terms,
         )
     units = over_z(unit_terms)
+    dgain2 = jnp.sum(grad_normed2 * unit2, axis=0)
+    dshift2 = jnp.sum(grad_normed2, axis=0)
+    dproj_bias = jnp.sum(grad_f32, axis=0)
+    grad_middle = grad_f32 + norm_back(grad_normed2, unit2, rstd2, gain2)
+
+    grad_branch = grad_middle.astype(BF16)
+    dout_bias = jnp.sum(grad_branch.astype(F32), axis=0)
+    grad_attended = dot(grad_branch, full_out, NT).astype(BF16)
+    dq, dkv_ctx = attention_backward(
+        queries, grad_attended, attended, norms, kv_ctx, seg_own, seg_ctx, padding_id
+    )
     with jax.named_scope("mlp_out_scatter"):
         mlp_out, _ = scatter_plane(
             lambda first, count: jnp.concatenate(
                 [dot(act_late[first : first + count], own, NN) for own in proj_parts], axis=1
             ),
             rows,
-            scattered,
+            dq,
         )
-    dgain2 = jnp.sum(grad_normed2 * unit2, axis=0)
-    dshift2 = jnp.sum(grad_normed2, axis=0)
-    dproj_bias = jnp.sum(grad_f32, axis=0)
-    grad_middle = grad_f32 + norm_back(grad_normed2, unit2, rstd2, gain2)
-
-    grad_branch = grad_middle.astype(BF16)
-    dout_bias = jnp.sum(grad_branch.astype(F32), axis=0)
-    grad_attended = dot(grad_branch, full_out, NT).astype(BF16)
-    dq, dkv_ctx = attention_backward(
-        queries, grad_attended, attended, norms, kv_ctx, seg_own, seg_ctx, padding_id
-    )
-    result = (middle + mlp_out + proj_shift).astype(BF16)
-    with jax.named_scope("result_to_stored"):
-        hidden_out = to_stored(result).astype(BF16)
     dkv = dkv_ctx[halo * rows :]
     for back in range(1, halo + 1):
         pairs = [(i + back, i) for i in range(seqs - back)]
@@ -694,9 +691,12 @@
 
     proj_near = near_rep([units[fc_rows:]])
     fc_near = near_rep(rows_of_y(units[:fc_rows]))
-    head_terms, input_grad, hidden_out, proj_near, fc_near = together(
-        jnp.concatenate([dqkv_own, dout_own], axis=1), input_grad, hidden_out, proj_near, fc_near
-    )
+    result = (middle + mlp_out + proj_shift).astype(BF16)
+    result, proj_near, fc_near = together(result, proj_near, fc_near)
+    with jax.named_scope("result_to_stored"):
+        hidden_out = to_stored(result).astype(BF16)
+    head_terms = jnp.concatenate([dqkv_own, dout_own], axis=1)
+    heads = over_z(head_terms)
     with jax.named_scope("proj_grad_rows"):
         proj_pieces = far_rep(proj_near)
         dproj_weight = assemble(
@@ -747,10 +747,8 @@
 
     mids = reduce_small(mids)
     lasts = reduce_small(lasts)
+    heads, dfc_weight, dproj_weight = together(heads, dfc_weight, dproj_weight)
     with jax.named_scope("attention_grad_rows"):
-        heads, dfc_weight, dproj_weight, mids, lasts = together(
-            over_z(head_terms), dfc_weight, dproj_weight, mids, lasts
-        )
         dout_bias, dgain2, dshift2, dfc_bias, dproj_bias = mids
         dgain1, dshift1, dqv_bias = lasts
         head_pieces = far_rep(near_rep(rows_of_y(heads)))

time: 826 us -> 807 us (0.977)
  waiting for transfers between devices: 386 us -> 361 us
    all_to_all x3, waiting for transfers between devices: 19.7 us -> 8.77 us  [exchange(): moved = lax.all_to_all(packed, SEQ, split_axis=0, concat_axis=0, tiled=True)]
  transfers between devices with their start and end apart: 111 -> 111, of which waited for: 55 -> 47; matrix products, arithmetic and copies ran while one was open for 26% -> 27% of each run, Pallas kernels for 8% -> 9%
where the time goes in v4:
time: 807 us; the launch traced here: 801 us
  waiting for transfers between devices  361 us (45%)
  matrix products  148 us (18%)
  starting transfers between devices  108 us (13%)
  Pallas kernels  71.5 us (9%)
  local copies, waits for them, and re-layouts  52.5 us (7%)
  other arithmetic  43.6 us (5%)
  between operations  16.1 us (2%)
    ppermute x90, waiting for transfers between devices, swap(): return lax.ppermute(block, axis, [(0, 1), (1, 0)])  258 us
    dot_general x26, matrix products, dot(): lax.dot_general(left, right, (dims, ((), ())), preferred_element_type=F32)  148 us
    ppermute x90, starting transfers between devices, swap(): return lax.ppermute(block, axis, [(0, 1), (1, 0)])  62.5 us
    all_gather x1, waiting for transfers between devices, shards(): columns = lax.all_gather(quarters, 'z', axis=0, tiled=True)  55.1 us
    pallas_call x3, Pallas kernels, assemble(): pl.pallas_call(functools.partial(assemble_kernel, count, slices, by_colum...  18.9 us
    unnamed x245, local copies, waits for them, and re-layouts  17 us
    pallas_call x2, Pallas kernels, place_rows(): pl.pallas_call(functools.partial(place_kernel, count, parts), grid_spec=p...  16.5 us
  transfers between devices with their start and end apart: 111, of which 47 were waited for; matrix products, arithmetic and copies ran while one was open for 27% of the time, Pallas kernels for 9%

profile of v4, /device:TPU:0, one launch (start us, length us, event | category | flops | bytes accessed | tf_op | source)
XLA Modules:
  0.0 801.0 jit_solution(3743166212106420400)
XLA Ops:
  32.1 22.7 %collective-permute-done = bf16[256,1024]{1,0:T(8,128)(2,1)S(1)} collective-permute-done((bf16[256,1024]{1,0:T(8,128)(2,1)S(1)}, bf16[256,1024]{1,0:T(8,128)(2,1)S(1)}, u32[]{:S(2)}, u32[]{:S(2)}) %collective-permute-start) | collective-permute-done | bytes 524320 | tf_op jit(solution)/shard_map/ppermute | solution.py:184
  58.3 55.1 %all-gather.5.cloned.1.call-done = bf16[256,4352]{1,0:T(8,128)(2,1)} async-done(((bf16[64,4352]{1,0:T(8,128)(2,1)}), bf16[256,4352]{1,0:T(8,128)(2,1)}) %all-gather.5.cloned.1.call-update) | async-done | bytes 2228240 | tf_op jit(solution)/shard_map/attention_weights/all_gather | solution.py:519
  135.2 21.4 %collective-permute-done.3.refs_10_ = bf16[128,2304]{1,0:T(8,128)(2,1)} collective-permute-done((bf16[128,2304]{1,0:T(8,128)(2,1)}, bf16[128,2304]{1,0:T(8,128)(2,1)}, u32[]{:S(2)}, u32[]{:S(2)}) %collective-permute-start.3) | collective-permute-done | bytes 589856 | tf_op jit(solution)/shard_map/ppermute | solution.py:184
  167.5 10.4 %collective-permute-done.8.refs_6_ = bf16[128,2304]{1,0:T(8,128)(2,1)} collective-permute-done((bf16[128,2304]{1,0:T(8,128)(2,1)}, bf16[128,2304]{1,0:T(8,128)(2,1)}, u32[]{:S(2)}, u32[]{:S(2)}) %collective-permute-start.8) | collective-permute-done | bytes 589856 | tf_op jit(solution)/shard_map/qkv_gather/ppermute | solution.py:184
  199.8 9.5 %collective-permute-done.39.refs_10_ = bf16[128,2048]{1,0:T(8,128)(2,1)} collective-permute-done((bf16[128,2048]{1,0:T(8,128)(2,1)S(1)}, bf16[128,2048]{1,0:T(8,128)(2,1)}, u32[]{:S(2)}, u32[]{:S(2)}) %collective-permute-start.39) | collective-permute-done | bytes 524320 | tf_op jit(solution)/shard_map/out_gather/ppermute | solution.py:184
  214.7 9.3 %collective-permute-done.36.refs_6_ = bf16[128,2048]{1,0:T(8,128)(2,1)} collective-permute-done((bf16[128,2048]{1,0:T(8,128)(2,1)}, bf16[128,2048]{1,0:T(8,128)(2,1)}, u32[]{:S(2)}, u32[]{:S(2)}) %collective-permute-start.36) | collective-permute-done | bytes 524320 | tf_op jit(solution)/shard_map/out_gather/ppermute | solution.py:184
  225.4 8.8 %all-to-all-done.1 = bf16[8,64,2048]{2,1,0:T(8,128)(2,1)} async-done(((bf16[8,64,2048]{2,1,0:T(8,128)(2,1)}), bf16[8,64,2048]{2,1,0:T(8,128)(2,1)}, u32[]{:S(2)}, u32[]{:S(2)}) %all-to-all-start.1) | async-done | bytes 2097184 | tf_op jit(solution)/shard_map/grad_to_places/all_to_all | solution.py:482
  258.3 11.1 %collective-permute-done.17.refs_1_ = bf16[128,2048]{1,0:T(8,128)(2,1)S(1)} collective-permute-done((bf16[128,2048]{1,0:T(8,128)(2,1)S(1)}, bf16[128,2048]{1,0:T(8,128)(2,1)S(1)}, u32[]{:S(2)}, u32[]{:S(2)}) %collective-permute-start.17) | collective-permute-done | bytes 524320 | tf_op jit(solution)/shard_map/grad_gather/ppermute | solution.py:184
  292.9 9.0 %attention_forward.1 = (bf16[256,2048]{1,0:T(8,128)(2,1)S(1)}, f32[256,2048]{1,0:T(8,128)S(1)}, f32[256,2048]{1,0:T(8,128)S(1)}) custom-call(bf16[256,2048]{1,0:T(8,128)(2,1)S(1)} %fusion.32.q_ref, bf16[768,256]{1,0:T(8,128)(2,1)S(1)} %pad_maximum_fusion.11.kv_ref, s32[256,1]{1,0:T(8,128)S(1)} %copy.72.own_ref, s32[1,768]{1,0:T(1,128)S(1)} %broadcast_in_dim.25.ctx_ref), custom_call_target="tpu_custom_call" | custom-call | flops 1610612736 | bytes 6291456 | tf_op jit(solution)/shard_map/attention_forward/pallas_call | solution.py:73
  322.6 10.7 %collective-permute-done.46.refs_2_ = bf16[128,2048]{1,0:T(8,128)(2,1)S(1)} collective-permute-done((bf16[128,2048]{1,0:T(8,128)(2,1)S(1)}, bf16[128,2048]{1,0:T(8,128)(2,1)S(1)}, u32[]{:S(2)}, u32[]{:S(2)}) %collective-permute-start.46) | collective-permute-done | bytes 524320 | tf_op jit(solution)/shard_map/normed2_gather/ppermute | solution.py:184
  334.8 11.2 %collective-permute-done.45.refs_1_ = bf16[128,2048]{1,0:T(8,128)(2,1)S(1)} collective-permute-done((bf16[128,2048]{1,0:T(8,128)(2,1)S(1)}, bf16[128,2048]{1,0:T(8,128)(2,1)S(1)}, u32[]{:S(2)}, u32[]{:S(2)}) %collective-permute-start.45) | collective-permute-done | bytes 524320 | tf_op jit(solution)/shard_map/normed2_gather/ppermute | solution.py:184
  347.3 8.8 %collective-permute-done.47.refs_3_ = bf16[128,2048]{1,0:T(8,128)(2,1)} collective-permute-done((bf16[128,2048]{1,0:T(8,128)(2,1)S(1)}, bf16[128,2048]{1,0:T(8,128)(2,1)}, u32[]{:S(2)}, u32[]{:S(2)}) %collective-permute-start.47) | collective-permute-done | bytes 524320 | tf_op jit(solution)/shard_map/normed2_gather/ppermute | solution.py:184
  374.6 12.7 %fusion.17 = f32[2048,1024]{1,0:T(8,128)} fusion(bf16[1024,1024]{1,0:T(8,128)(2,1)S(1)} %bitcast.179, bf16[2048,2048]{1,0:T(8,128)(2,1)} %join_rows.2), kind=kOutput, calls=%fused_computation.27 | convolution fusion | flops 4294967296 | bytes 14680064 | tf_op jit(solution)/shard_map/dot_general | solution.py:29
  387.4 13.2 %multiply_convert_fusion = (bf16[2048,1024]{1,0:T(8,128)(2,1)}, f32[2048,1024]{1,0:T(8,128)}) fusion(f32[1024]{0:T(1024)S(1)} %bitcast.211, bf16[2048,2048]{1,0:T(8,128)(2,1)S(1)} %bitcast.164, bf16[2048,1024]{1,0:T(8,128)(2,1)S(1)} %bitcast.169), kind=kOutput, calls=%fused_computation.18 | convolution fusion | flops 8610906112 | bytes 25169920 | tf_op jit(solution)/shard_map/dot_general | solution.py:29
  400.6 13.5 %convert_reduce_fusion = (f32[1024]{0:T(1024)S(1)}, bf16[2048,1024]{1,0:T(8,128)(2,1)}) fusion(f32[2048,1024]{1,0:T(8,128)} %get-tuple-element.171, f32[1024]{0:T(1024)S(1)} %bitcast.212, f32[2048,1024]{1,0:T(8,128)} %fusion.17, bf16[1024,1024]{1,0:T(8,128)(2,1)S(1)} %bitcast.176, bf16[2048,2048]{1,0:T(8,128)(2,1)S(1)} %bitcast.162), kind=kOutput, calls=%fused_computation.12 | convolution fusion | flops 4343200768 | bytes 27271168 | tf_op jit(solution)/shard_map/dot_general | solution.py:29
  428.1 11.5 %convolution_convert_fusion.1 = bf16[2048,1024]{1,0:T(8,128)(2,1)S(1)} fusion(bf16[2048,2048]{1,0:T(8,128)(2,1)} %join_rows.3, bf16[2048,1024]{1,0:T(8,128)(2,1)S(1)} %copy-done.108), kind=kOutput, calls=%fused_computation.21 | convolution fusion | flops 8592031744 | bytes 16777216 | tf_op jit(solution)/shard_map/dot_general | solution.py:29
  448.2 14.6 %all-gather.7.cloned.1.call-done = bf16[2048,4096]{1,0:T(8,128)(2,1)} async-done(((bf16[256,4096]{1,0:T(8,128)(2,1)}), bf16[2048,4096]{1,0:T(8,128)(2,1)}) %all-gather.7.cloned.1.call-update) | async-done | bytes 16777232 | tf_op jit(solution)/shard_map/both_gather/all_gather | solution.py:587
  485.9 12.3 %collective-permute-done.61 = bf16[256,2048]{1,0:T(8,128)(2,1)S(1)} collective-permute-done((bf16[256,2048]{1,0:T(8,128)(2,1)S(1)}, bf16[256,2048]{1,0:T(8,128)(2,1)S(1)}, u32[]{:S(2)}, u32[]{:S(2)}) %collective-permute-start.61) | collective-permute-done | bytes 1048608 | tf_op jit(solution)/shard_map/grad_normed2_scatter/ppermute | solution.py:184
  525.4 12.0 %attention_backward.1 = (bf16[256,2048]{1,0:T(8,128)(2,1)S(1)}, f32[768,256]{1,0:T(8,128)S(1)}) custom-call(bf16[256,2048]{1,0:T(8,128)(2,1)S(1)} %copy-done.3, bf16[256,2048]{1,0:T(8,128)(2,1)S(1)} %convolution_convert_fusion.7.g_ref, f32[256,2048]{1,0:T(8,128)} %copy-done.10, f32[256,2048]{1,0:T(8,128)} %copy-done.11, bf16[768,256]{1,0:T(8,128)(2,1)S(1)} %copy-done.5, ...), custom_call_target="tpu_custom_call" | custom-call | flops 4026531840 | bytes 7340032 | tf_op jit(solution)/shard_map/attention_backward/pallas_call | solution.py:132
  548.8 11.2 %collective-permute-done.74 = bf16[256,256]{1,0:T(8,128)(2,1)} collective-permute-done((bf16[256,256]{1,0:T(8,128)(2,1)}, bf16[256,256]{1,0:T(8,128)(2,1)}, u32[]{:S(2)}, u32[]{:S(2)}) %collective-permute-start.74) | collective-permute-done | bytes 131104 | tf_op jit(solution)/shard_map/ppermute | solution.py:640
  621.6 9.4 %collective-permute-done.67 = bf16[256,2048]{1,0:T(8,128)(2,1)} collective-permute-done((bf16[256,2048]{1,0:T(8,128)(2,1)}, bf16[256,2048]{1,0:T(8,128)(2,1)}, u32[]{:S(2)}, u32[]{:S(2)}) %collective-permute-start.67) | collective-permute-done | bytes 1048608 | tf_op jit(solution)/shard_map/mlp_out_scatter/ppermute | solution.py:184
  668.3 24.5 %collective-permute-done.71.refs_2_ = bf16[256,1024]{1,0:T(8,128)(2,1)} collective-permute-done((bf16[256,1024]{1,0:T(8,128)(2,1)S(1)}, bf16[256,1024]{1,0:T(8,128)(2,1)}, u32[]{:S(2)}, u32[]{:S(2)}) %collective-permute-start.71) | collective-permute-done | bytes 524320 | tf_op jit(solution)/shard_map/ppermute | solution.py:184
  692.8 9.0 %collective-permute-done.72.refs_3_ = bf16[256,1024]{1,0:T(8,128)(2,1)} collective-permute-done((bf16[256,1024]{1,0:T(8,128)(2,1)}, bf16[256,1024]{1,0:T(8,128)(2,1)}, u32[]{:S(2)}, u32[]{:S(2)}) %collective-permute-start.72) | collective-permute-done | bytes 524320 | tf_op jit(solution)/shard_map/ppermute | solution.py:184
  718.6 8.8 %collective-permute-done.96 = f32[128,128]{1,0:T(8,128)S(1)} collective-permute-done((f32[128,128]{1,0:T(8,128)S(1)}, f32[128,128]{1,0:T(8,128)S(1)}, u32[]{:S(2)}, u32[]{:S(2)}) %collective-permute-start.96) | collective-permute-done | bytes 65568 | tf_op jit(solution)/shard_map/ppermute | solution.py:184
  (604 shorter events, 444.3 us)
Async XLA Ops:
  16.6 97.0 %all-to-all-start = ((bf16[8,72,2048]{2,1,0:T(8,128)(2,1)}), bf16[8,72,2048]{2,1,0:T(8,128)(2,1)S(1)}, u32[]{:S(2)}, u32[]{:S(2)}) async-start(bf16[8,72,2048]{2,1,0:T(8,128)(2,1)} %bitcast.175), calls=%async_computation | async-start | bytes 4718592 | tf_op jit(solution)/shard_map/hidden_to_places/all_to_all | solution.py:472
  23.9 89.5 %all-gather.5.cloned.1.call-start = ((), (), s32[]{:S(2)}) async-start(), calls=%async_computation.8 | async-start | bytes 2785280 | tf_op jit(solution)/shard_map/attention_weights/all_gather | solution.py:519
  24.7 344.5 %all-gather.9.cloned.1.call-start = ((), (), s32[]{:S(2)}) async-start(), calls=%async_computation.12 | async-start | bytes 10485760 | tf_op jit(solution)/shard_map/units_gather/all_gather | solution.py:529
  118.8 37.8 %collective-permute-start.3 = (bf16[128,2304]{1,0:T(8,128)(2,1)}, bf16[128,2304]{1,0:T(8,128)(2,1)}, u32[]{:S(2)}, u32[]{:S(2)}) collective-permute-start(bf16[128,2304]{1,0:T(8,128)(2,1)} %get-tuple-element.62.refs_8_), channel_id=1, source_target_pairs={{0,4},{4,0},{1,5},{5,1},{2,6},{6,2},{3,7},{7,3},{8,12},{12,8},{9,1... | collective-permute-start | bytes 1769480 | tf_op jit(solution)/shard_map/ppermute | solution.py:184
  119.4 37.2 %collective-permute-start.4 = (bf16[128,2304]{1,0:T(8,128)(2,1)}, bf16[128,2304]{1,0:T(8,128)(2,1)}, u32[]{:S(2)}, u32[]{:S(2)}) collective-permute-start(bf16[128,2304]{1,0:T(8,128)(2,1)} %get-tuple-element.62.refs_8_), channel_id=1, source_target_pairs={{0,2},{2,0},{1,3},{3,1},{4,6},{6,4},{5,7},{7,5},{8,10},{10,8},{9,1... | collective-permute-start | bytes 1769480 | tf_op jit(solution)/shard_map/ppermute | solution.py:184
  122.3 111.9 %all-to-all-start.1 = ((bf16[8,64,2048]{2,1,0:T(8,128)(2,1)}), bf16[8,64,2048]{2,1,0:T(8,128)(2,1)}, u32[]{:S(2)}, u32[]{:S(2)}) async-start(bf16[8,64,2048]{2,1,0:T(8,128)(2,1)} %bitcast.166), calls=%async_computation.1 | async-start | bytes 4194304 | tf_op jit(solution)/shard_map/grad_to_places/all_to_all | solution.py:482
  126.7 336.1 %all-gather.7.cloned.1.call-start = ((), (), s32[]{:S(2)}) async-start(), calls=%async_computation.9 | async-start | bytes 18874368 | tf_op jit(solution)/shard_map/both_gather/all_gather | solution.py:587
  270.9 32.3 %collective-permute-start.25 = (bf16[128,2048]{1,0:T(8,128)(2,1)}, bf16[128,2048]{1,0:T(8,128)(2,1)}, u32[]{:S(2)}, u32[]{:S(2)}) collective-permute-start(bf16[128,2048]{1,0:T(8,128)(2,1)} %collective-permute-done.18.refs_2_), channel_id=1, source_target_pairs={{0,1},{1,0},{2,3},{3,2},{4,5},{5,4},{6,7},{7,6},{8,9},{9,8},{10,11... | collective-permute-start | bytes 1572872 | tf_op jit(solution)/shard_map/grad_gather/ppermute | solution.py:184
  271.4 31.8 %collective-permute-start.29 = (bf16[128,2048]{1,0:T(8,128)(2,1)}, bf16[128,2048]{1,0:T(8,128)(2,1)}, u32[]{:S(2)}, u32[]{:S(2)}) collective-permute-start(bf16[128,2048]{1,0:T(8,128)(2,1)} %collective-permute-done.21.refs_6_), channel_id=1, source_target_pairs={{0,1},{1,0},{2,3},{3,2},{4,5},{5,4},{6,7},{7,6},{8,9},{9,8},{10,11... | collective-permute-start | bytes 1572872 | tf_op jit(solution)/shard_map/grad_gather/ppermute | solution.py:184
  368.2 276.4 %reduce-scatter.3.cloned.1.call-start = ((), (), s32[]{:S(2)}) async-start(), calls=%async_computation.10 | async-start | bytes 10485760 | tf_op jit(solution)/shard_map/reduce_scatter | solution.py:602
  422.7 41.3 %collective-permute-start.60 = (bf16[1024,2048]{1,0:T(8,128)(2,1)}, bf16[1024,2048]{1,0:T(8,128)(2,1)}, u32[]{:S(2)}, u32[]{:S(2)}) collective-permute-start(bf16[1024,2048]{1,0:T(8,128)(2,1)} %convolution_convert_fusion), channel_id=1, source_target_pairs={{0,1},{1,0},{2,3},{3,2},{4,5},{5,4},{6,7},{7,6},{8,9},{9,8},{10,11... | collective-permute-start | bytes 12582920 | tf_op jit(solution)/shard_map/grad_normed2_scatter/ppermute | solution.py:184
  508.6 63.7 %collective-permute-start.59 = (bf16[1024,2048]{1,0:T(8,128)(2,1)}, bf16[1024,2048]{1,0:T(8,128)(2,1)}, u32[]{:S(2)}, u32[]{:S(2)}) collective-permute-start(bf16[1024,2048]{1,0:T(8,128)(2,1)} %pad_maximum_fusion.1), channel_id=1, source_target_pairs={{0,1},{1,0},{2,3},{3,2},{4,5},{5,4},{6,7},{7,6},{8,9},{9,8},{10,11... | collective-permute-start | bytes 12582920 | tf_op jit(solution)/shard_map/mlp_out_scatter/ppermute | solution.py:184
  543.2 36.2 %all-to-all-start.5 = ((bf16[8,256,256]{2,1,0:T(8,128)(2,1)}), bf16[8,256,256]{2,1,0:T(8,128)(2,1)S(1)}, u32[]{:S(2)}, u32[]{:S(2)}) async-start(bf16[8,256,256]{2,1,0:T(8,128)(2,1)} %bitcast.172), calls=%async_computation.6 | async-start | bytes 2097152 | tf_op jit(solution)/shard_map/all_to_all | solution.py:659
  586.3 35.3 %collective-permute-start.65 = (bf16[256,2048]{1,0:T(8,128)(2,1)}, bf16[256,2048]{1,0:T(8,128)(2,1)}, u32[]{:S(2)}, u32[]{:S(2)}) collective-permute-start(bf16[256,2048]{1,0:T(8,128)(2,1)} %get-tuple-element.112), channel_id=1, source_target_pairs={{0,2},{2,0},{1,3},{3,1},{4,6},{6,4},{5,7},{7,5},{8,10},{10,8},{9,1... | collective-permute-start | bytes 3145736 | tf_op jit(solution)/shard_map/mlp_out_scatter/ppermute | solution.py:184
  588.3 42.7 %collective-permute-start.67 = (bf16[256,2048]{1,0:T(8,128)(2,1)}, bf16[256,2048]{1,0:T(8,128)(2,1)}, u32[]{:S(2)}, u32[]{:S(2)}) collective-permute-start(bf16[256,2048]{1,0:T(8,128)(2,1)} %get-tuple-element.113), channel_id=1, source_target_pairs={{0,4},{4,0},{1,5},{5,1},{2,6},{6,2},{3,7},{7,3},{8,12},{12,8},{9,1... | collective-permute-start | bytes 3145736 | tf_op jit(solution)/shard_map/mlp_out_scatter/ppermute | solution.py:184
  601.4 102.6 %all-to-all-start.3 = ((bf16[8,64,2048]{2,1,0:T(8,128)(2,1)}), bf16[8,64,2048]{2,1,0:T(8,128)(2,1)S(1)}, u32[]{:S(2)}, u32[]{:S(2)}) async-start(bf16[8,64,2048]{2,1,0:T(8,128)(2,1)} %bitcast.53), calls=%async_computation.4 | async-start | bytes 4194304 | tf_op jit(solution)/shard_map/input_grad_to_stored/all_to_all | solution.py:482
  606.4 145.2 %reduce-scatter.5.cloned.1.call-start = ((), (), s32[]{:S(2)}) async-start(), calls=%async_computation.11 | async-start | bytes 3276800 | tf_op jit(solution)/shard_map/reduce_scatter | solution.py:602
  647.6 54.2 %collective-permute-start.69 = (bf16[512,1024]{1,0:T(8,128)(2,1)}, bf16[512,1024]{1,0:T(8,128)(2,1)}, u32[]{:S(2)}, u32[]{:S(2)}) collective-permute-start(bf16[512,1024]{1,0:T(8,128)(2,1)} %get-tuple-element.89.refs_0_), channel_id=1, source_target_pairs={{0,2},{2,0},{1,3},{3,1},{4,6},{6,4},{5,7},{7,5},{8,10},{10,8},{9,1... | collective-permute-start | bytes 3145736 | tf_op jit(solution)/shard_map/ppermute | solution.py:184
  660.3 32.5 %collective-permute-start.71 = (bf16[256,1024]{1,0:T(8,128)(2,1)S(1)}, bf16[256,1024]{1,0:T(8,128)(2,1)}, u32[]{:S(2)}, u32[]{:S(2)}) collective-permute-start(bf16[256,1024]{1,0:T(8,128)(2,1)S(1)} %get-tuple-element.85.refs_0_), channel_id=1, source_target_pairs={{0,2},{2,0},{1,3},{3,1},{4,6},{6,4},{5,7},{7,5},{8,10},{10,8},{9,1... | collective-permute-start | bytes 1572872 | tf_op jit(solution)/shard_map/ppermute | solution.py:184
  666.5 35.3 %collective-permute-start.72 = (bf16[256,1024]{1,0:T(8,128)(2,1)}, bf16[256,1024]{1,0:T(8,128)(2,1)}, u32[]{:S(2)}, u32[]{:S(2)}) collective-permute-start(bf16[256,1024]{1,0:T(8,128)(2,1)} %collective-permute-done.70.refs_1_), channel_id=1, source_target_pairs={{0,2},{2,0},{1,3},{3,1},{4,6},{6,4},{5,7},{7,5},{8,10},{10,8},{9,1... | collective-permute-start | bytes 1572872 | tf_op jit(solution)/shard_map/ppermute | solution.py:184
  704.0 86.9 %all-to-all-start.2 = ((bf16[8,64,2048]{2,1,0:T(8,128)(2,1)}), bf16[8,64,2048]{2,1,0:T(8,128)(2,1)}, u32[]{:S(2)}, u32[]{:S(2)}) async-start(bf16[8,64,2048]{2,1,0:T(8,128)(2,1)} %bitcast.165), calls=%async_computation.3 | async-start | bytes 4194304 | tf_op jit(solution)/shard_map/result_to_stored/all_to_all | solution.py:482
  712.1 30.1 %collective-permute-start.86 = (bf16[512,1024]{1,0:T(8,128)(2,1)}, bf16[512,1024]{1,0:T(8,128)(2,1)}, u32[]{:S(2)}, u32[]{:S(2)}) collective-permute-start(bf16[512,1024]{1,0:T(8,128)(2,1)} %collective-permute-done.69.refs_1_), channel_id=1, source_target_pairs={{0,1},{1,0},{2,3},{3,2},{4,5},{5,4},{6,7},{7,6},{8,9},{9,8},{10,11... | collective-permute-start | bytes 3145736 | tf_op jit(solution)/shard_map/proj_grad_rows/ppermute | solution.py:184
  730.3 42.2 %collective-permute-start.97 = (f32[128,128]{1,0:T(8,128)S(1)}, f32[128,128]{1,0:T(8,128)S(1)}, u32[]{:S(2)}, u32[]{:S(2)}) collective-permute-start(f32[128,128]{1,0:T(8,128)S(1)} %add.813), channel_id=1, source_target_pairs={{0,8},{8,16},{16,24},{24,0},{1,9},{9,17},{17,25},{25,1},{2,10},{10... | collective-permute-start | bytes 196616 | tf_op jit(solution)/shard_map/ppermute | solution.py:269
  731.7 40.7 %collective-permute-start.98 = (f32[128,128]{1,0:T(8,128)S(1)}, f32[128,128]{1,0:T(8,128)S(1)}, u32[]{:S(2)}, u32[]{:S(2)}) collective-permute-start(f32[128,128]{1,0:T(8,128)S(1)} %add.813), channel_id=1, source_target_pairs={{0,16},{8,24},{16,0},{24,8},{1,17},{9,25},{17,1},{25,9},{2,18},{10... | collective-permute-start | bytes 196616 | tf_op jit(solution)/shard_map/ppermute | solution.py:269
  (203 other events, 3478.8 us)
Sparse Core Ops, SparseCore 0:
  26.9 86.4 all-gather.4
  115.0 192.2 all-gather.8
  368.3 94.3 all-gather.6
  465.5 154.5 reduce-scatter.2
  642.2 60.3 reduce-scatter.4

commit v5 on v4

--- a/solution.py
+++ b/solution.py
@@ -22,7 +22,7 @@
 ALL = ("z", "y", "x", "c")
 BF16 = jnp.bfloat16
 F32 = jnp.float32
-HEADS_STEP = 2
+HEADS_STEP = 4
 
 
 def dot(left, right, dims):

time: 807 us -> 805 us (level)
  no operation moved by 1% of the time
where the time goes in v5:
time: 805 us; the launch traced here: 799 us
  waiting for transfers between devices  363 us (45%)
  matrix products  148 us (18%)
  starting transfers between devices  105 us (13%)
  Pallas kernels  69.9 us (9%)
  local copies, waits for them, and re-layouts  52.6 us (7%)
  other arithmetic  43.5 us (5%)
  between operations  16.1 us (2%)
    ppermute x90, waiting for transfers between devices, swap(): return lax.ppermute(block, axis, [(0, 1), (1, 0)])  259 us
    dot_general x26, matrix products, dot(): lax.dot_general(left, right, (dims, ((), ())), preferred_element_type=F32)  148 us
    ppermute x90, starting transfers between devices, swap(): return lax.ppermute(block, axis, [(0, 1), (1, 0)])  62.3 us
    all_gather x1, waiting for transfers between devices, shards(): columns = lax.all_gather(quarters, 'z', axis=0, tiled=True)  55.1 us
    pallas_call x3, Pallas kernels, assemble(): pl.pallas_call(functools.partial(assemble_kernel, count, slices, by_colum...  18.9 us
    unnamed x245, local copies, waits for them, and re-layouts  17 us
    pallas_call x2, Pallas kernels, place_rows(): pl.pallas_call(functools.partial(place_kernel, count, parts), grid_spec=p...  16.5 us
  transfers between devices with their start and end apart: 111, of which 47 were waited for; matrix products, arithmetic and copies ran while one was open for 27% of the time, Pallas kernels for 9%

profile of v5, /device:TPU:0, one launch (start us, length us, event | category | flops | bytes accessed | tf_op | source)
XLA Modules:
  0.0 798.8 jit_solution(3412738214379111865)
XLA Ops:
  32.1 22.7 %collective-permute-done = bf16[256,1024]{1,0:T(8,128)(2,1)S(1)} collective-permute-done((bf16[256,1024]{1,0:T(8,128)(2,1)S(1)}, bf16[256,1024]{1,0:T(8,128)(2,1)S(1)}, u32[]{:S(2)}, u32[]{:S(2)}) %collective-permute-start) | collective-permute-done | bytes 524320 | tf_op jit(solution)/shard_map/ppermute | solution.py:184
  58.3 55.1 %all-gather.5.cloned.1.call-done = bf16[256,4352]{1,0:T(8,128)(2,1)} async-done(((bf16[64,4352]{1,0:T(8,128)(2,1)}), bf16[256,4352]{1,0:T(8,128)(2,1)}) %all-gather.5.cloned.1.call-update) | async-done | bytes 2228240 | tf_op jit(solution)/shard_map/attention_weights/all_gather | solution.py:519
  135.2 21.4 %collective-permute-done.3.refs_10_ = bf16[128,2304]{1,0:T(8,128)(2,1)} collective-permute-done((bf16[128,2304]{1,0:T(8,128)(2,1)}, bf16[128,2304]{1,0:T(8,128)(2,1)}, u32[]{:S(2)}, u32[]{:S(2)}) %collective-permute-start.3) | collective-permute-done | bytes 589856 | tf_op jit(solution)/shard_map/ppermute | solution.py:184
  167.5 10.4 %collective-permute-done.8.refs_6_ = bf16[128,2304]{1,0:T(8,128)(2,1)} collective-permute-done((bf16[128,2304]{1,0:T(8,128)(2,1)}, bf16[128,2304]{1,0:T(8,128)(2,1)}, u32[]{:S(2)}, u32[]{:S(2)}) %collective-permute-start.8) | collective-permute-done | bytes 589856 | tf_op jit(solution)/shard_map/qkv_gather/ppermute | solution.py:184
  199.8 9.5 %collective-permute-done.39.refs_10_ = bf16[128,2048]{1,0:T(8,128)(2,1)} collective-permute-done((bf16[128,2048]{1,0:T(8,128)(2,1)S(1)}, bf16[128,2048]{1,0:T(8,128)(2,1)}, u32[]{:S(2)}, u32[]{:S(2)}) %collective-permute-start.39) | collective-permute-done | bytes 524320 | tf_op jit(solution)/shard_map/out_gather/ppermute | solution.py:184
  214.7 9.3 %collective-permute-done.36.refs_6_ = bf16[128,2048]{1,0:T(8,128)(2,1)} collective-permute-done((bf16[128,2048]{1,0:T(8,128)(2,1)}, bf16[128,2048]{1,0:T(8,128)(2,1)}, u32[]{:S(2)}, u32[]{:S(2)}) %collective-permute-start.36) | collective-permute-done | bytes 524320 | tf_op jit(solution)/shard_map/out_gather/ppermute | solution.py:184
  225.4 8.8 %all-to-all-done.1 = bf16[8,64,2048]{2,1,0:T(8,128)(2,1)} async-done(((bf16[8,64,2048]{2,1,0:T(8,128)(2,1)}), bf16[8,64,2048]{2,1,0:T(8,128)(2,1)}, u32[]{:S(2)}, u32[]{:S(2)}) %all-to-all-start.1) | async-done | bytes 2097184 | tf_op jit(solution)/shard_map/grad_to_places/all_to_all | solution.py:482
  258.3 11.1 %collective-permute-done.17.refs_1_ = bf16[128,2048]{1,0:T(8,128)(2,1)S(1)} collective-permute-done((bf16[128,2048]{1,0:T(8,128)(2,1)S(1)}, bf16[128,2048]{1,0:T(8,128)(2,1)S(1)}, u32[]{:S(2)}, u32[]{:S(2)}) %collective-permute-start.17) | collective-permute-done | bytes 524320 | tf_op jit(solution)/shard_map/grad_gather/ppermute | solution.py:184
  321.8 10.7 %collective-permute-done.46.refs_2_ = bf16[128,2048]{1,0:T(8,128)(2,1)S(1)} collective-permute-done((bf16[128,2048]{1,0:T(8,128)(2,1)S(1)}, bf16[128,2048]{1,0:T(8,128)(2,1)S(1)}, u32[]{:S(2)}, u32[]{:S(2)}) %collective-permute-start.46) | collective-permute-done | bytes 524320 | tf_op jit(solution)/shard_map/normed2_gather/ppermute | solution.py:184
  334.0 11.2 %collective-permute-done.45.refs_1_ = bf16[128,2048]{1,0:T(8,128)(2,1)S(1)} collective-permute-done((bf16[128,2048]{1,0:T(8,128)(2,1)S(1)}, bf16[128,2048]{1,0:T(8,128)(2,1)S(1)}, u32[]{:S(2)}, u32[]{:S(2)}) %collective-permute-start.45) | collective-permute-done | bytes 524320 | tf_op jit(solution)/shard_map/normed2_gather/ppermute | solution.py:184
  346.5 8.8 %collective-permute-done.47.refs_3_ = bf16[128,2048]{1,0:T(8,128)(2,1)} collective-permute-done((bf16[128,2048]{1,0:T(8,128)(2,1)S(1)}, bf16[128,2048]{1,0:T(8,128)(2,1)}, u32[]{:S(2)}, u32[]{:S(2)}) %collective-permute-start.47) | collective-permute-done | bytes 524320 | tf_op jit(solution)/shard_map/normed2_gather/ppermute | solution.py:184
  373.8 12.7 %fusion.17 = f32[2048,1024]{1,0:T(8,128)} fusion(bf16[1024,1024]{1,0:T(8,128)(2,1)S(1)} %bitcast.179, bf16[2048,2048]{1,0:T(8,128)(2,1)} %join_rows.2), kind=kOutput, calls=%fused_computation.27 | convolution fusion | flops 4294967296 | bytes 14680064 | tf_op jit(solution)/shard_map/dot_general | solution.py:29
  386.6 13.2 %multiply_convert_fusion = (bf16[2048,1024]{1,0:T(8,128)(2,1)}, f32[2048,1024]{1,0:T(8,128)}) fusion(f32[1024]{0:T(1024)S(1)} %bitcast.211, bf16[2048,2048]{1,0:T(8,128)(2,1)S(1)} %bitcast.164, bf16[2048,1024]{1,0:T(8,128)(2,1)S(1)} %bitcast.169), kind=kOutput, calls=%fused_computation.18 | convolution fusion | flops 8610906112 | bytes 25169920 | tf_op jit(solution)/shard_map/dot_general | solution.py:29
  399.8 13.5 %convert_reduce_fusion = (f32[1024]{0:T(1024)S(1)}, bf16[2048,1024]{1,0:T(8,128)(2,1)}) fusion(f32[2048,1024]{1,0:T(8,128)} %get-tuple-element.171, f32[1024]{0:T(1024)S(1)} %bitcast.212, f32[2048,1024]{1,0:T(8,128)} %fusion.17, bf16[1024,1024]{1,0:T(8,128)(2,1)S(1)} %bitcast.176, bf16[2048,2048]{1,0:T(8,128)(2,1)S(1)} %bitcast.162), kind=kOutput, calls=%fused_computation.12 | convolution fusion | flops 4343200768 | bytes 27271168 | tf_op jit(solution)/shard_map/dot_general | solution.py:29
  427.5 11.5 %convolution_convert_fusion.1 = bf16[2048,1024]{1,0:T(8,128)(2,1)S(1)} fusion(bf16[2048,2048]{1,0:T(8,128)(2,1)} %join_rows.3, bf16[2048,1024]{1,0:T(8,128)(2,1)S(1)} %copy-done.108), kind=kOutput, calls=%fused_computation.21 | convolution fusion | flops 8592031744 | bytes 16777216 | tf_op jit(solution)/shard_map/dot_general | solution.py:29
  447.6 14.3 %all-gather.7.cloned.1.call-done = bf16[2048,4096]{1,0:T(8,128)(2,1)} async-done(((bf16[256,4096]{1,0:T(8,128)(2,1)}), bf16[2048,4096]{1,0:T(8,128)(2,1)}) %all-gather.7.cloned.1.call-update) | async-done | bytes 16777232 | tf_op jit(solution)/shard_map/both_gather/all_gather | solution.py:587
  462.9 8.6 %add_convert_fusion = bf16[1024,2048]{1,0:T(8,128)(2,1)S(1)} fusion(bf16[1024,2048]{1,0:T(8,128)(2,1)} %collective-permute-done.60, bf16[2048,1024]{1,0:T(8,128)(2,1)} %bitcast.171, bf16[2048,1024]{1,0:T(8,128)(2,1)} %get-tuple-element.174), kind=kOutput, calls=%fused_computation.17 | convolution fusion | flops 4301258752 | bytes 14680064 | tf_op jit(solution)/shard_map/grad_normed2_scatter/dot_general | solution.py:29
  484.9 12.3 %collective-permute-done.61 = bf16[256,2048]{1,0:T(8,128)(2,1)S(1)} collective-permute-done((bf16[256,2048]{1,0:T(8,128)(2,1)S(1)}, bf16[256,2048]{1,0:T(8,128)(2,1)S(1)}, u32[]{:S(2)}, u32[]{:S(2)}) %collective-permute-start.61) | collective-permute-done | bytes 1048608 | tf_op jit(solution)/shard_map/grad_normed2_scatter/ppermute | solution.py:184
  524.3 11.2 %attention_backward.1 = (bf16[256,2048]{1,0:T(8,128)(2,1)S(1)}, f32[768,256]{1,0:T(8,128)S(1)}) custom-call(bf16[256,2048]{1,0:T(8,128)(2,1)S(1)} %copy-done.3, bf16[256,2048]{1,0:T(8,128)(2,1)S(1)} %convolution_convert_fusion.7.g_ref, f32[256,2048]{1,0:T(8,128)} %copy-done.10, f32[256,2048]{1,0:T(8,128)} %copy-done.11, bf16[768,256]{1,0:T(8,128)(2,1)S(1)} %copy-done.5, ...), custom_call_target="tpu_custom_call" | custom-call | flops 4026531840 | bytes 7340032 | tf_op jit(solution)/shard_map/attention_backward/pallas_call | solution.py:132
  547.3 11.4 %collective-permute-done.74 = bf16[256,256]{1,0:T(8,128)(2,1)} collective-permute-done((bf16[256,256]{1,0:T(8,128)(2,1)}, bf16[256,256]{1,0:T(8,128)(2,1)}, u32[]{:S(2)}, u32[]{:S(2)}) %collective-permute-start.74) | collective-permute-done | bytes 131104 | tf_op jit(solution)/shard_map/ppermute | solution.py:640
  619.9 9.3 %collective-permute-done.67 = bf16[256,2048]{1,0:T(8,128)(2,1)} collective-permute-done((bf16[256,2048]{1,0:T(8,128)(2,1)}, bf16[256,2048]{1,0:T(8,128)(2,1)}, u32[]{:S(2)}, u32[]{:S(2)}) %collective-permute-start.67) | collective-permute-done | bytes 1048608 | tf_op jit(solution)/shard_map/mlp_out_scatter/ppermute | solution.py:184
  666.8 23.8 %collective-permute-done.71.refs_2_ = bf16[256,1024]{1,0:T(8,128)(2,1)} collective-permute-done((bf16[256,1024]{1,0:T(8,128)(2,1)S(1)}, bf16[256,1024]{1,0:T(8,128)(2,1)}, u32[]{:S(2)}, u32[]{:S(2)}) %collective-permute-start.71) | collective-permute-done | bytes 524320 | tf_op jit(solution)/shard_map/ppermute | solution.py:184
  690.6 9.5 %collective-permute-done.72.refs_3_ = bf16[256,1024]{1,0:T(8,128)(2,1)} collective-permute-done((bf16[256,1024]{1,0:T(8,128)(2,1)}, bf16[256,1024]{1,0:T(8,128)(2,1)}, u32[]{:S(2)}, u32[]{:S(2)}) %collective-permute-start.72) | collective-permute-done | bytes 524320 | tf_op jit(solution)/shard_map/ppermute | solution.py:184
  716.1 9.1 %collective-permute-done.96 = f32[128,128]{1,0:T(8,128)S(1)} collective-permute-done((f32[128,128]{1,0:T(8,128)S(1)}, f32[128,128]{1,0:T(8,128)S(1)}, u32[]{:S(2)}, u32[]{:S(2)}) %collective-permute-start.96) | collective-permute-done | bytes 65568 | tf_op jit(solution)/shard_map/ppermute | solution.py:184
  (604 shorter events, 443.1 us)
Async XLA Ops:
  16.6 97.0 %all-to-all-start = ((bf16[8,72,2048]{2,1,0:T(8,128)(2,1)}), bf16[8,72,2048]{2,1,0:T(8,128)(2,1)S(1)}, u32[]{:S(2)}, u32[]{:S(2)}) async-start(bf16[8,72,2048]{2,1,0:T(8,128)(2,1)} %bitcast.175), calls=%async_computation | async-start | bytes 4718592 | tf_op jit(solution)/shard_map/hidden_to_places/all_to_all | solution.py:472
  23.9 89.5 %all-gather.5.cloned.1.call-start = ((), (), s32[]{:S(2)}) async-start(), calls=%async_computation.8 | async-start | bytes 2785280 | tf_op jit(solution)/shard_map/attention_weights/all_gather | solution.py:519
  24.7 343.7 %all-gather.9.cloned.1.call-start = ((), (), s32[]{:S(2)}) async-start(), calls=%async_computation.12 | async-start | bytes 10485760 | tf_op jit(solution)/shard_map/units_gather/all_gather | solution.py:529
  118.8 37.8 %collective-permute-start.3 = (bf16[128,2304]{1,0:T(8,128)(2,1)}, bf16[128,2304]{1,0:T(8,128)(2,1)}, u32[]{:S(2)}, u32[]{:S(2)}) collective-permute-start(bf16[128,2304]{1,0:T(8,128)(2,1)} %get-tuple-element.62.refs_8_), channel_id=1, source_target_pairs={{0,4},{4,0},{1,5},{5,1},{2,6},{6,2},{3,7},{7,3},{8,12},{12,8},{9,1... | collective-permute-start | bytes 1769480 | tf_op jit(solution)/shard_map/ppermute | solution.py:184
  119.4 37.2 %collective-permute-start.4 = (bf16[128,2304]{1,0:T(8,128)(2,1)}, bf16[128,2304]{1,0:T(8,128)(2,1)}, u32[]{:S(2)}, u32[]{:S(2)}) collective-permute-start(bf16[128,2304]{1,0:T(8,128)(2,1)} %get-tuple-element.62.refs_8_), channel_id=1, source_target_pairs={{0,2},{2,0},{1,3},{3,1},{4,6},{6,4},{5,7},{7,5},{8,10},{10,8},{9,1... | collective-permute-start | bytes 1769480 | tf_op jit(solution)/shard_map/ppermute | solution.py:184
  122.3 111.9 %all-to-all-start.1 = ((bf16[8,64,2048]{2,1,0:T(8,128)(2,1)}), bf16[8,64,2048]{2,1,0:T(8,128)(2,1)}, u32[]{:S(2)}, u32[]{:S(2)}) async-start(bf16[8,64,2048]{2,1,0:T(8,128)(2,1)} %bitcast.166), calls=%async_computation.1 | async-start | bytes 4194304 | tf_op jit(solution)/shard_map/grad_to_places/all_to_all | solution.py:482
  126.7 335.3 %all-gather.7.cloned.1.call-start = ((), (), s32[]{:S(2)}) async-start(), calls=%async_computation.9 | async-start | bytes 18874368 | tf_op jit(solution)/shard_map/both_gather/all_gather | solution.py:587
  270.9 31.5 %collective-permute-start.25 = (bf16[128,2048]{1,0:T(8,128)(2,1)}, bf16[128,2048]{1,0:T(8,128)(2,1)}, u32[]{:S(2)}, u32[]{:S(2)}) collective-permute-start(bf16[128,2048]{1,0:T(8,128)(2,1)} %collective-permute-done.18.refs_2_), channel_id=1, source_target_pairs={{0,1},{1,0},{2,3},{3,2},{4,5},{5,4},{6,7},{7,6},{8,9},{9,8},{10,11... | collective-permute-start | bytes 1572872 | tf_op jit(solution)/shard_map/grad_gather/ppermute | solution.py:184
  271.4 31.0 %collective-permute-start.29 = (bf16[128,2048]{1,0:T(8,128)(2,1)}, bf16[128,2048]{1,0:T(8,128)(2,1)}, u32[]{:S(2)}, u32[]{:S(2)}) collective-permute-start(bf16[128,2048]{1,0:T(8,128)(2,1)} %collective-permute-done.21.refs_6_), channel_id=1, source_target_pairs={{0,1},{1,0},{2,3},{3,2},{4,5},{5,4},{6,7},{7,6},{8,9},{9,8},{10,11... | collective-permute-start | bytes 1572872 | tf_op jit(solution)/shard_map/grad_gather/ppermute | solution.py:184
  367.4 275.5 %reduce-scatter.3.cloned.1.call-start = ((), (), s32[]{:S(2)}) async-start(), calls=%async_computation.10 | async-start | bytes 10485760 | tf_op jit(solution)/shard_map/reduce_scatter | solution.py:602
  421.9 41.0 %collective-permute-start.60 = (bf16[1024,2048]{1,0:T(8,128)(2,1)}, bf16[1024,2048]{1,0:T(8,128)(2,1)}, u32[]{:S(2)}, u32[]{:S(2)}) collective-permute-start(bf16[1024,2048]{1,0:T(8,128)(2,1)} %convolution_convert_fusion), channel_id=1, source_target_pairs={{0,1},{1,0},{2,3},{3,2},{4,5},{5,4},{6,7},{7,6},{8,9},{9,8},{10,11... | collective-permute-start | bytes 12582920 | tf_op jit(solution)/shard_map/grad_normed2_scatter/ppermute | solution.py:184
  507.6 63.5 %collective-permute-start.59 = (bf16[1024,2048]{1,0:T(8,128)(2,1)}, bf16[1024,2048]{1,0:T(8,128)(2,1)}, u32[]{:S(2)}, u32[]{:S(2)}) collective-permute-start(bf16[1024,2048]{1,0:T(8,128)(2,1)} %pad_maximum_fusion.1), channel_id=1, source_target_pairs={{0,1},{1,0},{2,3},{3,2},{4,5},{5,4},{6,7},{7,6},{8,9},{9,8},{10,11... | collective-permute-start | bytes 12582920 | tf_op jit(solution)/shard_map/mlp_out_scatter/ppermute | solution.py:184
  541.3 36.6 %all-to-all-start.5 = ((bf16[8,256,256]{2,1,0:T(8,128)(2,1)}), bf16[8,256,256]{2,1,0:T(8,128)(2,1)S(1)}, u32[]{:S(2)}, u32[]{:S(2)}) async-start(bf16[8,256,256]{2,1,0:T(8,128)(2,1)} %bitcast.172), calls=%async_computation.6 | async-start | bytes 2097152 | tf_op jit(solution)/shard_map/all_to_all | solution.py:659
  584.6 35.3 %collective-permute-start.65 = (bf16[256,2048]{1,0:T(8,128)(2,1)}, bf16[256,2048]{1,0:T(8,128)(2,1)}, u32[]{:S(2)}, u32[]{:S(2)}) collective-permute-start(bf16[256,2048]{1,0:T(8,128)(2,1)} %get-tuple-element.112), channel_id=1, source_target_pairs={{0,2},{2,0},{1,3},{3,1},{4,6},{6,4},{5,7},{7,5},{8,10},{10,8},{9,1... | collective-permute-start | bytes 3145736 | tf_op jit(solution)/shard_map/mlp_out_scatter/ppermute | solution.py:184
  586.5 42.7 %collective-permute-start.67 = (bf16[256,2048]{1,0:T(8,128)(2,1)}, bf16[256,2048]{1,0:T(8,128)(2,1)}, u32[]{:S(2)}, u32[]{:S(2)}) collective-permute-start(bf16[256,2048]{1,0:T(8,128)(2,1)} %get-tuple-element.113), channel_id=1, source_target_pairs={{0,4},{4,0},{1,5},{5,1},{2,6},{6,2},{3,7},{7,3},{8,12},{12,8},{9,1... | collective-permute-start | bytes 3145736 | tf_op jit(solution)/shard_map/mlp_out_scatter/ppermute | solution.py:184
  599.8 102.6 %all-to-all-start.3 = ((bf16[8,64,2048]{2,1,0:T(8,128)(2,1)}), bf16[8,64,2048]{2,1,0:T(8,128)(2,1)S(1)}, u32[]{:S(2)}, u32[]{:S(2)}) async-start(bf16[8,64,2048]{2,1,0:T(8,128)(2,1)} %bitcast.53), calls=%async_computation.4 | async-start | bytes 4194304 | tf_op jit(solution)/shard_map/input_grad_to_stored/all_to_all | solution.py:482
  603.4 145.3 %reduce-scatter.5.cloned.1.call-start = ((), (), s32[]{:S(2)}) async-start(), calls=%async_computation.11 | async-start | bytes 3276800 | tf_op jit(solution)/shard_map/reduce_scatter | solution.py:602
  646.2 53.9 %collective-permute-start.69 = (bf16[512,1024]{1,0:T(8,128)(2,1)}, bf16[512,1024]{1,0:T(8,128)(2,1)}, u32[]{:S(2)}, u32[]{:S(2)}) collective-permute-start(bf16[512,1024]{1,0:T(8,128)(2,1)} %get-tuple-element.89.refs_0_), channel_id=1, source_target_pairs={{0,2},{2,0},{1,3},{3,1},{4,6},{6,4},{5,7},{7,5},{8,10},{10,8},{9,1... | collective-permute-start | bytes 3145736 | tf_op jit(solution)/shard_map/ppermute | solution.py:184
  658.1 32.5 %collective-permute-start.71 = (bf16[256,1024]{1,0:T(8,128)(2,1)S(1)}, bf16[256,1024]{1,0:T(8,128)(2,1)}, u32[]{:S(2)}, u32[]{:S(2)}) collective-permute-start(bf16[256,1024]{1,0:T(8,128)(2,1)S(1)} %get-tuple-element.85.refs_0_), channel_id=1, source_target_pairs={{0,2},{2,0},{1,3},{3,1},{4,6},{6,4},{5,7},{7,5},{8,10},{10,8},{9,1... | collective-permute-start | bytes 1572872 | tf_op jit(solution)/shard_map/ppermute | solution.py:184
  664.8 35.3 %collective-permute-start.72 = (bf16[256,1024]{1,0:T(8,128)(2,1)}, bf16[256,1024]{1,0:T(8,128)(2,1)}, u32[]{:S(2)}, u32[]{:S(2)}) collective-permute-start(bf16[256,1024]{1,0:T(8,128)(2,1)} %collective-permute-done.70.refs_1_), channel_id=1, source_target_pairs={{0,2},{2,0},{1,3},{3,1},{4,6},{6,4},{5,7},{7,5},{8,10},{10,8},{9,1... | collective-permute-start | bytes 1572872 | tf_op jit(solution)/shard_map/ppermute | solution.py:184
  702.3 86.4 %all-to-all-start.2 = ((bf16[8,64,2048]{2,1,0:T(8,128)(2,1)}), bf16[8,64,2048]{2,1,0:T(8,128)(2,1)}, u32[]{:S(2)}, u32[]{:S(2)}) async-start(bf16[8,64,2048]{2,1,0:T(8,128)(2,1)} %bitcast.165), calls=%async_computation.3 | async-start | bytes 4194304 | tf_op jit(solution)/shard_map/result_to_stored/all_to_all | solution.py:482
  709.8 30.3 %collective-permute-start.86 = (bf16[512,1024]{1,0:T(8,128)(2,1)}, bf16[512,1024]{1,0:T(8,128)(2,1)}, u32[]{:S(2)}, u32[]{:S(2)}) collective-permute-start(bf16[512,1024]{1,0:T(8,128)(2,1)} %collective-permute-done.69.refs_1_), channel_id=1, source_target_pairs={{0,1},{1,0},{2,3},{3,2},{4,5},{5,4},{6,7},{7,6},{8,9},{9,8},{10,11... | collective-permute-start | bytes 3145736 | tf_op jit(solution)/shard_map/proj_grad_rows/ppermute | solution.py:184
  728.2 42.1 %collective-permute-start.97 = (f32[128,128]{1,0:T(8,128)S(1)}, f32[128,128]{1,0:T(8,128)S(1)}, u32[]{:S(2)}, u32[]{:S(2)}) collective-permute-start(f32[128,128]{1,0:T(8,128)S(1)} %add.813), channel_id=1, source_target_pairs={{0,8},{8,16},{16,24},{24,0},{1,9},{9,17},{17,25},{25,1},{2,10},{10... | collective-permute-start | bytes 196616 | tf_op jit(solution)/shard_map/ppermute | solution.py:269
  728.7 41.6 %collective-permute-start.98 = (f32[128,128]{1,0:T(8,128)S(1)}, f32[128,128]{1,0:T(8,128)S(1)}, u32[]{:S(2)}, u32[]{:S(2)}) collective-permute-start(f32[128,128]{1,0:T(8,128)S(1)} %add.813), channel_id=1, source_target_pairs={{0,16},{8,24},{16,0},{24,8},{1,17},{9,25},{17,1},{25,9},{2,18},{10... | collective-permute-start | bytes 196616 | tf_op jit(solution)/shard_map/ppermute | solution.py:269
  (203 other events, 3478.3 us)
Sparse Core Ops, SparseCore 0:
  26.9 86.4 all-gather.4
  115.0 192.2 all-gather.8
  367.5 94.3 all-gather.6
  464.7 157.1 reduce-scatter.2
  639.9 58.9 reduce-scatter.4
